TPU v7x, 512 devices: a whole 4x8x8 slice. The times are simulated.
512 devices in a mesh: section: 32 (over z, y_lo, core), tp: 4 (over y_hi), rep: 4 (over x).
Axes of the slice: x: 4, y: 8 (y_hi: 4, y_lo: 2; y = y_hi * 2 + y_lo), z: 8, core: 2. Of those that a mesh axis runs over, the one named last changes fastest.
Arguments:
- hidden: bfloat16 [32, 1536, 4096], P('section', 'rep', 'tp'), may hold values from -6 to 6
- cotangent: bfloat16 [32, 1536, 4096], P('section', 'rep', 'tp'), may hold values from -6 to 6
- w_down: bfloat16 [32, 4096, 1024], P('section', 'tp', 'rep'), may hold values from -0.09375 to 0.09375
- w_up: bfloat16 [32, 1024, 4096], P('section', 'rep', 'tp'), may hold values from -0.1875 to 0.1875
Outputs:
- rebuilt: bfloat16 [32, 1536, 4096], P('section', 'rep', 'tp')
- grad_hidden: bfloat16 [32, 1536, 4096], P('section', 'rep', 'tp')
- grad_up: bfloat16 [32, 1024, 4096], P('section', 'rep', 'tp')
- grad_down: bfloat16 [32, 4096, 1024], P('section', 'tp', 'rep')
All inputs are finite; a program needn't handle non-finite values.
Results may differ from a plain program's by a relative error of at most 0.022.
Values may be sent and summed in bfloat16 or wider, within the bound.
No kernel may reach another device: no remote copies, remote signals or barrier semaphores. Data moves between devices by JAX's collectives and lax.ppermute only.
A program may use at most 64 MiB of HBM per device.

v0:
```python
import jax
import jax.numpy as jnp
from jax import lax
from jax.sharding import PartitionSpec as P


def from_behind(block, axis, distance):
    devices = range(lax.axis_size(axis))
    route = [((i - distance) % len(devices), i) for i in devices]
    return lax.ppermute(block, axis, route)


def contract_last(left, right):
    return lax.dot_general(
        left, right, (((1,), (1,)), ((), ())), preferred_element_type=jnp.float32
    )


def contract_first(left, right):
    return lax.dot_general(
        left, right, (((0,), (0,)), ((), ())), preferred_element_type=jnp.float32
    )


def shards(hidden, cotangent, w_down, w_up):
    rows = hidden[0]
    upstream = cotangent[0]
    down_full = lax.all_gather(w_down[0], "rep", axis=1, tiled=True)
    up_full = lax.all_gather(w_up[0], "rep", axis=0, tiled=True)
    code_part = jnp.dot(rows, down_full, preferred_element_type=jnp.float32)
    code = lax.psum(code_part.astype(jnp.bfloat16), "tp")
    taken = from_behind(code, "section", 1)
    rebuilt = jnp.dot(taken, up_full, preferred_element_type=jnp.float32).astype(jnp.bfloat16)
    back_part = contract_last(upstream, up_full)
    back = lax.psum(back_part.astype(jnp.bfloat16), "tp")
    returned = from_behind(back, "section", -1)
    grad_hidden = contract_last(returned, down_full).astype(jnp.bfloat16)
    grad_up = lax.psum_scatter(
        contract_first(taken, upstream).astype(jnp.bfloat16), "rep", scatter_dimension=0, tiled=True
    )
    down_term = contract_first(rows, returned)
    grad_down = lax.psum_scatter(
        down_term.astype(jnp.bfloat16), "rep", scatter_dimension=1, tiled=True
    )
    return (rebuilt[None], grad_hidden[None], grad_up[None], grad_down[None])


def solution(mesh):
    return jax.shard_map(
        shards,
        mesh=mesh,
        in_specs=(
            P("section", "rep", "tp"),
            P("section", "rep", "tp"),
            P("section", "tp", "rep"),
            P("section", "rep", "tp"),
        ),
        out_specs=(
            P("section", "rep", "tp"),
            P("section", "rep", "tp"),
            P("section", "rep", "tp"),
            P("section", "tp", "rep"),
        ),
        check_vma=False,
    )
```

profile of v0, /device:TPU:1, one launch (start us, length us, event | category | flops | bytes accessed | tf_op | source)
XLA Modules:
  0.0 283.5 jit_solution(12537918148756244410)
XLA Ops:
  7.2 0.7 all-gather.7.cloned.1.call-update
  8.0 0.7 all-gather.5.cloned.1.call-update
  8.7 43.1 %all-gather.7.cloned.1.call-done = bf16[1,1024,1024]{2,1,0:T(8,128)(2,1)} async-done(((bf16[1,256,1024]{2,1,0:T(8,128)(2,1)}), bf16[1,1024,1024]{2,1,0:T(8,128)(2,1)}) %all-gather.7.cloned.1.call-update) | async-done | bytes 2097168 | tf_op jit(solution)/shard_map/all_gather | solution.py:29
  51.8 3.7 %fusion.17 = bf16[384,1024]{1,0:T(8,128)(2,1)} fusion(bf16[1,1024,1024]{2,1,0:T(8,128)(2,1)} %all-gather.7.cloned.1.call-done, bf16[1,384,1024]{2,1,0:T(8,128)(2,1)} %param.5), kind=kOutput, calls=%fused_computation.13 | convolution fusion | flops 805699584 | bytes 3670016 | tf_op jit(solution)/shard_map/dot_general | solution.py:14
  55.5 37.4 %all-gather.5.cloned.1.call-done = bf16[1,1024,1024]{2,1,0:T(8,128)(2,1)} async-done(((bf16[1,1024,256]{2,1,0:T(8,128)(2,1)}), bf16[1,1024,1024]{2,1,0:T(8,128)(2,1)}) %all-gather.5.cloned.1.call-update) | async-done | bytes 2097168 | tf_op jit(solution)/shard_map/all_gather | solution.py:28
  92.9 3.5 %fusion.8 = bf16[384,1024]{1,0:T(8,128)(2,1)} fusion(bf16[1,1024,1024]{2,1,0:T(8,128)(2,1)} %all-gather.5.cloned.1.call-done, bf16[1,384,1024]{2,1,0:T(8,128)(2,1)S(1)} %copy-done), kind=kOutput, calls=%fused_computation.10 | convolution fusion | flops 805699584 | bytes 3670016 | tf_op jit(solution)/shard_map/dot_general | solution.py:30
  96.4 0.0 reduce-scatter.5.cloned.1.call-start
  96.5 90.5 %all-reduce.3.cloned.1.call-done = (bf16[384,1024]{1,0:T(8,128)(2,1)}, bf16[384,1024]{1,0:T(8,128)(2,1)}) async-done(((bf16[384,1024]{1,0:T(8,128)(2,1)}, bf16[384,1024]{1,0:T(8,128)(2,1)}), (bf16[384,1024]{1,0:T(8,128)(2,1)}, bf16[384,1024]{1,0:T(8,128)(2,1)})) %all-reduce.3.cloned.1.call-update) | async-done | bytes 1572880 | tf_op jit(solution)/shard_map/psum | solution.py:31
  187.0 2.9 %collective-permute-start.1 = (bf16[384,1024]{1,0:T(8,128)(2,1)}, bf16[384,1024]{1,0:T(8,128)(2,1)S(1)}, u32[]{:S(2)}, u32[]{:S(2)}) collective-permute-start(bf16[384,1024]{1,0:T(8,128)(2,1)} %get-tuple-element.9), channel_id=1, source_target_pairs={{16,0},{32,16},{48,32},{64,48},{80,64},{96,80},{112,96},{128,112},... | collective-permute-start | bytes 2359304 | tf_op jit(solution)/shard_map/ppermute | solution.py:10
  189.9 10.6 %collective-permute-done.1 = bf16[384,1024]{1,0:T(8,128)(2,1)S(1)} collective-permute-done((bf16[384,1024]{1,0:T(8,128)(2,1)}, bf16[384,1024]{1,0:T(8,128)(2,1)S(1)}, u32[]{:S(2)}, u32[]{:S(2)}) %collective-permute-start.1) | collective-permute-done | bytes 786464 | tf_op jit(solution)/shard_map/ppermute | solution.py:10
  200.5 1.0 copy-done.5
  201.5 2.7 convert_bitcast_fusion
  204.2 0.0 reduce-scatter.3.cloned.1.call-start
  204.2 1.1 copy-done.4
  205.3 1.9 collective-permute-start
  207.2 8.9 %collective-permute-done = bf16[384,1024]{1,0:T(8,128)(2,1)S(1)} collective-permute-done((bf16[384,1024]{1,0:T(8,128)(2,1)S(1)}, bf16[384,1024]{1,0:T(8,128)(2,1)S(1)}, u32[]{:S(2)}, u32[]{:S(2)}) %collective-permute-start) | collective-permute-done | bytes 786464 | tf_op jit(solution)/shard_map/ppermute | solution.py:10
  216.1 0.9 copy-done.7
  217.0 2.7 convolution_convert_fusion
  219.7 1.6 copy-done.1
  221.2 3.1 %fusion.20 = bf16[1,384,1024]{2,1,0:T(8,128)(2,1)} fusion(bf16[384,1024]{1,0:T(8,128)(2,1)} %copy-done.7, bf16[1,1024,1024]{2,1,0:T(8,128)(2,1)S(1)} %copy-done.1), kind=kOutput, calls=%fused_computation.14 | convolution fusion | flops 805699584 | bytes 3670016 | tf_op jit(solution)/shard_map/dot_general | solution.py:33
  224.4 1.9 fusion.23
  226.3 12.4 %reduce-scatter.5.cloned.1.call-done = bf16[1024,256]{0,1:T(8,128)(2,1)} async-done(((bf16[1024,1024]{0,1:T(8,128)(2,1)}), bf16[1024,256]{0,1:T(8,128)(2,1)}) %reduce-scatter.5.cloned.1.call-update) | async-done | bytes 524304 | tf_op jit(solution)/shard_map/reduce_scatter | solution.py:42
  238.7 2.0 copy.8
  240.7 36.3 %reduce-scatter.3.cloned.1.call-done = bf16[256,1024]{1,0:T(8,128)(2,1)} async-done(((bf16[1024,1024]{1,0:T(8,128)(2,1)}), bf16[256,1024]{1,0:T(8,128)(2,1)}) %reduce-scatter.3.cloned.1.call-update) | async-done | bytes 524304 | tf_op jit(solution)/shard_map/reduce_scatter | solution.py:38
  (18 shorter events, 0.2 us)
Async XLA Ops:
  7.2 85.8 %copy-start = (bf16[1,384,1024]{2,1,0:T(8,128)(2,1)S(1)}, bf16[1,384,1024]{2,1,0:T(8,128)(2,1)}, u32[]{:S(2)}) copy-start(bf16[1,384,1024]{2,1,0:T(8,128)(2,1)} %param.4) | copy-start | bytes 2359300
  7.2 44.6 %all-gather.7.cloned.1.call-start = ((), (), s32[]{:S(2)}) async-start(), calls=%async_computation.5 | async-start | bytes 2621440 | tf_op jit(solution)/shard_map/all_gather | solution.py:29
  7.9 85.0 %all-gather.5.cloned.1.call-start = ((), (), s32[]{:S(2)}) async-start(), calls=%async_computation.4 | async-start | bytes 2621440 | tf_op jit(solution)/shard_map/all_gather | solution.py:28
  8.7 178.3 %all-reduce.3.cloned.1.call-start = ((), (), s32[]{:S(2)}) async-start(), calls=%async_computation.6 | async-start | bytes 3145728 | tf_op jit(solution)/shard_map/psum | solution.py:31
  96.4 142.2 %reduce-scatter.5.cloned.1.call-start = ((), (), s32[]{:S(2)}) async-start(), calls=%async_computation.3 | async-start | bytes 2621440 | tf_op jit(solution)/shard_map/reduce_scatter | solution.py:42
  187.0 13.5 %collective-permute-start.1 = (bf16[384,1024]{1,0:T(8,128)(2,1)}, bf16[384,1024]{1,0:T(8,128)(2,1)S(1)}, u32[]{:S(2)}, u32[]{:S(2)}) collective-permute-start(bf16[384,1024]{1,0:T(8,128)(2,1)} %get-tuple-element.9), channel_id=1, source_target_pairs={{16,0},{32,16},{48,32},{64,48},{80,64},{96,80},{112,96},{128,112},... | collective-permute-start | bytes 2359304 | tf_op jit(solution)/shard_map/ppermute | solution.py:10
  200.5 1.0 copy-start.5
  204.1 1.1 copy-start.4
  204.1 12.8 %copy-start.3 = (bf16[1,384,1024]{2,1,0:T(8,128)(2,1)S(1)}, bf16[1,384,1024]{2,1,0:T(8,128)(2,1)}, u32[]{:S(2)}) copy-start(bf16[1,384,1024]{2,1,0:T(8,128)(2,1)} %param.5) | copy-start | bytes 2359300
  204.2 72.8 %reduce-scatter.3.cloned.1.call-start = ((), (), s32[]{:S(2)}) async-start(), calls=%async_computation.2 | async-start | bytes 2621440 | tf_op jit(solution)/shard_map/reduce_scatter | solution.py:38
  205.3 10.8 %collective-permute-start = (bf16[384,1024]{1,0:T(8,128)(2,1)S(1)}, bf16[384,1024]{1,0:T(8,128)(2,1)S(1)}, u32[]{:S(2)}, u32[]{:S(2)}) collective-permute-start(bf16[384,1024]{1,0:T(8,128)(2,1)S(1)} %copy-done.4), channel_id=1, source_target_pairs={{496,0},{0,16},{16,32},{32,48},{48,64},{64,80},{80,96},{96,112},{1... | collective-permute-start | bytes 2359304 | tf_op jit(solution)/shard_map/ppermute | solution.py:10
  216.1 0.9 copy-start.7
  219.6 1.6 copy-start.1
  221.2 3.1 %copy-start.2 = (bf16[1,1024,1024]{2,1,0:T(8,128)(2,1)S(1)}, bf16[1,1024,1024]{2,1,0:T(8,128)(2,1)}, u32[]{:S(2)}) copy-start(bf16[1,1024,1024]{2,1,0:T(8,128)(2,1)} %all-gather.5.cloned.1.call-done) | copy-start | bytes 6291460
  221.2 3.1 %copy-start.6 = (bf16[384,1024]{1,0:T(8,128)(2,1)S(1)}, bf16[384,1024]{1,0:T(8,128)(2,1)}, u32[]{:S(2)}) copy-start(bf16[384,1024]{1,0:T(8,128)(2,1)} %copy-done.5) | copy-start | bytes 2359300
Sparse Core Ops, SparseCore 0:
  10.1 41.6 all-gather.6
  53.9 39.0 all-gather.4
  96.5 90.4 all-reduce.2
  204.3 34.3 reduce-scatter.4
  242.2 34.7 reduce-scatter.2
where the time goes:
time: 284 us
  waiting for transfers between devices  241 us (85%)
  matrix products  17.5 us (6%)
  between operations  13.8 us (5%)
  local copies, waits for them, and re-layouts  6.54 us (2%)
  starting transfers between devices  5.02 us (2%)
    psum x1, waiting for transfers between devices, shards(): code = lax.psum(code_part.astype(jnp.bfloat16), 'tp')  90.5 us
    all_gather x1, waiting for transfers between devices, shards(): up_full = lax.all_gather(w_up[0], 'rep', axis=0, tiled=True)  43.1 us
    all_gather x1, waiting for transfers between devices, shards(): down_full = lax.all_gather(w_down[0], 'rep', axis=1, tiled=True)  37.4 us
    reduce_scatter x1, waiting for transfers between devices, shards(): lax.psum_scatter(contract_first(taken, upstream).astype(jnp.bfloat16), 'r...  36.3 us
    ppermute x2, waiting for transfers between devices, from_behind(): return lax.ppermute(block, axis, route)  19.5 us
    reduce_scatter x1, waiting for transfers between devices, shards(): lax.psum_scatter(down_term.astype(jnp.bfloat16), 'rep', scatter_dimension...  12.4 us
    unnamed x17, local copies, waits for them, and re-layouts  6.54 us
  transfers between devices with their start and end apart: 7, of which 7 were waited for; matrix products, arithmetic and copies ran while one was open for 5% of the time, Pallas kernels for 0%

commit v1 on v0

v1 whole, which is shorter than its diff:
```python
import jax
import jax.numpy as jnp
from jax import lax
from jax.sharding import PartitionSpec as P

AXES = ("section", "tp", "rep")
EVEN = (1, 0, 3, 2)
ODD = (3, 2, 1, 0)


def route(sections, target):
    pairs = []
    for s in range(sections):
        for t in range(4):
            for r in range(4):
                a, b, c = target(s, t, r)
                pairs.append(((s * 4 + t) * 4 + r, ((a % sections) * 4 + b) * 4 + c))
    return pairs


def dot(left, right, dims):
    return lax.dot_general(left, right, (dims, ((), ())), preferred_element_type=jnp.float32)


def bf(x):
    return x.astype(jnp.bfloat16)


def f32(x):
    return x.astype(jnp.float32)


def shards(hidden, cotangent, w_down, w_up):
    sections = lax.axis_size("section")

    def send(x, target):
        return lax.ppermute(x, AXES, route(sections, target))

    def rep_pair(flip):
        table = (EVEN, ODD)
        return lambda s, t, r: (s, t, table[(s + flip) % 2][r])

    def tp_pair(flip, step=0):
        table = (EVEN, ODD)
        return lambda s, t, r: (s + step, table[(s + flip) % 2][t], r)

    parity = lax.axis_index("section") % 2
    tp = lax.axis_index("tp")
    v = ((tp == 1) | (tp == 2)).astype(jnp.int32)
    u = (tp >= 2).astype(jnp.int32)
    first = jnp.where(parity == 0, v, u)
    second = jnp.where(parity == 0, u, v)

    def reduce_and_shift(part, step):
        away = lax.dynamic_index_in_dim(part, 1 - first, 0, keepdims=False)
        came = send(away, tp_pair(0))
        kept = lax.dynamic_index_in_dim(part, first, 0, keepdims=False)
        half = bf(f32(kept) + f32(came))
        half = jnp.stack([half[:, :256], half[:, 256:]])
        over = lax.dynamic_index_in_dim(half, 1 - second, 0, keepdims=False)
        stay = lax.dynamic_index_in_dim(half, second, 0, keepdims=False)
        one = send(over, tp_pair(1, step))
        two = send(stay, lambda s, t, r: (s + step, t, r))
        return bf(f32(one) + f32(two))

    def gather(block):
        other = send(block, tp_pair(0))
        row = jnp.where(first == 0, jnp.concatenate([block, other], 1), jnp.concatenate([other, block], 1))
        rest = send(row, tp_pair(1))
        return jnp.where(second == 0, jnp.concatenate([row, rest], 0), jnp.concatenate([rest, row], 0))

    h, c, wd, wu = hidden[0], cotangent[0], w_down[0], w_up[0]
    h_in = send(h, rep_pair(0))
    wd_in = send(wd, rep_pair(1))
    c_in = send(c, rep_pair(1))
    wu_in = send(wu, rep_pair(0))
    hs = jnp.concatenate([h, h_in], 0)
    wds = jnp.concatenate([wd, wd_in], 1)
    cs = jnp.concatenate([c, c_in], 0)
    wus = jnp.concatenate([wu, wu_in], 0)
    code_part = bf(dot(hs, wds, ((1,), (0,)))).reshape(2, 384, 512)
    back_part = bf(dot(cs, wus, ((1,), (1,)))).reshape(2, 384, 512)
    code = gather(reduce_and_shift(code_part, 1))
    back = gather(reduce_and_shift(back_part, -1))
    r_out = bf(dot(code[384:], wus, ((1,), (0,))))
    r_in = send(r_out, rep_pair(1))
    u_out = bf(dot(code[:, 256:], cs, ((0,), (0,))))
    u_in = send(u_out, rep_pair(0))
    rebuilt = bf(dot(code[:384], wus, ((1,), (0,))) + f32(r_in))
    grad_up = bf(dot(code[:, :256], cs, ((0,), (0,))) + f32(u_in))
    g_out = bf(dot(back[384:], wds, ((1,), (1,))))
    g_in = send(g_out, rep_pair(0))
    d_out = bf(dot(hs, back[:, 256:], ((0,), (0,))))
    d_in = send(d_out, rep_pair(1))
    grad_hidden = bf(dot(back[:384], wds, ((1,), (1,))) + f32(g_in))
    grad_down = bf(dot(hs, back[:, :256], ((0,), (0,))) + f32(d_in))
    return (rebuilt[None], grad_hidden[None], grad_up[None], grad_down[None])


def solution(mesh):
    return jax.shard_map(
        shards,
        mesh=mesh,
        in_specs=(
            P("section", "rep", "tp"),
            P("section", "rep", "tp"),
            P("section", "tp", "rep"),
            P("section", "rep", "tp"),
        ),
        out_specs=(
            P("section", "rep", "tp"),
            P("section", "rep", "tp"),
            P("section", "rep", "tp"),
            P("section", "tp", "rep"),
        ),
        check_vma=False,
    )
```

time: 284 us -> 144 us (0.51)
  the two profiles are of different devices: /device:TPU:1 before, /device:TPU:14 now
where the time goes in v1:
time: 144 us; the launch traced here: 143 us
  waiting for transfers between devices  65.7 us (46%)
  starting transfers between devices  57.7 us (40%)
  matrix products  17.3 us (12%)
  other arithmetic  1.46 us (1%)
    ppermute x18, waiting for transfers between devices, send(): return lax.ppermute(x, AXES, route(sections, target))  65.7 us
    ppermute x18, starting transfers between devices, send(): return lax.ppermute(x, AXES, route(sections, target))  57.7 us
    dot_general x10, matrix products, dot(): lax.dot_general(left, right, (dims, ((), ())), preferred_element_type=jnp...  17.3 us
  transfers between devices with their start and end apart: 18, of which 12 were waited for; matrix products, arithmetic and copies ran while one was open for 12% of the time, Pallas kernels for 0%

profile of v1, /device:TPU:14, one launch (start us, length us, event | category | flops | bytes accessed | tf_op | source)
XLA Modules:
  0.0 143.4 jit_solution(942040180431977518)
XLA Ops:
  0.6 2.4 %collective-permute-start.9 = (bf16[384,1024]{1,0:T(8,128)(2,1)}, bf16[384,1024]{1,0:T(8,128)(2,1)S(1)}, u32[]{:S(2)}, u32[]{:S(2)}) collective-permute-start(bf16[384,1024]{1,0:T(8,128)(2,1)} %bitcast.44), channel_id=1, source_target_pairs={{0,3},{1,2},{2,1},{3,0},{4,7},{5,6},{6,5},{7,4},{8,11},{9,10},{10,... | collective-permute-start | bytes 2359304 | tf_op jit(solution)/shard_map/ppermute | solution.py:37
  3.0 2.8 %collective-permute-start.7 = (bf16[256,1024]{1,0:T(8,128)(2,1)}, bf16[256,1024]{1,0:T(8,128)(2,1)S(1)}, u32[]{:S(2)}, u32[]{:S(2)}) collective-permute-start(bf16[256,1024]{1,0:T(8,128)(2,1)} %bitcast.56), channel_id=1, source_target_pairs={{0,1},{1,0},{2,3},{3,2},{4,5},{5,4},{6,7},{7,6},{8,9},{9,8},{10,11... | collective-permute-start | bytes 1572872 | tf_op jit(solution)/shard_map/ppermute | solution.py:37
  5.8 3.1 %collective-permute-start = (bf16[384,1024]{1,0:T(8,128)(2,1)}, bf16[384,1024]{1,0:T(8,128)(2,1)}, u32[]{:S(2)}, u32[]{:S(2)}) collective-permute-start(bf16[384,1024]{1,0:T(8,128)(2,1)} %bitcast.48), channel_id=1, source_target_pairs={{0,1},{1,0},{2,3},{3,2},{4,5},{5,4},{6,7},{7,6},{8,9},{9,8},{10,11... | collective-permute-start | bytes 2359304 | tf_op jit(solution)/shard_map/ppermute | solution.py:37
  8.9 4.7 %collective-permute-start.1 = (bf16[1024,256]{1,0:T(8,128)(2,1)}, bf16[1024,256]{1,0:T(8,128)(2,1)}, u32[]{:S(2)}, u32[]{:S(2)}) collective-permute-start(bf16[1024,256]{1,0:T(8,128)(2,1)} %bitcast.52), channel_id=1, source_target_pairs={{0,3},{1,2},{2,1},{3,0},{4,7},{5,6},{6,5},{7,4},{8,11},{9,10},{10,... | collective-permute-start | bytes 1572872 | tf_op jit(solution)/shard_map/ppermute | solution.py:37
  13.6 6.4 %collective-permute-done.7 = bf16[256,1024]{1,0:T(8,128)(2,1)S(1)} collective-permute-done((bf16[256,1024]{1,0:T(8,128)(2,1)}, bf16[256,1024]{1,0:T(8,128)(2,1)S(1)}, u32[]{:S(2)}, u32[]{:S(2)}) %collective-permute-start.7) | collective-permute-done | bytes 524320 | tf_op jit(solution)/shard_map/ppermute | solution.py:37
  20.0 3.0 %collective-permute-done.9 = bf16[384,1024]{1,0:T(8,128)(2,1)S(1)} collective-permute-done((bf16[384,1024]{1,0:T(8,128)(2,1)}, bf16[384,1024]{1,0:T(8,128)(2,1)S(1)}, u32[]{:S(2)}, u32[]{:S(2)}) %collective-permute-start.9) | collective-permute-done | bytes 786464 | tf_op jit(solution)/shard_map/ppermute | solution.py:37
  23.0 2.3 %convolution_convert_fusion.1 = bf16[768,512]{1,0:T(8,128)(2,1)S(1)} fusion(bf16[384,1024]{1,0:T(8,128)(2,1)S(1)} %collective-permute-done.9, bf16[384,1024]{1,0:T(8,128)(2,1)} %bitcast.45, bf16[256,1024]{1,0:T(8,128)(2,1)S(1)} %collective-permute-done.7, bf16[256,1024]{1,0:T(8,128)(2,1)} %bitcast.57), kind=kOutput, calls=%fused_computation.5 | convolution fusion | flops 810942464 | bytes 3407872 | tf_op jit(solution)/shard_map/dot_general | solution.py:22
  25.3 4.6 %collective-permute-start.10 = (bf16[384,512]{1,0:T(8,128)(2,1)S(1)}, bf16[384,512]{1,0:T(8,128)(2,1)S(1)}, u32[]{:S(2)}, u32[]{:S(2)}) collective-permute-start(bf16[384,512]{1,0:T(8,128)(2,1)S(1)} %dynamic-slice_bitcast_fusion), channel_id=1, source_target_pairs={{0,4},{1,5},{2,6},{3,7},{4,0},{5,1},{6,2},{7,3},{8,12},{9,13},{10,... | collective-permute-start | bytes 1179656 | tf_op jit(solution)/shard_map/ppermute | solution.py:37
  30.0 4.3 %collective-permute-done.1 = bf16[1024,256]{1,0:T(8,128)(2,1)} collective-permute-done((bf16[1024,256]{1,0:T(8,128)(2,1)}, bf16[1024,256]{1,0:T(8,128)(2,1)}, u32[]{:S(2)}, u32[]{:S(2)}) %collective-permute-start.1) | collective-permute-done | bytes 524320 | tf_op jit(solution)/shard_map/ppermute | solution.py:37
  34.3 2.4 %convolution_convert_fusion.3 = bf16[768,512]{1,0:T(8,128)(2,1)S(1)} fusion(bf16[384,1024]{1,0:T(8,128)(2,1)} %collective-permute-done, bf16[384,1024]{1,0:T(8,128)(2,1)S(1)} %bitcast.49, bf16[1024,256]{1,0:T(8,128)(2,1)} %collective-permute-done.1, bf16[1024,256]{1,0:T(8,128)(2,1)} %bitcast.53), kind=kOutput, calls=%fused_computation.7 | convolution fusion | flops 810942464 | bytes 3407872 | tf_op jit(solution)/shard_map/dot_general | solution.py:22
  36.8 4.5 %collective-permute-start.2 = (bf16[384,512]{1,0:T(8,128)(2,1)S(1)}, bf16[384,512]{1,0:T(8,128)(2,1)S(1)}, u32[]{:S(2)}, u32[]{:S(2)}) collective-permute-start(bf16[384,512]{1,0:T(8,128)(2,1)S(1)} %dynamic-slice_bitcast_fusion.1), channel_id=1, source_target_pairs={{0,4},{1,5},{2,6},{3,7},{4,0},{5,1},{6,2},{7,3},{8,12},{9,13},{10,... | collective-permute-start | bytes 1179656 | tf_op jit(solution)/shard_map/ppermute | solution.py:37
  41.6 4.3 %collective-permute-start.11 = (bf16[384,256]{1,0:T(8,128)(2,1)S(1)}, bf16[384,256]{1,0:T(8,128)(2,1)S(1)}, u32[]{:S(2)}, u32[]{:S(2)}) collective-permute-start(bf16[384,256]{1,0:T(8,128)(2,1)S(1)} %get-tuple-element.4), channel_id=1, source_target_pairs={{0,508},{1,509},{2,510},{3,511},{4,504},{5,505},{6,506},{7,507},{8... | collective-permute-start | bytes 589832 | tf_op jit(solution)/shard_map/ppermute | solution.py:37
  46.0 2.7 %collective-permute-start.12 = (bf16[384,256]{1,0:T(8,128)(2,1)S(1)}, bf16[384,256]{1,0:T(8,128)(2,1)S(1)}, u32[]{:S(2)}, u32[]{:S(2)}) collective-permute-start(bf16[384,256]{1,0:T(8,128)(2,1)S(1)} %get-tuple-element.5), channel_id=1, source_target_pairs={{0,496},{1,497},{2,498},{3,499},{4,500},{5,501},{6,502},{7,503},{8... | collective-permute-start | bytes 589832 | tf_op jit(solution)/shard_map/ppermute | solution.py:37
  48.7 6.4 %collective-permute-done.2 = bf16[384,512]{1,0:T(8,128)(2,1)S(1)} collective-permute-done((bf16[384,512]{1,0:T(8,128)(2,1)S(1)}, bf16[384,512]{1,0:T(8,128)(2,1)S(1)}, u32[]{:S(2)}, u32[]{:S(2)}) %collective-permute-start.2) | collective-permute-done | bytes 393248 | tf_op jit(solution)/shard_map/ppermute | solution.py:37
  58.3 2.3 %collective-permute-start.13 = (bf16[384,256]{1,0:T(8,128)(2,1)S(1)}, bf16[384,256]{1,0:T(8,128)(2,1)S(1)}, u32[]{:S(2)}, u32[]{:S(2)}) collective-permute-start(bf16[384,256]{1,0:T(8,128)(2,1)S(1)} %add_convert_fusion.2), channel_id=1, source_target_pairs={{0,4},{1,5},{2,6},{3,7},{4,0},{5,1},{6,2},{7,3},{8,12},{9,13},{10,... | collective-permute-start | bytes 589832 | tf_op jit(solution)/shard_map/ppermute | solution.py:37
  60.7 6.4 %collective-permute-start.3 = (bf16[384,256]{1,0:T(8,128)(2,1)S(1)}, bf16[384,256]{1,0:T(8,128)(2,1)S(1)}, u32[]{:S(2)}, u32[]{:S(2)}) collective-permute-start(bf16[384,256]{1,0:T(8,128)(2,1)S(1)} %get-tuple-element.8), channel_id=1, source_target_pairs={{0,28},{1,29},{2,30},{3,31},{4,24},{5,25},{6,26},{7,27},{8,20},{9,... | collective-permute-start | bytes 589832 | tf_op jit(solution)/shard_map/ppermute | solution.py:37
  69.3 4.2 %collective-permute-start.14 = (bf16[384,512]{1,0:T(8,128)(2,1)S(1)}, bf16[384,512]{1,0:T(8,128)(2,1)S(1)}, u32[]{:S(2)}, u32[]{:S(2)}) collective-permute-start(bf16[384,512]{1,0:T(8,128)(2,1)S(1)} %maximum_select_fusion.3), channel_id=1, source_target_pairs={{0,12},{1,13},{2,14},{3,15},{4,8},{5,9},{6,10},{7,11},{8,4},{9,5},... | collective-permute-start | bytes 1179656 | tf_op jit(solution)/shard_map/ppermute | solution.py:37
  74.8 6.4 %collective-permute-done.4 = bf16[384,256]{1,0:T(8,128)(2,1)S(1)} collective-permute-done((bf16[384,256]{1,0:T(8,128)(2,1)S(1)}, bf16[384,256]{1,0:T(8,128)(2,1)S(1)}, u32[]{:S(2)}, u32[]{:S(2)}) %collective-permute-start.4) | collective-permute-done | bytes 196640 | tf_op jit(solution)/shard_map/ppermute | solution.py:37
  83.2 11.1 %collective-permute-done.5 = bf16[384,256]{1,0:T(8,128)(2,1)S(1)} collective-permute-done((bf16[384,256]{1,0:T(8,128)(2,1)S(1)}, bf16[384,256]{1,0:T(8,128)(2,1)S(1)}, u32[]{:S(2)}, u32[]{:S(2)}) %collective-permute-start.5) | collective-permute-done | bytes 196640 | tf_op jit(solution)/shard_map/ppermute | solution.py:37
  100.5 9.8 %collective-permute-done.6 = bf16[384,512]{1,0:T(8,128)(2,1)S(1)} collective-permute-done((bf16[384,512]{1,0:T(8,128)(2,1)S(1)}, bf16[384,512]{1,0:T(8,128)(2,1)S(1)}, u32[]{:S(2)}, u32[]{:S(2)}) %collective-permute-start.6) | collective-permute-done | bytes 393248 | tf_op jit(solution)/shard_map/ppermute | solution.py:37
  115.1 3.9 %collective-permute-start.15 = (bf16[384,1024]{1,0:T(8,128)(2,1)S(1)}, bf16[384,1024]{1,0:T(8,128)(2,1)S(1)}, u32[]{:S(2)}, u32[]{:S(2)}) collective-permute-start(bf16[384,1024]{1,0:T(8,128)(2,1)S(1)} %convolution_convert_fusion), channel_id=1, source_target_pairs={{0,1},{1,0},{2,3},{3,2},{4,5},{5,4},{6,7},{7,6},{8,9},{9,8},{10,11... | collective-permute-start | bytes 2359304 | tf_op jit(solution)/shard_map/ppermute | solution.py:37
  125.0 2.6 %fusion.4 = bf16[1,1024,256]{2,1,0:T(8,128)(2,1)} fusion(bf16[1024,256]{1,0:T(8,128)(2,1)S(1)} %collective-permute-done.17, bf16[384,1024]{1,0:T(8,128)(2,1)} %collective-permute-done, bf16[384,1024]{1,0:T(8,128)(2,1)S(1)} %bitcast.51, bf16[768,512]{1,0:T(8,128)(2,1)S(1)} %maximum_select_fusion.1), kind=kOutput, calls=%fused_computation.16 | convolution fusion | flops 406585344 | bytes 3014656 | tf_op jit(solution)/shard_map/dot_general | solution.py:22
  127.5 11.8 %collective-permute-done.15 = bf16[384,1024]{1,0:T(8,128)(2,1)S(1)} collective-permute-done((bf16[384,1024]{1,0:T(8,128)(2,1)S(1)}, bf16[384,1024]{1,0:T(8,128)(2,1)S(1)}, u32[]{:S(2)}, u32[]{:S(2)}) %collective-permute-start.15) | collective-permute-done | bytes 786464 | tf_op jit(solution)/shard_map/ppermute | solution.py:37
  139.4 2.5 %fusion.3 = bf16[1,384,1024]{2,1,0:T(8,128)(2,1)} fusion(bf16[384,1024]{1,0:T(8,128)(2,1)S(1)} %collective-permute-done.15, bf16[768,512]{1,0:T(8,128)(2,1)S(1)} %maximum_select_fusion.1, bf16[1024,256]{1,0:T(8,128)(2,1)} %collective-permute-done.1, bf16[1024,256]{1,0:T(8,128)(2,1)S(1)} %bitcast.55), kind=kOutput, calls=%fused_computation.13 | convolution fusion | flops 405929984 | bytes 3014656 | tf_op jit(solution)/shard_map/dot_general | solution.py:22
  (48 shorter events, 27.3 us)
Async XLA Ops:
  0.6 22.4 %collective-permute-start.9 = (bf16[384,1024]{1,0:T(8,128)(2,1)}, bf16[384,1024]{1,0:T(8,128)(2,1)S(1)}, u32[]{:S(2)}, u32[]{:S(2)}) collective-permute-start(bf16[384,1024]{1,0:T(8,128)(2,1)} %bitcast.44), channel_id=1, source_target_pairs={{0,3},{1,2},{2,1},{3,0},{4,7},{5,6},{6,5},{7,4},{8,11},{9,10},{10,... | collective-permute-start | bytes 2359304 | tf_op jit(solution)/shard_map/ppermute | solution.py:37
  3.0 17.0 %collective-permute-start.7 = (bf16[256,1024]{1,0:T(8,128)(2,1)}, bf16[256,1024]{1,0:T(8,128)(2,1)S(1)}, u32[]{:S(2)}, u32[]{:S(2)}) collective-permute-start(bf16[256,1024]{1,0:T(8,128)(2,1)} %bitcast.56), channel_id=1, source_target_pairs={{0,1},{1,0},{2,3},{3,2},{4,5},{5,4},{6,7},{7,6},{8,9},{9,8},{10,11... | collective-permute-start | bytes 1572872 | tf_op jit(solution)/shard_map/ppermute | solution.py:37
  5.8 28.5 %collective-permute-start = (bf16[384,1024]{1,0:T(8,128)(2,1)}, bf16[384,1024]{1,0:T(8,128)(2,1)}, u32[]{:S(2)}, u32[]{:S(2)}) collective-permute-start(bf16[384,1024]{1,0:T(8,128)(2,1)} %bitcast.48), channel_id=1, source_target_pairs={{0,1},{1,0},{2,3},{3,2},{4,5},{5,4},{6,7},{7,6},{8,9},{9,8},{10,11... | collective-permute-start | bytes 2359304 | tf_op jit(solution)/shard_map/ppermute | solution.py:37
  8.9 25.4 %collective-permute-start.1 = (bf16[1024,256]{1,0:T(8,128)(2,1)}, bf16[1024,256]{1,0:T(8,128)(2,1)}, u32[]{:S(2)}, u32[]{:S(2)}) collective-permute-start(bf16[1024,256]{1,0:T(8,128)(2,1)} %bitcast.52), channel_id=1, source_target_pairs={{0,3},{1,2},{2,1},{3,0},{4,7},{5,6},{6,5},{7,4},{8,11},{9,10},{10,... | collective-permute-start | bytes 1572872 | tf_op jit(solution)/shard_map/ppermute | solution.py:37
  20.0 3.0 %copy-start.4 = (bf16[256,1024]{1,0:T(8,128)(2,1)}, bf16[256,1024]{1,0:T(8,128)(2,1)S(1)}, u32[]{:S(2)}) copy-start(bf16[256,1024]{1,0:T(8,128)(2,1)S(1)} %collective-permute-done.7) | copy-start | bytes 1572868
  25.3 9.0 %copy-start.1 = (bf16[1,384,1024]{2,1,0:T(8,128)(2,1)S(1)}, bf16[1,384,1024]{2,1,0:T(8,128)(2,1)}, u32[]{:S(2)}) copy-start(bf16[1,384,1024]{2,1,0:T(8,128)(2,1)} %param.4) | copy-start | bytes 2359300
  25.3 16.0 %collective-permute-start.10 = (bf16[384,512]{1,0:T(8,128)(2,1)S(1)}, bf16[384,512]{1,0:T(8,128)(2,1)S(1)}, u32[]{:S(2)}, u32[]{:S(2)}) collective-permute-start(bf16[384,512]{1,0:T(8,128)(2,1)S(1)} %dynamic-slice_bitcast_fusion), channel_id=1, source_target_pairs={{0,4},{1,5},{2,6},{3,7},{4,0},{5,1},{6,2},{7,3},{8,12},{9,13},{10,... | collective-permute-start | bytes 1179656 | tf_op jit(solution)/shard_map/ppermute | solution.py:37
  36.8 18.2 %collective-permute-start.2 = (bf16[384,512]{1,0:T(8,128)(2,1)S(1)}, bf16[384,512]{1,0:T(8,128)(2,1)S(1)}, u32[]{:S(2)}, u32[]{:S(2)}) collective-permute-start(bf16[384,512]{1,0:T(8,128)(2,1)S(1)} %dynamic-slice_bitcast_fusion.1), channel_id=1, source_target_pairs={{0,4},{1,5},{2,6},{3,7},{4,0},{5,1},{6,2},{7,3},{8,12},{9,13},{10,... | collective-permute-start | bytes 1179656 | tf_op jit(solution)/shard_map/ppermute | solution.py:37
  41.6 14.5 %collective-permute-start.11 = (bf16[384,256]{1,0:T(8,128)(2,1)S(1)}, bf16[384,256]{1,0:T(8,128)(2,1)S(1)}, u32[]{:S(2)}, u32[]{:S(2)}) collective-permute-start(bf16[384,256]{1,0:T(8,128)(2,1)S(1)} %get-tuple-element.4), channel_id=1, source_target_pairs={{0,508},{1,509},{2,510},{3,511},{4,504},{5,505},{6,506},{7,507},{8... | collective-permute-start | bytes 589832 | tf_op jit(solution)/shard_map/ppermute | solution.py:37
  46.0 12.3 %collective-permute-start.12 = (bf16[384,256]{1,0:T(8,128)(2,1)S(1)}, bf16[384,256]{1,0:T(8,128)(2,1)S(1)}, u32[]{:S(2)}, u32[]{:S(2)}) collective-permute-start(bf16[384,256]{1,0:T(8,128)(2,1)S(1)} %get-tuple-element.5), channel_id=1, source_target_pairs={{0,496},{1,497},{2,498},{3,499},{4,500},{5,501},{6,502},{7,503},{8... | collective-permute-start | bytes 589832 | tf_op jit(solution)/shard_map/ppermute | solution.py:37
  58.3 10.9 %collective-permute-start.13 = (bf16[384,256]{1,0:T(8,128)(2,1)S(1)}, bf16[384,256]{1,0:T(8,128)(2,1)S(1)}, u32[]{:S(2)}, u32[]{:S(2)}) collective-permute-start(bf16[384,256]{1,0:T(8,128)(2,1)S(1)} %add_convert_fusion.2), channel_id=1, source_target_pairs={{0,4},{1,5},{2,6},{3,7},{4,0},{5,1},{6,2},{7,3},{8,12},{9,13},{10,... | collective-permute-start | bytes 589832 | tf_op jit(solution)/shard_map/ppermute | solution.py:37
  60.7 14.1 %collective-permute-start.3 = (bf16[384,256]{1,0:T(8,128)(2,1)S(1)}, bf16[384,256]{1,0:T(8,128)(2,1)S(1)}, u32[]{:S(2)}, u32[]{:S(2)}) collective-permute-start(bf16[384,256]{1,0:T(8,128)(2,1)S(1)} %get-tuple-element.8), channel_id=1, source_target_pairs={{0,28},{1,29},{2,30},{3,31},{4,24},{5,25},{6,26},{7,27},{8,20},{9,... | collective-permute-start | bytes 589832 | tf_op jit(solution)/shard_map/ppermute | solution.py:37
  67.2 14.0 %collective-permute-start.4 = (bf16[384,256]{1,0:T(8,128)(2,1)S(1)}, bf16[384,256]{1,0:T(8,128)(2,1)S(1)}, u32[]{:S(2)}, u32[]{:S(2)}) collective-permute-start(bf16[384,256]{1,0:T(8,128)(2,1)S(1)} %get-tuple-element.9), channel_id=1, source_target_pairs={{0,16},{1,17},{2,18},{3,19},{4,20},{5,21},{6,22},{7,23},{8,24},{9,... | collective-permute-start | bytes 589832 | tf_op jit(solution)/shard_map/ppermute | solution.py:37
  69.3 27.1 %collective-permute-start.14 = (bf16[384,512]{1,0:T(8,128)(2,1)S(1)}, bf16[384,512]{1,0:T(8,128)(2,1)S(1)}, u32[]{:S(2)}, u32[]{:S(2)}) collective-permute-start(bf16[384,512]{1,0:T(8,128)(2,1)S(1)} %maximum_select_fusion.3), channel_id=1, source_target_pairs={{0,12},{1,13},{2,14},{3,15},{4,8},{5,9},{6,10},{7,11},{8,4},{9,5},... | collective-permute-start | bytes 1179656 | tf_op jit(solution)/shard_map/ppermute | solution.py:37
  81.3 13.0 %collective-permute-start.5 = (bf16[384,256]{1,0:T(8,128)(2,1)S(1)}, bf16[384,256]{1,0:T(8,128)(2,1)S(1)}, u32[]{:S(2)}, u32[]{:S(2)}) collective-permute-start(bf16[384,256]{1,0:T(8,128)(2,1)S(1)} %add_convert_fusion.3), channel_id=1, source_target_pairs={{0,4},{1,5},{2,6},{3,7},{4,0},{5,1},{6,2},{7,3},{8,12},{9,13},{10,... | collective-permute-start | bytes 589832 | tf_op jit(solution)/shard_map/ppermute | solution.py:37
  94.4 16.0 %collective-permute-start.6 = (bf16[384,512]{1,0:T(8,128)(2,1)S(1)}, bf16[384,512]{1,0:T(8,128)(2,1)S(1)}, u32[]{:S(2)}, u32[]{:S(2)}) collective-permute-start(bf16[384,512]{1,0:T(8,128)(2,1)S(1)} %maximum_select_fusion.2), channel_id=1, source_target_pairs={{0,12},{1,13},{2,14},{3,15},{4,8},{5,9},{6,10},{7,11},{8,4},{9,5},... | collective-permute-start | bytes 1179656 | tf_op jit(solution)/shard_map/ppermute | solution.py:37
  98.4 12.2 %copy-start = (bf16[1,384,1024]{2,1,0:T(8,128)(2,1)S(1)}, bf16[1,384,1024]{2,1,0:T(8,128)(2,1)}, u32[]{:S(2)}) copy-start(bf16[1,384,1024]{2,1,0:T(8,128)(2,1)} %param.5) | copy-start | bytes 2359300
  98.5 26.5 %collective-permute-start.17 = (bf16[1024,256]{1,0:T(8,128)(2,1)S(1)}, bf16[1024,256]{1,0:T(8,128)(2,1)S(1)}, u32[]{:S(2)}, u32[]{:S(2)}) collective-permute-start(bf16[1024,256]{1,0:T(8,128)(2,1)S(1)} %convolution_convert_fusion.4), channel_id=1, source_target_pairs={{0,3},{1,2},{2,1},{3,0},{4,7},{5,6},{6,5},{7,4},{8,11},{9,10},{10,... | collective-permute-start | bytes 1572872 | tf_op jit(solution)/shard_map/ppermute | solution.py:37
  110.7 2.7 %copy-start.2 = (bf16[1,1024,256]{2,1,0:T(8,128)(2,1)S(1)}, bf16[1,1024,256]{2,1,0:T(8,128)(2,1)}, u32[]{:S(2)}) copy-start(bf16[1,1024,256]{2,1,0:T(8,128)(2,1)} %param.6) | copy-start | bytes 1572868
  111.3 7.7 %copy-start.3 = (bf16[1,256,1024]{2,1,0:T(8,128)(2,1)S(1)}, bf16[1,256,1024]{2,1,0:T(8,128)(2,1)}, u32[]{:S(2)}) copy-start(bf16[1,256,1024]{2,1,0:T(8,128)(2,1)} %param.7) | copy-start | bytes 1572868
  111.3 7.7 %copy-start.5 = (bf16[256,1024]{1,0:T(8,128)(2,1)S(1)}, bf16[256,1024]{1,0:T(8,128)(2,1)}, u32[]{:S(2)}) copy-start(bf16[256,1024]{1,0:T(8,128)(2,1)} %copy-done.4) | copy-start | bytes 1572868
  111.3 12.2 %collective-permute-start.16 = (bf16[256,1024]{1,0:T(8,128)(2,1)S(1)}, bf16[256,1024]{1,0:T(8,128)(2,1)S(1)}, u32[]{:S(2)}, u32[]{:S(2)}) collective-permute-start(bf16[256,1024]{1,0:T(8,128)(2,1)S(1)} %convolution_convert_fusion.5), channel_id=1, source_target_pairs={{0,1},{1,0},{2,3},{3,2},{4,5},{5,4},{6,7},{7,6},{8,9},{9,8},{10,11... | collective-permute-start | bytes 1572872 | tf_op jit(solution)/shard_map/ppermute | solution.py:37
  115.1 24.3 %collective-permute-start.15 = (bf16[384,1024]{1,0:T(8,128)(2,1)S(1)}, bf16[384,1024]{1,0:T(8,128)(2,1)S(1)}, u32[]{:S(2)}, u32[]{:S(2)}) collective-permute-start(bf16[384,1024]{1,0:T(8,128)(2,1)S(1)} %convolution_convert_fusion), channel_id=1, source_target_pairs={{0,1},{1,0},{2,3},{3,2},{4,5},{5,4},{6,7},{7,6},{8,9},{9,8},{10,11... | collective-permute-start | bytes 2359304 | tf_op jit(solution)/shard_map/ppermute | solution.py:37
  119.6 22.3 %collective-permute-start.8 = (bf16[384,1024]{1,0:T(8,128)(2,1)S(1)}, bf16[384,1024]{1,0:T(8,128)(2,1)S(1)}, u32[]{:S(2)}, u32[]{:S(2)}) collective-permute-start(bf16[384,1024]{1,0:T(8,128)(2,1)S(1)} %convolution_convert_fusion.2), channel_id=1, source_target_pairs={{0,3},{1,2},{2,1},{3,0},{4,7},{5,6},{6,5},{7,4},{8,11},{9,10},{10,... | collective-permute-start | bytes 2359304 | tf_op jit(solution)/shard_map/ppermute | solution.py:37

commit v2 on v1

v2 whole, which is shorter than its diff:
```python
import jax
import jax.numpy as jnp
from jax import lax
from jax.sharding import PartitionSpec as P

AXES = ("section", "tp", "rep")
EVEN = (1, 0, 3, 2)
ODD = (3, 2, 1, 0)


def route(sections, target):
    pairs = []
    for s in range(sections):
        for t in range(4):
            for r in range(4):
                a, b, c = target(s, t, r)
                pairs.append(((s * 4 + t) * 4 + r, ((a % sections) * 4 + b) * 4 + c))
    return pairs


def dot(left, right, dims):
    return lax.dot_general(left, right, (dims, ((), ())), preferred_element_type=jnp.float32)


def bf(x):
    return x.astype(jnp.bfloat16)


def f32(x):
    return x.astype(jnp.float32)


barrier = lax.optimization_barrier


def shards(hidden, cotangent, w_down, w_up):
    sections = lax.axis_size("section")

    def send(x, target):
        return lax.ppermute(x, AXES, route(sections, target))

    def rep_pair(flip):
        table = (EVEN, ODD)
        return lambda s, t, r: (s, t, table[(s + flip) % 2][r])

    def tp_pair(flip, step=0):
        table = (EVEN, ODD)
        return lambda s, t, r: (s + step, table[(s + flip) % 2][t], r)

    parity = lax.axis_index("section") % 2
    tp = lax.axis_index("tp")
    v = ((tp == 1) | (tp == 2)).astype(jnp.int32)
    u = (tp >= 2).astype(jnp.int32)
    first = jnp.where(parity == 0, v, u)
    second = jnp.where(parity == 0, u, v)

    def pick(bit, zero, one):
        return jnp.where(bit == 0, zero, one)

    def reduce_and_shift(own, other, weight, dims, step):
        away = bf(dot(pick(first, other, own), weight, dims))
        came = send(away, tp_pair(0))
        kept = bf(dot(pick(first, own, other), weight, dims))
        half = bf(f32(kept) + f32(came))
        one = send(half, tp_pair(1, step))
        two = send(half, lambda s, t, r: (s + step, t, r))
        return bf(f32(one) + f32(two))

    def complete(half):
        rest = send(half, tp_pair(1))
        return pick(second, half, rest), pick(second, rest, half)

    h, c, wd, wu = hidden[0], cotangent[0], w_down[0], w_up[0]
    c_in = send(c, rep_pair(1))
    wu_in = send(wu, rep_pair(0))
    h_in = send(h, rep_pair(0))
    wd_in = send(wd, rep_pair(1))
    wus = jnp.concatenate([wu, wu_in], 0)
    back_half = reduce_and_shift(c, c_in, wus, ((1,), (1,)), -1)
    wds = jnp.concatenate([wd, wd_in], 1)
    code_half = reduce_and_shift(h, h_in, wds, ((1,), (0,)), 1)
    hs = jnp.concatenate([h, h_in], 0)
    cs = jnp.concatenate([c, c_in], 0)
    back_own, back_other = complete(back_half)
    back = jnp.concatenate([back_own, back_other], 0)
    g_out = bf(dot(back_other, wds, ((1,), (1,))))
    d_out = bf(dot(hs, back[:, 256:], ((0,), (0,))))
    code_half, g_out, d_out = barrier((code_half, g_out, d_out))
    g_in = send(g_out, rep_pair(0))
    d_in = send(d_out, rep_pair(1))
    g_own = dot(back_own, wds, ((1,), (1,)))
    d_own = dot(hs, back[:, :256], ((0,), (0,)))
    code_own, code_other = complete(code_half)
    code = jnp.concatenate([code_own, code_other], 0)
    r_out = bf(dot(code_other, wus, ((1,), (0,))))
    r_in = send(r_out, rep_pair(1))
    u_out = bf(dot(code[:, 256:], cs, ((0,), (0,))))
    u_in = send(u_out, rep_pair(0))
    r_own = dot(code_own, wus, ((1,), (0,)))
    u_own = dot(code[:, :256], cs, ((0,), (0,)))
    r_own, u_own, g_own, d_own = barrier((r_own, u_own, g_own, d_own))
    grad_hidden = bf(g_own + f32(g_in))
    grad_down = bf(d_own + f32(d_in))
    rebuilt = bf(r_own + f32(r_in))
    grad_up = bf(u_own + f32(u_in))
    return (rebuilt[None], grad_hidden[None], grad_up[None], grad_down[None])


def solution(mesh):
    return jax.shard_map(
        shards,
        mesh=mesh,
        in_specs=(
            P("section", "rep", "tp"),
            P("section", "rep", "tp"),
            P("section", "tp", "rep"),
            P("section", "rep", "tp"),
        ),
        out_specs=(
            P("section", "rep", "tp"),
            P("section", "rep", "tp"),
            P("section", "rep", "tp"),
            P("section", "tp", "rep"),
        ),
        check_vma=False,
    )
```

time: 144 us -> 134 us (0.931)
  the two profiles are of different devices: /device:TPU:14 before, /device:TPU:1 now
where the time goes in v2:
time: 134 us; the launch traced here: 133 us
  starting transfers between devices  63.1 us (47%)
  waiting for transfers between devices  49.2 us (37%)
  matrix products  12.9 us (10%)
  other arithmetic  5.47 us (4%)
    ppermute x16, starting transfers between devices, send(): return lax.ppermute(x, AXES, route(sections, target))  63.1 us
    ppermute x16, waiting for transfers between devices, send(): return lax.ppermute(x, AXES, route(sections, target))  49.2 us
    dot_general x12, matrix products, dot(): lax.dot_general(left, right, (dims, ((), ())), preferred_element_type=jnp...  12.9 us
    broadcast_in_dim x4, other arithmetic, shards(): return (rebuilt[None], grad_hidden[None], grad_up[None], grad_down[None])  4.16 us
  transfers between devices with their start and end apart: 16, of which 8 were waited for; matrix products, arithmetic and copies ran while one was open for 10% of the time, Pallas kernels for 0%

profile of v2, /device:TPU:1, one launch (start us, length us, event | category | flops | bytes accessed | tf_op | source)
XLA Modules:
  0.0 132.9 jit_solution(11717160887247369959)
XLA Ops:
  0.6 4.0 %collective-permute-start.5 = (bf16[384,1024]{1,0:T(8,128)(2,1)}, bf16[384,1024]{1,0:T(8,128)(2,1)S(1)}, u32[]{:S(2)}, u32[]{:S(2)}) collective-permute-start(bf16[384,1024]{1,0:T(8,128)(2,1)} %bitcast.45), channel_id=1, source_target_pairs={{0,3},{1,2},{2,1},{3,0},{4,7},{5,6},{6,5},{7,4},{8,11},{9,10},{10,... | collective-permute-start | bytes 2359304 | tf_op jit(solution)/shard_map/ppermute | solution.py:40
  4.6 3.7 %collective-permute-start.6 = (bf16[256,1024]{1,0:T(8,128)(2,1)}, bf16[256,1024]{1,0:T(8,128)(2,1)S(1)}, u32[]{:S(2)}, u32[]{:S(2)}) collective-permute-start(bf16[256,1024]{1,0:T(8,128)(2,1)} %bitcast.37), channel_id=1, source_target_pairs={{0,1},{1,0},{2,3},{3,2},{4,5},{5,4},{6,7},{7,6},{8,9},{9,8},{10,11... | collective-permute-start | bytes 1572872 | tf_op jit(solution)/shard_map/ppermute | solution.py:40
  8.3 2.8 %collective-permute-start = (bf16[384,1024]{1,0:T(8,128)(2,1)}, bf16[384,1024]{1,0:T(8,128)(2,1)}, u32[]{:S(2)}, u32[]{:S(2)}) collective-permute-start(bf16[384,1024]{1,0:T(8,128)(2,1)} %bitcast.42), channel_id=1, source_target_pairs={{0,1},{1,0},{2,3},{3,2},{4,5},{5,4},{6,7},{7,6},{8,9},{9,8},{10,11... | collective-permute-start | bytes 2359304 | tf_op jit(solution)/shard_map/ppermute | solution.py:40
  11.1 1.9 %collective-permute-start.1 = (bf16[1024,256]{1,0:T(8,128)(2,1)}, bf16[1024,256]{1,0:T(8,128)(2,1)S(1)}, u32[]{:S(2)}, u32[]{:S(2)}) collective-permute-start(bf16[1024,256]{1,0:T(8,128)(2,1)} %bitcast.32), channel_id=1, source_target_pairs={{0,3},{1,2},{2,1},{3,0},{4,7},{5,6},{6,5},{7,4},{8,11},{9,10},{10,... | collective-permute-start | bytes 1572872 | tf_op jit(solution)/shard_map/ppermute | solution.py:40
  13.1 5.9 %collective-permute-done.6 = bf16[256,1024]{1,0:T(8,128)(2,1)S(1)} collective-permute-done((bf16[256,1024]{1,0:T(8,128)(2,1)}, bf16[256,1024]{1,0:T(8,128)(2,1)S(1)}, u32[]{:S(2)}, u32[]{:S(2)}) %collective-permute-start.6) | collective-permute-done | bytes 524320 | tf_op jit(solution)/shard_map/ppermute | solution.py:40
  19.0 2.2 %convolution_convert_fusion.4 = bf16[384,512]{1,0:T(8,128)(2,1)S(1)} fusion(bf16[384,1024]{1,0:T(8,128)(2,1)S(1)} %collective-permute-done.5, pred[]{:T(512)S(6)} %eq.28, bf16[1,384,1024]{2,1,0:T(8,128)(2,1)} %param.5, bf16[256,1024]{1,0:T(8,128)(2,1)S(1)} %collective-permute-done.6, bf16[256,1024]{1,0:T(8,128)(2,1)} %bitcast.38), kind=kOutput, calls=%fused_computation.8 | convolution fusion | flops 405340160 | bytes 3014657 | tf_op jit(solution)/shard_map/dot_general | solution.py:22
  21.2 8.9 %collective-permute-start.7 = (bf16[384,512]{1,0:T(8,128)(2,1)S(1)}, bf16[384,512]{1,0:T(8,128)(2,1)S(1)}, u32[]{:S(2)}, u32[]{:S(2)}) collective-permute-start(bf16[384,512]{1,0:T(8,128)(2,1)S(1)} %convolution_convert_fusion.4), channel_id=1, source_target_pairs={{0,4},{1,5},{2,6},{3,7},{4,0},{5,1},{6,2},{7,3},{8,12},{9,13},{10,... | collective-permute-start | bytes 1179656 | tf_op jit(solution)/shard_map/ppermute | solution.py:40
  30.2 5.7 %collective-permute-done = bf16[384,1024]{1,0:T(8,128)(2,1)} collective-permute-done((bf16[384,1024]{1,0:T(8,128)(2,1)}, bf16[384,1024]{1,0:T(8,128)(2,1)}, u32[]{:S(2)}, u32[]{:S(2)}) %collective-permute-start) | collective-permute-done | bytes 786464 | tf_op jit(solution)/shard_map/ppermute | solution.py:40
  37.6 5.4 %collective-permute-start.2 = (bf16[384,512]{1,0:T(8,128)(2,1)S(1)}, bf16[384,512]{1,0:T(8,128)(2,1)S(1)}, u32[]{:S(2)}, u32[]{:S(2)}) collective-permute-start(bf16[384,512]{1,0:T(8,128)(2,1)S(1)} %convolution_convert_fusion.6), channel_id=1, source_target_pairs={{0,4},{1,5},{2,6},{3,7},{4,0},{5,1},{6,2},{7,3},{8,12},{9,13},{10,... | collective-permute-start | bytes 1179656 | tf_op jit(solution)/shard_map/ppermute | solution.py:40
  43.7 3.1 %collective-permute-start.9 = (bf16[384,512]{1,0:T(8,128)(2,1)S(1)}, bf16[384,512]{1,0:T(8,128)(2,1)S(1)}, u32[]{:S(2)}, u32[]{:S(2)}) collective-permute-start(bf16[384,512]{1,0:T(8,128)(2,1)S(1)} %fusion.2), channel_id=1, source_target_pairs={{0,496},{1,497},{2,498},{3,499},{4,500},{5,501},{6,502},{7,503},{8... | collective-permute-start | bytes 1179656 | tf_op jit(solution)/shard_map/ppermute | solution.py:40
  46.8 11.8 %collective-permute-start.8 = (bf16[384,512]{1,0:T(8,128)(2,1)S(1)}, bf16[384,512]{1,0:T(8,128)(2,1)S(1)}, u32[]{:S(2)}, u32[]{:S(2)}) collective-permute-start(bf16[384,512]{1,0:T(8,128)(2,1)S(1)} %fusion.2), channel_id=1, source_target_pairs={{0,508},{1,509},{2,510},{3,511},{4,504},{5,505},{6,506},{7,507},{8... | collective-permute-start | bytes 1179656 | tf_op jit(solution)/shard_map/ppermute | solution.py:40
  61.8 1.9 %collective-permute-start.3 = (bf16[384,512]{1,0:T(8,128)(2,1)}, bf16[384,512]{1,0:T(8,128)(2,1)S(1)}, u32[]{:S(2)}, u32[]{:S(2)}) collective-permute-start(bf16[384,512]{1,0:T(8,128)(2,1)} %fusion.5), channel_id=1, source_target_pairs={{0,28},{1,29},{2,30},{3,31},{4,24},{5,25},{6,26},{7,27},{8,20},{9,... | collective-permute-start | bytes 1179656 | tf_op jit(solution)/shard_map/ppermute | solution.py:40
  63.8 8.7 %collective-permute-done.8 = bf16[384,512]{1,0:T(8,128)(2,1)S(1)} collective-permute-done((bf16[384,512]{1,0:T(8,128)(2,1)S(1)}, bf16[384,512]{1,0:T(8,128)(2,1)S(1)}, u32[]{:S(2)}, u32[]{:S(2)}) %collective-permute-start.8) | collective-permute-done | bytes 393248 | tf_op jit(solution)/shard_map/ppermute | solution.py:40
  72.5 1.9 %collective-permute-start.10 = (bf16[384,512]{1,0:T(8,128)(2,1)S(1)}, bf16[384,512]{1,0:T(8,128)(2,1)}, u32[]{:S(2)}, u32[]{:S(2)}) collective-permute-start(bf16[384,512]{1,0:T(8,128)(2,1)S(1)} %add_convert_fusion.4), channel_id=1, source_target_pairs={{0,12},{1,13},{2,14},{3,15},{4,8},{5,9},{6,10},{7,11},{8,4},{9,5},... | collective-permute-start | bytes 1179656 | tf_op jit(solution)/shard_map/ppermute | solution.py:40
  74.5 6.5 %collective-permute-done.4 = bf16[384,512]{1,0:T(8,128)(2,1)S(1)} collective-permute-done((bf16[384,512]{1,0:T(8,128)(2,1)}, bf16[384,512]{1,0:T(8,128)(2,1)S(1)}, u32[]{:S(2)}, u32[]{:S(2)}) %collective-permute-start.4) | collective-permute-done | bytes 393248 | tf_op jit(solution)/shard_map/ppermute | solution.py:40
  80.9 4.2 %collective-permute-done.3 = bf16[384,512]{1,0:T(8,128)(2,1)S(1)} collective-permute-done((bf16[384,512]{1,0:T(8,128)(2,1)}, bf16[384,512]{1,0:T(8,128)(2,1)S(1)}, u32[]{:S(2)}, u32[]{:S(2)}) %collective-permute-start.3) | collective-permute-done | bytes 393248 | tf_op jit(solution)/shard_map/ppermute | solution.py:40
  85.3 4.0 %collective-permute-done.10 = bf16[384,512]{1,0:T(8,128)(2,1)} collective-permute-done((bf16[384,512]{1,0:T(8,128)(2,1)S(1)}, bf16[384,512]{1,0:T(8,128)(2,1)}, u32[]{:S(2)}, u32[]{:S(2)}) %collective-permute-start.10) | collective-permute-done | bytes 393248 | tf_op jit(solution)/shard_map/ppermute | solution.py:40
  93.2 5.0 %collective-permute-start.11 = (bf16[384,512]{1,0:T(8,128)(2,1)S(1)}, bf16[384,512]{1,0:T(8,128)(2,1)S(1)}, u32[]{:S(2)}, u32[]{:S(2)}) collective-permute-start(bf16[384,512]{1,0:T(8,128)(2,1)S(1)} %add_convert_fusion.5), channel_id=1, source_target_pairs={{0,12},{1,13},{2,14},{3,15},{4,8},{5,9},{6,10},{7,11},{8,4},{9,5},... | collective-permute-start | bytes 1179656 | tf_op jit(solution)/shard_map/ppermute | solution.py:40
  98.2 2.0 %collective-permute-start.15 = (bf16[1024,256]{1,0:T(8,128)(2,1)S(1)}, bf16[1024,256]{1,0:T(8,128)(2,1)S(1)}, u32[]{:S(2)}, u32[]{:S(2)}) collective-permute-start(bf16[1024,256]{1,0:T(8,128)(2,1)S(1)} %convolution_convert_fusion.3), channel_id=1, source_target_pairs={{0,3},{1,2},{2,1},{3,0},{4,7},{5,6},{6,5},{7,4},{8,11},{9,10},{10,... | collective-permute-start | bytes 1572872 | tf_op jit(solution)/shard_map/ppermute | solution.py:40
  100.2 4.2 %collective-permute-start.13 = (bf16[384,1024]{1,0:T(8,128)(2,1)S(1)}, bf16[384,1024]{1,0:T(8,128)(2,1)S(1)}, u32[]{:S(2)}, u32[]{:S(2)}) collective-permute-start(bf16[384,1024]{1,0:T(8,128)(2,1)S(1)} %convolution_convert_fusion.1), channel_id=1, source_target_pairs={{0,1},{1,0},{2,3},{3,2},{4,5},{5,4},{6,7},{7,6},{8,9},{9,8},{10,11... | collective-permute-start | bytes 2359304 | tf_op jit(solution)/shard_map/ppermute | solution.py:40
  108.1 2.3 %collective-permute-start.14 = (bf16[256,1024]{1,0:T(8,128)(2,1)S(1)}, bf16[256,1024]{1,0:T(8,128)(2,1)S(1)}, u32[]{:S(2)}, u32[]{:S(2)}) collective-permute-start(bf16[256,1024]{1,0:T(8,128)(2,1)S(1)} %convolution_convert_fusion.2), channel_id=1, source_target_pairs={{0,1},{1,0},{2,3},{3,2},{4,5},{5,4},{6,7},{7,6},{8,9},{9,8},{10,11... | collective-permute-start | bytes 1572872 | tf_op jit(solution)/shard_map/ppermute | solution.py:40
  112.2 2.4 %collective-permute-start.12 = (bf16[384,1024]{1,0:T(8,128)(2,1)S(1)}, bf16[384,1024]{1,0:T(8,128)(2,1)S(1)}, u32[]{:S(2)}, u32[]{:S(2)}) collective-permute-start(bf16[384,1024]{1,0:T(8,128)(2,1)S(1)} %convolution_convert_fusion), channel_id=1, source_target_pairs={{0,3},{1,2},{2,1},{3,0},{4,7},{5,6},{6,5},{7,4},{8,11},{9,10},{10,... | collective-permute-start | bytes 2359304 | tf_op jit(solution)/shard_map/ppermute | solution.py:40
  115.6 4.0 %collective-permute-done.13 = bf16[384,1024]{1,0:T(8,128)(2,1)S(1)} collective-permute-done((bf16[384,1024]{1,0:T(8,128)(2,1)S(1)}, bf16[384,1024]{1,0:T(8,128)(2,1)S(1)}, u32[]{:S(2)}, u32[]{:S(2)}) %collective-permute-start.13) | collective-permute-done | bytes 786464 | tf_op jit(solution)/shard_map/ppermute | solution.py:40
  120.7 10.1 %collective-permute-done.14 = bf16[256,1024]{1,0:T(8,128)(2,1)S(1)} collective-permute-done((bf16[256,1024]{1,0:T(8,128)(2,1)S(1)}, bf16[256,1024]{1,0:T(8,128)(2,1)S(1)}, u32[]{:S(2)}, u32[]{:S(2)}) %collective-permute-start.14) | collective-permute-done | bytes 524320 | tf_op jit(solution)/shard_map/ppermute | solution.py:40
  (44 shorter events, 19.4 us)
Async XLA Ops:
  0.6 18.4 %collective-permute-start.5 = (bf16[384,1024]{1,0:T(8,128)(2,1)}, bf16[384,1024]{1,0:T(8,128)(2,1)S(1)}, u32[]{:S(2)}, u32[]{:S(2)}) collective-permute-start(bf16[384,1024]{1,0:T(8,128)(2,1)} %bitcast.45), channel_id=1, source_target_pairs={{0,3},{1,2},{2,1},{3,0},{4,7},{5,6},{6,5},{7,4},{8,11},{9,10},{10,... | collective-permute-start | bytes 2359304 | tf_op jit(solution)/shard_map/ppermute | solution.py:40
  4.6 14.4 %collective-permute-start.6 = (bf16[256,1024]{1,0:T(8,128)(2,1)}, bf16[256,1024]{1,0:T(8,128)(2,1)S(1)}, u32[]{:S(2)}, u32[]{:S(2)}) collective-permute-start(bf16[256,1024]{1,0:T(8,128)(2,1)} %bitcast.37), channel_id=1, source_target_pairs={{0,1},{1,0},{2,3},{3,2},{4,5},{5,4},{6,7},{7,6},{8,9},{9,8},{10,11... | collective-permute-start | bytes 1572872 | tf_op jit(solution)/shard_map/ppermute | solution.py:40
  8.3 27.6 %collective-permute-start = (bf16[384,1024]{1,0:T(8,128)(2,1)}, bf16[384,1024]{1,0:T(8,128)(2,1)}, u32[]{:S(2)}, u32[]{:S(2)}) collective-permute-start(bf16[384,1024]{1,0:T(8,128)(2,1)} %bitcast.42), channel_id=1, source_target_pairs={{0,1},{1,0},{2,3},{3,2},{4,5},{5,4},{6,7},{7,6},{8,9},{9,8},{10,11... | collective-permute-start | bytes 2359304 | tf_op jit(solution)/shard_map/ppermute | solution.py:40
  11.1 19.0 %collective-permute-start.1 = (bf16[1024,256]{1,0:T(8,128)(2,1)}, bf16[1024,256]{1,0:T(8,128)(2,1)S(1)}, u32[]{:S(2)}, u32[]{:S(2)}) collective-permute-start(bf16[1024,256]{1,0:T(8,128)(2,1)} %bitcast.32), channel_id=1, source_target_pairs={{0,3},{1,2},{2,1},{3,0},{4,7},{5,6},{6,5},{7,4},{8,11},{9,10},{10,... | collective-permute-start | bytes 1572872 | tf_op jit(solution)/shard_map/ppermute | solution.py:40
  13.1 22.8 %copy-start = (bf16[1,1024,256]{2,1,0:T(8,128)(2,1)S(1)}, bf16[1,1024,256]{2,1,0:T(8,128)(2,1)}, u32[]{:S(2)}) copy-start(bf16[1,1024,256]{2,1,0:T(8,128)(2,1)} %param.6) | copy-start | bytes 1572868
  13.1 22.8 %copy-start.2 = (bf16[1,384,1024]{2,1,0:T(8,128)(2,1)S(1)}, bf16[1,384,1024]{2,1,0:T(8,128)(2,1)}, u32[]{:S(2)}) copy-start(bf16[1,384,1024]{2,1,0:T(8,128)(2,1)} %param.4) | copy-start | bytes 2359300
  19.0 24.0 %copy-start.6 = (bf16[384,1024]{1,0:T(8,128)(2,1)}, bf16[384,1024]{1,0:T(8,128)(2,1)S(1)}, u32[]{:S(2)}) copy-start(bf16[384,1024]{1,0:T(8,128)(2,1)S(1)} %collective-permute-done.5) | copy-start | bytes 2359300
  21.2 21.9 %copy-start.1 = (bf16[1,256,1024]{2,1,0:T(8,128)(2,1)S(1)}, bf16[1,256,1024]{2,1,0:T(8,128)(2,1)}, u32[]{:S(2)}) copy-start(bf16[1,256,1024]{2,1,0:T(8,128)(2,1)} %param.7) | copy-start | bytes 1572868
  21.2 21.9 %copy-start.4 = (bf16[1,384,1024]{2,1,0:T(8,128)(2,1)S(1)}, bf16[1,384,1024]{2,1,0:T(8,128)(2,1)}, u32[]{:S(2)}) copy-start(bf16[1,384,1024]{2,1,0:T(8,128)(2,1)} %param.5) | copy-start | bytes 2359300
  21.2 21.8 %collective-permute-start.7 = (bf16[384,512]{1,0:T(8,128)(2,1)S(1)}, bf16[384,512]{1,0:T(8,128)(2,1)S(1)}, u32[]{:S(2)}, u32[]{:S(2)}) collective-permute-start(bf16[384,512]{1,0:T(8,128)(2,1)S(1)} %convolution_convert_fusion.4), channel_id=1, source_target_pairs={{0,4},{1,5},{2,6},{3,7},{4,0},{5,1},{6,2},{7,3},{8,12},{9,13},{10,... | collective-permute-start | bytes 1179656 | tf_op jit(solution)/shard_map/ppermute | solution.py:40
  37.6 20.9 %collective-permute-start.2 = (bf16[384,512]{1,0:T(8,128)(2,1)S(1)}, bf16[384,512]{1,0:T(8,128)(2,1)S(1)}, u32[]{:S(2)}, u32[]{:S(2)}) collective-permute-start(bf16[384,512]{1,0:T(8,128)(2,1)S(1)} %convolution_convert_fusion.6), channel_id=1, source_target_pairs={{0,4},{1,5},{2,6},{3,7},{4,0},{5,1},{6,2},{7,3},{8,12},{9,13},{10,... | collective-permute-start | bytes 1179656 | tf_op jit(solution)/shard_map/ppermute | solution.py:40
  43.7 20.0 %collective-permute-start.9 = (bf16[384,512]{1,0:T(8,128)(2,1)S(1)}, bf16[384,512]{1,0:T(8,128)(2,1)S(1)}, u32[]{:S(2)}, u32[]{:S(2)}) collective-permute-start(bf16[384,512]{1,0:T(8,128)(2,1)S(1)} %fusion.2), channel_id=1, source_target_pairs={{0,496},{1,497},{2,498},{3,499},{4,500},{5,501},{6,502},{7,503},{8... | collective-permute-start | bytes 1179656 | tf_op jit(solution)/shard_map/ppermute | solution.py:40
  46.8 25.6 %collective-permute-start.8 = (bf16[384,512]{1,0:T(8,128)(2,1)S(1)}, bf16[384,512]{1,0:T(8,128)(2,1)S(1)}, u32[]{:S(2)}, u32[]{:S(2)}) collective-permute-start(bf16[384,512]{1,0:T(8,128)(2,1)S(1)} %fusion.2), channel_id=1, source_target_pairs={{0,508},{1,509},{2,510},{3,511},{4,504},{5,505},{6,506},{7,507},{8... | collective-permute-start | bytes 1179656 | tf_op jit(solution)/shard_map/ppermute | solution.py:40
  59.9 21.0 %collective-permute-start.4 = (bf16[384,512]{1,0:T(8,128)(2,1)}, bf16[384,512]{1,0:T(8,128)(2,1)S(1)}, u32[]{:S(2)}, u32[]{:S(2)}) collective-permute-start(bf16[384,512]{1,0:T(8,128)(2,1)} %fusion.5), channel_id=1, source_target_pairs={{0,16},{1,17},{2,18},{3,19},{4,20},{5,21},{6,22},{7,23},{8,24},{9,... | collective-permute-start | bytes 1179656 | tf_op jit(solution)/shard_map/ppermute | solution.py:40
  61.8 23.3 %collective-permute-start.3 = (bf16[384,512]{1,0:T(8,128)(2,1)}, bf16[384,512]{1,0:T(8,128)(2,1)S(1)}, u32[]{:S(2)}, u32[]{:S(2)}) collective-permute-start(bf16[384,512]{1,0:T(8,128)(2,1)} %fusion.5), channel_id=1, source_target_pairs={{0,28},{1,29},{2,30},{3,31},{4,24},{5,25},{6,26},{7,27},{8,20},{9,... | collective-permute-start | bytes 1179656 | tf_op jit(solution)/shard_map/ppermute | solution.py:40
  72.5 16.7 %collective-permute-start.10 = (bf16[384,512]{1,0:T(8,128)(2,1)S(1)}, bf16[384,512]{1,0:T(8,128)(2,1)}, u32[]{:S(2)}, u32[]{:S(2)}) collective-permute-start(bf16[384,512]{1,0:T(8,128)(2,1)S(1)} %add_convert_fusion.4), channel_id=1, source_target_pairs={{0,12},{1,13},{2,14},{3,15},{4,8},{5,9},{6,10},{7,11},{8,4},{9,5},... | collective-permute-start | bytes 1179656 | tf_op jit(solution)/shard_map/ppermute | solution.py:40
  90.3 1.1 copy-start.3
  93.2 13.6 %collective-permute-start.11 = (bf16[384,512]{1,0:T(8,128)(2,1)S(1)}, bf16[384,512]{1,0:T(8,128)(2,1)S(1)}, u32[]{:S(2)}, u32[]{:S(2)}) collective-permute-start(bf16[384,512]{1,0:T(8,128)(2,1)S(1)} %add_convert_fusion.5), channel_id=1, source_target_pairs={{0,12},{1,13},{2,14},{3,15},{4,8},{5,9},{6,10},{7,11},{8,4},{9,5},... | collective-permute-start | bytes 1179656 | tf_op jit(solution)/shard_map/ppermute | solution.py:40
  98.2 16.4 %collective-permute-start.15 = (bf16[1024,256]{1,0:T(8,128)(2,1)S(1)}, bf16[1024,256]{1,0:T(8,128)(2,1)S(1)}, u32[]{:S(2)}, u32[]{:S(2)}) collective-permute-start(bf16[1024,256]{1,0:T(8,128)(2,1)S(1)} %convolution_convert_fusion.3), channel_id=1, source_target_pairs={{0,3},{1,2},{2,1},{3,0},{4,7},{5,6},{6,5},{7,4},{8,11},{9,10},{10,... | collective-permute-start | bytes 1572872 | tf_op jit(solution)/shard_map/ppermute | solution.py:40
  100.2 19.4 %collective-permute-start.13 = (bf16[384,1024]{1,0:T(8,128)(2,1)S(1)}, bf16[384,1024]{1,0:T(8,128)(2,1)S(1)}, u32[]{:S(2)}, u32[]{:S(2)}) collective-permute-start(bf16[384,1024]{1,0:T(8,128)(2,1)S(1)} %convolution_convert_fusion.1), channel_id=1, source_target_pairs={{0,1},{1,0},{2,3},{3,2},{4,5},{5,4},{6,7},{7,6},{8,9},{9,8},{10,11... | collective-permute-start | bytes 2359304 | tf_op jit(solution)/shard_map/ppermute | solution.py:40
  106.2 1.1 copy-start.5
  106.2 1.4 %copy-start.7 = (bf16[384,1024]{1,0:T(8,128)(2,1)S(1)}, bf16[384,1024]{1,0:T(8,128)(2,1)}, u32[]{:S(2)}) copy-start(bf16[384,1024]{1,0:T(8,128)(2,1)} %copy-done.6) | copy-start | bytes 2359300
  108.1 22.7 %collective-permute-start.14 = (bf16[256,1024]{1,0:T(8,128)(2,1)S(1)}, bf16[256,1024]{1,0:T(8,128)(2,1)S(1)}, u32[]{:S(2)}, u32[]{:S(2)}) collective-permute-start(bf16[256,1024]{1,0:T(8,128)(2,1)S(1)} %convolution_convert_fusion.2), channel_id=1, source_target_pairs={{0,1},{1,0},{2,3},{3,2},{4,5},{5,4},{6,7},{7,6},{8,9},{9,8},{10,11... | collective-permute-start | bytes 1572872 | tf_op jit(solution)/shard_map/ppermute | solution.py:40
  112.2 19.6 %collective-permute-start.12 = (bf16[384,1024]{1,0:T(8,128)(2,1)S(1)}, bf16[384,1024]{1,0:T(8,128)(2,1)S(1)}, u32[]{:S(2)}, u32[]{:S(2)}) collective-permute-start(bf16[384,1024]{1,0:T(8,128)(2,1)S(1)} %convolution_convert_fusion), channel_id=1, source_target_pairs={{0,3},{1,2},{2,1},{3,0},{4,7},{5,6},{6,5},{7,4},{8,11},{9,10},{10,... | collective-permute-start | bytes 2359304 | tf_op jit(solution)/shard_map/ppermute | solution.py:40

commit v3 on v2

--- a/solution.py
+++ b/solution.py
@@ -57,17 +57,30 @@
     def pick(bit, zero, one):
         return jnp.where(bit == 0, zero, one)
 
-    def reduce_and_shift(own, other, weight, dims, step):
+    def half_sum(own, other, weight, dims):
         away = bf(dot(pick(first, other, own), weight, dims))
         came = send(away, tp_pair(0))
         kept = bf(dot(pick(first, own, other), weight, dims))
-        half = bf(f32(kept) + f32(came))
+        return bf(f32(kept) + f32(came))
+
+    def shift(half, step):
         one = send(half, tp_pair(1, step))
         two = send(half, lambda s, t, r: (s + step, t, r))
-        return bf(f32(one) + f32(two))
+        return one, two
 
-    def complete(half):
-        rest = send(half, tp_pair(1))
+    def gather_pairs(half):
+        groups = []
+        for at in range(sections):
+            for one, two in ((0, 1), (3, 2)) if at % 2 == 1 else ((0, 3), (1, 2)):
+                for r in range(4):
+                    groups.append([(at * 4 + one) * 4 + r, (at * 4 + two) * 4 + r])
+        both = lax.all_gather(half, AXES, axis=0, tiled=True, axis_index_groups=groups)
+        return both[:384], both[384:]
+
+    def other_half(half):
+        return send(half, tp_pair(1))
+
+    def in_order(half, rest):
         return pick(second, half, rest), pick(second, rest, half)
 
     h, c, wd, wu = hidden[0], cotangent[0], w_down[0], w_up[0]
@@ -75,33 +88,41 @@
     wu_in = send(wu, rep_pair(0))
     h_in = send(h, rep_pair(0))
     wd_in = send(wd, rep_pair(1))
-    wus = jnp.concatenate([wu, wu_in], 0)
-    back_half = reduce_and_shift(c, c_in, wus, ((1,), (1,)), -1)
-    wds = jnp.concatenate([wd, wd_in], 1)
-    code_half = reduce_and_shift(h, h_in, wds, ((1,), (0,)), 1)
-    hs = jnp.concatenate([h, h_in], 0)
-    cs = jnp.concatenate([c, c_in], 0)
-    back_own, back_other = complete(back_half)
+    back_half = half_sum(c, c_in, jnp.concatenate([wu, wu_in], 0), ((1,), (1,)))
+    code_half = half_sum(h, h_in, jnp.concatenate([wd, wd_in], 1), ((1,), (0,)))
+    back_half, back_kept = shift(back_half, -1)
+    code_half, code_kept = shift(code_half, 1)
+    back_kept, wu, wd, wu_in, wd_in = barrier((back_kept, wu, wd, wu_in, wd_in))
+    wus = barrier(jnp.concatenate([wu, wu_in], 0))
+    wds = barrier(jnp.concatenate([wd, wd_in], 1))
+    back_half = bf(f32(back_half) + f32(back_kept))
+    code_half = bf(f32(code_half) + f32(code_kept))
+    wus_far = send(wus, rep_pair(1))
+    wds_far = send(wds, rep_pair(0))
+    code_half, wus_far, wds_far = barrier((code_half, wus_far, wds_far))
+    hs = barrier(jnp.concatenate([h, h_in], 0))
+    cs = barrier(jnp.concatenate([c, c_in], 0))
+    back_own, back_other = gather_pairs(back_half)
+    code_rest = other_half(code_half)
+    back_far = send(back_other, rep_pair(0))
     back = jnp.concatenate([back_own, back_other], 0)
-    g_out = bf(dot(back_other, wds, ((1,), (1,))))
     d_out = bf(dot(hs, back[:, 256:], ((0,), (0,))))
-    code_half, g_out, d_out = barrier((code_half, g_out, d_out))
-    g_in = send(g_out, rep_pair(0))
     d_in = send(d_out, rep_pair(1))
     g_own = dot(back_own, wds, ((1,), (1,)))
     d_own = dot(hs, back[:, :256], ((0,), (0,)))
-    code_own, code_other = complete(code_half)
+    code_rest, d_out, g_own, d_own = barrier((code_rest, d_out, g_own, d_own))
+    code_own, code_other = in_order(code_half, code_rest)
+    code_far = send(code_other, rep_pair(1))
     code = jnp.concatenate([code_own, code_other], 0)
-    r_out = bf(dot(code_other, wus, ((1,), (0,))))
-    r_in = send(r_out, rep_pair(1))
     u_out = bf(dot(code[:, 256:], cs, ((0,), (0,))))
     u_in = send(u_out, rep_pair(0))
+    code_own, code, u_out = barrier((code_own, code, u_out))
     r_own = dot(code_own, wus, ((1,), (0,)))
     u_own = dot(code[:, :256], cs, ((0,), (0,)))
-    r_own, u_own, g_own, d_own = barrier((r_own, u_own, g_own, d_own))
-    grad_hidden = bf(g_own + f32(g_in))
+    r_own, u_own = barrier((r_own, u_own))
+    grad_hidden = bf(g_own + dot(back_far, wds_far, ((1,), (1,))))
     grad_down = bf(d_own + f32(d_in))
-    rebuilt = bf(r_own + f32(r_in))
+    rebuilt = bf(r_own + dot(code_far, wus_far, ((1,), (0,))))
     grad_up = bf(u_own + f32(u_in))
     return (rebuilt[None], grad_hidden[None], grad_up[None], grad_down[None])
 

time: 134 us -> 127 us (0.948); the launches traced: 133 us -> 124 us
  waiting for transfers between devices: 49.2 us -> 24.9 us
  blocking collectives: 0 us -> 17 us
  starting transfers between devices: 63.1 us -> 68.3 us
  matrix products: 12.9 us -> 9.32 us
  other arithmetic: 5.47 us -> 3.71 us
    ppermute x16 -> x17, waiting for transfers between devices: 49.2 us -> 24.9 us  [send(): return lax.ppermute(x, AXES, route(sections, target))]
    all_gather x0 -> x1, blocking collectives: none -> 17 us  [gather_pairs(): lax.all_gather(half, AXES, axis=0, tiled=True, axis_index_groups=groups)]
    ppermute x16 -> x17, starting transfers between devices: 63.1 us -> 68.3 us  [send(): return lax.ppermute(x, AXES, route(sections, target))]
    dot_general x12, matrix products: 12.9 us -> 9.32 us  [dot(): lax.dot_general(left, right, (dims, ((), ())), preferred_element_type=jnp...]
    broadcast_in_dim x4 -> x3, other arithmetic: 4.16 us -> 3.02 us  [shards(): return (rebuilt[None], grad_hidden[None], grad_up[None], grad_down[None])]
  transfers between devices with their start and end apart: 16 -> 17, of which waited for: 8 -> 6; matrix products, arithmetic and copies ran while one was open for 10% -> 10% of each run, Pallas kernels for 0% -> 0%
where the time goes in v3:
time: 127 us; the launch traced here: 124 us
  starting transfers between devices  68.3 us (54%)
  waiting for transfers between devices  24.9 us (20%)
  blocking collectives  17 us (13%)
  matrix products  9.32 us (7%)
  other arithmetic  3.71 us (3%)
    ppermute x17, starting transfers between devices, send(): return lax.ppermute(x, AXES, route(sections, target))  68.3 us
    ppermute x17, waiting for transfers between devices, send(): return lax.ppermute(x, AXES, route(sections, target))  24.9 us
    all_gather x1, blocking collectives, gather_pairs(): lax.all_gather(half, AXES, axis=0, tiled=True, axis_index_groups=groups)  17 us
    dot_general x12, matrix products, dot(): lax.dot_general(left, right, (dims, ((), ())), preferred_element_type=jnp...  9.32 us
    broadcast_in_dim x3, other arithmetic, shards(): return (rebuilt[None], grad_hidden[None], grad_up[None], grad_down[None])  3.02 us
  transfers between devices with their start and end apart: 17, of which 6 were waited for; matrix products, arithmetic and copies ran while one was open for 10% of the time, Pallas kernels for 0%

profile of v3, /device:TPU:1, one launch (start us, length us, event | category | flops | bytes accessed | tf_op | source)
XLA Modules:
  0.0 124.4 jit_solution(9331157253528780174)
XLA Ops:
  0.6 3.9 %collective-permute-start.5 = (bf16[384,1024]{1,0:T(8,128)(2,1)}, bf16[384,1024]{1,0:T(8,128)(2,1)S(1)}, u32[]{:S(2)}, u32[]{:S(2)}) collective-permute-start(bf16[384,1024]{1,0:T(8,128)(2,1)} %bitcast.39), channel_id=1, source_target_pairs={{0,3},{1,2},{2,1},{3,0},{4,7},{5,6},{6,5},{7,4},{8,11},{9,10},{10,... | collective-permute-start | bytes 2359304 | tf_op jit(solution)/shard_map/ppermute | solution.py:40
  4.6 3.7 %collective-permute-start.6 = (bf16[256,1024]{1,0:T(8,128)(2,1)}, bf16[256,1024]{1,0:T(8,128)(2,1)S(1)}, u32[]{:S(2)}, u32[]{:S(2)}) collective-permute-start(bf16[256,1024]{1,0:T(8,128)(2,1)} %bitcast.43), channel_id=1, source_target_pairs={{0,1},{1,0},{2,3},{3,2},{4,5},{5,4},{6,7},{7,6},{8,9},{9,8},{10,11... | collective-permute-start | bytes 1572872 | tf_op jit(solution)/shard_map/ppermute | solution.py:40
  8.3 2.8 %collective-permute-start = (bf16[384,1024]{1,0:T(8,128)(2,1)}, bf16[384,1024]{1,0:T(8,128)(2,1)S(1)}, u32[]{:S(2)}, u32[]{:S(2)}) collective-permute-start(bf16[384,1024]{1,0:T(8,128)(2,1)} %bitcast.41), channel_id=1, source_target_pairs={{0,1},{1,0},{2,3},{3,2},{4,5},{5,4},{6,7},{7,6},{8,9},{9,8},{10,11... | collective-permute-start | bytes 2359304 | tf_op jit(solution)/shard_map/ppermute | solution.py:40
  11.1 1.9 %collective-permute-start.1 = (bf16[1024,256]{1,0:T(8,128)(2,1)}, bf16[1024,256]{1,0:T(8,128)(2,1)S(1)}, u32[]{:S(2)}, u32[]{:S(2)}) collective-permute-start(bf16[1024,256]{1,0:T(8,128)(2,1)} %bitcast.47), channel_id=1, source_target_pairs={{0,3},{1,2},{2,1},{3,0},{4,7},{5,6},{6,5},{7,4},{8,11},{9,10},{10,... | collective-permute-start | bytes 1572872 | tf_op jit(solution)/shard_map/ppermute | solution.py:40
  13.1 6.0 %collective-permute-done.6 = bf16[256,1024]{1,0:T(8,128)(2,1)S(1)} collective-permute-done((bf16[256,1024]{1,0:T(8,128)(2,1)}, bf16[256,1024]{1,0:T(8,128)(2,1)S(1)}, u32[]{:S(2)}, u32[]{:S(2)}) %collective-permute-start.6) | collective-permute-done | bytes 524320 | tf_op jit(solution)/shard_map/ppermute | solution.py:40
  19.0 1.9 %convolution_convert_fusion.2 = bf16[384,512]{1,0:T(8,128)(2,1)S(1)} fusion(bf16[384,1024]{1,0:T(8,128)(2,1)S(1)} %collective-permute-done.5, pred[]{:T(512)S(6)} %eq.26, bf16[256,1024]{1,0:T(8,128)(2,1)S(1)} %collective-permute-done.6, bf16[256,1024]{1,0:T(8,128)(2,1)} %bitcast.44, bf16[1,384,1024]{2,1,0:T(8,128)(2,1)} %param.5), kind=kOutput, calls=%fused_computation.7 | convolution fusion | flops 405340160 | bytes 3014657 | tf_op jit(solution)/shard_map/dot_general | solution.py:22
  20.9 8.9 %collective-permute-start.7 = (bf16[384,512]{1,0:T(8,128)(2,1)S(1)}, bf16[384,512]{1,0:T(8,128)(2,1)S(1)}, u32[]{:S(2)}, u32[]{:S(2)}) collective-permute-start(bf16[384,512]{1,0:T(8,128)(2,1)S(1)} %convolution_convert_fusion.2), channel_id=1, source_target_pairs={{0,4},{1,5},{2,6},{3,7},{4,0},{5,1},{6,2},{7,3},{8,12},{9,13},{10,... | collective-permute-start | bytes 1179656 | tf_op jit(solution)/shard_map/ppermute | solution.py:40
  30.0 5.9 %collective-permute-done = bf16[384,1024]{1,0:T(8,128)(2,1)S(1)} collective-permute-done((bf16[384,1024]{1,0:T(8,128)(2,1)}, bf16[384,1024]{1,0:T(8,128)(2,1)S(1)}, u32[]{:S(2)}, u32[]{:S(2)}) %collective-permute-start) | collective-permute-done | bytes 786464 | tf_op jit(solution)/shard_map/ppermute | solution.py:40
  36.5 6.6 %collective-permute-start.2 = (bf16[384,512]{1,0:T(8,128)(2,1)S(1)}, bf16[384,512]{1,0:T(8,128)(2,1)S(1)}, u32[]{:S(2)}, u32[]{:S(2)}) collective-permute-start(bf16[384,512]{1,0:T(8,128)(2,1)S(1)} %convolution_convert_fusion.4), channel_id=1, source_target_pairs={{0,4},{1,5},{2,6},{3,7},{4,0},{5,1},{6,2},{7,3},{8,12},{9,13},{10,... | collective-permute-start | bytes 1179656 | tf_op jit(solution)/shard_map/ppermute | solution.py:40
  43.7 6.2 %collective-permute-start.8 = (bf16[384,512]{1,0:T(8,128)(2,1)S(1)}, bf16[384,512]{1,0:T(8,128)(2,1)S(1)}, u32[]{:S(2)}, u32[]{:S(2)}) collective-permute-start(bf16[384,512]{1,0:T(8,128)(2,1)S(1)} %fusion.3), channel_id=1, source_target_pairs={{0,496},{1,497},{2,498},{3,499},{4,500},{5,501},{6,502},{7,503},{8... | collective-permute-start | bytes 1179656 | tf_op jit(solution)/shard_map/ppermute | solution.py:40
  50.0 8.7 %collective-permute-start.12 = (bf16[384,512]{1,0:T(8,128)(2,1)S(1)}, bf16[384,512]{1,0:T(8,128)(2,1)S(1)}, u32[]{:S(2)}, u32[]{:S(2)}) collective-permute-start(bf16[384,512]{1,0:T(8,128)(2,1)S(1)} %fusion.3), channel_id=1, source_target_pairs={{0,508},{1,509},{2,510},{3,511},{4,504},{5,505},{6,506},{7,507},{8... | collective-permute-start | bytes 1179656 | tf_op jit(solution)/shard_map/ppermute | solution.py:40
  59.3 1.9 %collective-permute-start.4 = (bf16[384,512]{1,0:T(8,128)(2,1)S(1)}, bf16[384,512]{1,0:T(8,128)(2,1)S(1)}, u32[]{:S(2)}, u32[]{:S(2)}) collective-permute-start(bf16[384,512]{1,0:T(8,128)(2,1)S(1)} %fusion.6), channel_id=1, source_target_pairs={{0,16},{1,17},{2,18},{3,19},{4,20},{5,21},{6,22},{7,23},{8,24},{9,... | collective-permute-start | bytes 1179656 | tf_op jit(solution)/shard_map/ppermute | solution.py:40
  61.2 1.9 %collective-permute-start.3 = (bf16[384,512]{1,0:T(8,128)(2,1)S(1)}, bf16[384,512]{1,0:T(8,128)(2,1)S(1)}, u32[]{:S(2)}, u32[]{:S(2)}) collective-permute-start(bf16[384,512]{1,0:T(8,128)(2,1)S(1)} %fusion.6), channel_id=1, source_target_pairs={{0,28},{1,29},{2,30},{3,31},{4,24},{5,25},{6,26},{7,27},{8,20},{9,... | collective-permute-start | bytes 1179656 | tf_op jit(solution)/shard_map/ppermute | solution.py:40
  63.3 4.4 %collective-permute-start.10 = (bf16[1024,512]{1,0:T(8,128)(2,1)S(1)}, bf16[1024,512]{1,0:T(8,128)(2,1)S(1)}, u32[]{:S(2)}, u32[]{:S(2)}) collective-permute-start(bf16[1024,512]{1,0:T(8,128)(2,1)S(1)} %pad_maximum_fusion.5), channel_id=1, source_target_pairs={{0,1},{1,0},{2,3},{3,2},{4,5},{5,4},{6,7},{7,6},{8,9},{9,8},{10,11... | collective-permute-start | bytes 3145736 | tf_op jit(solution)/shard_map/ppermute | solution.py:40
  67.7 1.9 %collective-permute-start.9 = (bf16[512,1024]{1,0:T(8,128)(2,1)S(1)}, bf16[512,1024]{1,0:T(8,128)(2,1)S(1)}, u32[]{:S(2)}, u32[]{:S(2)}) collective-permute-start(bf16[512,1024]{1,0:T(8,128)(2,1)S(1)} %pad_maximum_fusion.4), channel_id=1, source_target_pairs={{0,3},{1,2},{2,1},{3,0},{4,7},{5,6},{6,5},{7,4},{8,11},{9,10},{10,... | collective-permute-start | bytes 3145736 | tf_op jit(solution)/shard_map/ppermute | solution.py:40
  69.6 2.5 %collective-permute-done.12 = bf16[384,512]{1,0:T(8,128)(2,1)S(1)} collective-permute-done((bf16[384,512]{1,0:T(8,128)(2,1)S(1)}, bf16[384,512]{1,0:T(8,128)(2,1)S(1)}, u32[]{:S(2)}, u32[]{:S(2)}) %collective-permute-start.12) | collective-permute-done | bytes 393248 | tf_op jit(solution)/shard_map/ppermute | solution.py:40
  72.2 17.0 %all_gather.3 = bf16[768,512]{1,0:T(8,128)(2,1)S(1)} all-gather(bf16[384,512]{1,0:T(8,128)(2,1)S(1)} %add_convert_fusion.4), channel_id=1, replica_groups={{0,12},{1,13},{2,14},{3,15},{4,8},{5,9},{6,10},{7,11},{16,20},{17,21},{..., dimensions={0}, use_global_device_ids=true | all-gather | bytes 1179648 | tf_op jit(solution)/shard_map/all_gather | solution.py:77
  89.9 4.4 %collective-permute-start.14 = (bf16[384,512]{1,0:T(8,128)(2,1)S(1)}, bf16[384,512]{1,0:T(8,128)(2,1)S(1)}, u32[]{:S(2)}, u32[]{:S(2)}) collective-permute-start(bf16[384,512]{1,0:T(8,128)(2,1)S(1)} %slice.31), channel_id=1, source_target_pairs={{0,1},{1,0},{2,3},{3,2},{4,5},{5,4},{6,7},{7,6},{8,9},{9,8},{10,11... | collective-permute-start | bytes 1179656 | tf_op jit(solution)/shard_map/ppermute | solution.py:40
  95.1 5.0 %collective-permute-start.11 = (bf16[384,512]{1,0:T(8,128)(2,1)S(1)}, bf16[384,512]{1,0:T(8,128)(2,1)S(1)}, u32[]{:S(2)}, u32[]{:S(2)}) collective-permute-start(bf16[384,512]{1,0:T(8,128)(2,1)S(1)} %add_convert_fusion.5), channel_id=1, source_target_pairs={{0,12},{1,13},{2,14},{3,15},{4,8},{5,9},{6,10},{7,11},{8,4},{9,5},... | collective-permute-start | bytes 1179656 | tf_op jit(solution)/shard_map/ppermute | solution.py:40
  100.7 1.9 %collective-permute-start.16 = (bf16[1024,256]{1,0:T(8,128)(2,1)S(1)}, bf16[1024,256]{1,0:T(8,128)(2,1)S(1)}, u32[]{:S(2)}, u32[]{:S(2)}) collective-permute-start(bf16[1024,256]{1,0:T(8,128)(2,1)S(1)} %convolution_convert_fusion.1), channel_id=1, source_target_pairs={{0,3},{1,2},{2,1},{3,0},{4,7},{5,6},{6,5},{7,4},{8,11},{9,10},{10,... | collective-permute-start | bytes 1572872 | tf_op jit(solution)/shard_map/ppermute | solution.py:40
  103.3 5.7 %collective-permute-done.11 = bf16[384,512]{1,0:T(8,128)(2,1)S(1)} collective-permute-done((bf16[384,512]{1,0:T(8,128)(2,1)S(1)}, bf16[384,512]{1,0:T(8,128)(2,1)S(1)}, u32[]{:S(2)}, u32[]{:S(2)}) %collective-permute-start.11) | collective-permute-done | bytes 393248 | tf_op jit(solution)/shard_map/ppermute | solution.py:40
  109.1 1.9 %collective-permute-start.13 = (bf16[384,512]{1,0:T(8,128)(2,1)S(1)}, bf16[384,512]{1,0:T(8,128)(2,1)S(1)}, u32[]{:S(2)}, u32[]{:S(2)}) collective-permute-start(bf16[384,512]{1,0:T(8,128)(2,1)S(1)} %get-tuple-element.34), channel_id=1, source_target_pairs={{0,3},{1,2},{2,1},{3,0},{4,7},{5,6},{6,5},{7,4},{8,11},{9,10},{10,... | collective-permute-start | bytes 1179656 | tf_op jit(solution)/shard_map/ppermute | solution.py:40
  111.7 2.2 %collective-permute-start.15 = (bf16[256,1024]{1,0:T(8,128)(2,1)S(1)}, bf16[256,1024]{1,0:T(8,128)(2,1)S(1)}, u32[]{:S(2)}, u32[]{:S(2)}) collective-permute-start(bf16[256,1024]{1,0:T(8,128)(2,1)S(1)} %convolution_convert_fusion), channel_id=1, source_target_pairs={{0,1},{1,0},{2,3},{3,2},{4,5},{5,4},{6,7},{7,6},{8,9},{9,8},{10,11... | collective-permute-start | bytes 1572872 | tf_op jit(solution)/shard_map/ppermute | solution.py:40
  120.1 3.3 %collective-permute-done.15 = bf16[256,1024]{1,0:T(8,128)(2,1)S(1)} collective-permute-done((bf16[256,1024]{1,0:T(8,128)(2,1)S(1)}, bf16[256,1024]{1,0:T(8,128)(2,1)S(1)}, u32[]{:S(2)}, u32[]{:S(2)}) %collective-permute-start.15) | collective-permute-done | bytes 524320 | tf_op jit(solution)/shard_map/ppermute | solution.py:40
  (43 shorter events, 12.7 us)
Async XLA Ops:
  0.6 18.4 %collective-permute-start.5 = (bf16[384,1024]{1,0:T(8,128)(2,1)}, bf16[384,1024]{1,0:T(8,128)(2,1)S(1)}, u32[]{:S(2)}, u32[]{:S(2)}) collective-permute-start(bf16[384,1024]{1,0:T(8,128)(2,1)} %bitcast.39), channel_id=1, source_target_pairs={{0,3},{1,2},{2,1},{3,0},{4,7},{5,6},{6,5},{7,4},{8,11},{9,10},{10,... | collective-permute-start | bytes 2359304 | tf_op jit(solution)/shard_map/ppermute | solution.py:40
  4.6 14.4 %collective-permute-start.6 = (bf16[256,1024]{1,0:T(8,128)(2,1)}, bf16[256,1024]{1,0:T(8,128)(2,1)S(1)}, u32[]{:S(2)}, u32[]{:S(2)}) collective-permute-start(bf16[256,1024]{1,0:T(8,128)(2,1)} %bitcast.43), channel_id=1, source_target_pairs={{0,1},{1,0},{2,3},{3,2},{4,5},{5,4},{6,7},{7,6},{8,9},{9,8},{10,11... | collective-permute-start | bytes 1572872 | tf_op jit(solution)/shard_map/ppermute | solution.py:40
  8.3 27.6 %collective-permute-start = (bf16[384,1024]{1,0:T(8,128)(2,1)}, bf16[384,1024]{1,0:T(8,128)(2,1)S(1)}, u32[]{:S(2)}, u32[]{:S(2)}) collective-permute-start(bf16[384,1024]{1,0:T(8,128)(2,1)} %bitcast.41), channel_id=1, source_target_pairs={{0,1},{1,0},{2,3},{3,2},{4,5},{5,4},{6,7},{7,6},{8,9},{9,8},{10,11... | collective-permute-start | bytes 2359304 | tf_op jit(solution)/shard_map/ppermute | solution.py:40
  11.1 18.9 %collective-permute-start.1 = (bf16[1024,256]{1,0:T(8,128)(2,1)}, bf16[1024,256]{1,0:T(8,128)(2,1)S(1)}, u32[]{:S(2)}, u32[]{:S(2)}) collective-permute-start(bf16[1024,256]{1,0:T(8,128)(2,1)} %bitcast.47), channel_id=1, source_target_pairs={{0,3},{1,2},{2,1},{3,0},{4,7},{5,6},{6,5},{7,4},{8,11},{9,10},{10,... | collective-permute-start | bytes 1572872 | tf_op jit(solution)/shard_map/ppermute | solution.py:40
  13.1 16.8 %copy-start = (bf16[1,384,1024]{2,1,0:T(8,128)(2,1)S(1)}, bf16[1,384,1024]{2,1,0:T(8,128)(2,1)}, u32[]{:S(2)}) copy-start(bf16[1,384,1024]{2,1,0:T(8,128)(2,1)} %param.5) | copy-start | bytes 2359300
  20.9 15.0 %copy-start.1 = (bf16[1,384,1024]{2,1,0:T(8,128)(2,1)S(1)}, bf16[1,384,1024]{2,1,0:T(8,128)(2,1)}, u32[]{:S(2)}) copy-start(bf16[1,384,1024]{2,1,0:T(8,128)(2,1)} %param.4) | copy-start | bytes 2359300
  20.9 14.9 %copy-start.3 = (bf16[1,1024,256]{2,1,0:T(8,128)(2,1)S(1)}, bf16[1,1024,256]{2,1,0:T(8,128)(2,1)}, u32[]{:S(2)}) copy-start(bf16[1,1024,256]{2,1,0:T(8,128)(2,1)} %param.6) | copy-start | bytes 1572868
  20.9 22.1 %collective-permute-start.7 = (bf16[384,512]{1,0:T(8,128)(2,1)S(1)}, bf16[384,512]{1,0:T(8,128)(2,1)S(1)}, u32[]{:S(2)}, u32[]{:S(2)}) collective-permute-start(bf16[384,512]{1,0:T(8,128)(2,1)S(1)} %convolution_convert_fusion.2), channel_id=1, source_target_pairs={{0,4},{1,5},{2,6},{3,7},{4,0},{5,1},{6,2},{7,3},{8,12},{9,13},{10,... | collective-permute-start | bytes 1179656 | tf_op jit(solution)/shard_map/ppermute | solution.py:40
  30.0 13.1 %copy-start.2 = (bf16[1,256,1024]{2,1,0:T(8,128)(2,1)S(1)}, bf16[1,256,1024]{2,1,0:T(8,128)(2,1)}, u32[]{:S(2)}) copy-start(bf16[1,256,1024]{2,1,0:T(8,128)(2,1)} %param.7) | copy-start | bytes 1572868
  36.5 22.2 %collective-permute-start.2 = (bf16[384,512]{1,0:T(8,128)(2,1)S(1)}, bf16[384,512]{1,0:T(8,128)(2,1)S(1)}, u32[]{:S(2)}, u32[]{:S(2)}) collective-permute-start(bf16[384,512]{1,0:T(8,128)(2,1)S(1)} %convolution_convert_fusion.4), channel_id=1, source_target_pairs={{0,4},{1,5},{2,6},{3,7},{4,0},{5,1},{6,2},{7,3},{8,12},{9,13},{10,... | collective-permute-start | bytes 1179656 | tf_op jit(solution)/shard_map/ppermute | solution.py:40
  43.7 19.4 %collective-permute-start.8 = (bf16[384,512]{1,0:T(8,128)(2,1)S(1)}, bf16[384,512]{1,0:T(8,128)(2,1)S(1)}, u32[]{:S(2)}, u32[]{:S(2)}) collective-permute-start(bf16[384,512]{1,0:T(8,128)(2,1)S(1)} %fusion.3), channel_id=1, source_target_pairs={{0,496},{1,497},{2,498},{3,499},{4,500},{5,501},{6,502},{7,503},{8... | collective-permute-start | bytes 1179656 | tf_op jit(solution)/shard_map/ppermute | solution.py:40
  50.0 22.1 %collective-permute-start.12 = (bf16[384,512]{1,0:T(8,128)(2,1)S(1)}, bf16[384,512]{1,0:T(8,128)(2,1)S(1)}, u32[]{:S(2)}, u32[]{:S(2)}) collective-permute-start(bf16[384,512]{1,0:T(8,128)(2,1)S(1)} %fusion.3), channel_id=1, source_target_pairs={{0,508},{1,509},{2,510},{3,511},{4,504},{5,505},{6,506},{7,507},{8... | collective-permute-start | bytes 1179656 | tf_op jit(solution)/shard_map/ppermute | solution.py:40
  59.3 35.7 %collective-permute-start.4 = (bf16[384,512]{1,0:T(8,128)(2,1)S(1)}, bf16[384,512]{1,0:T(8,128)(2,1)S(1)}, u32[]{:S(2)}, u32[]{:S(2)}) collective-permute-start(bf16[384,512]{1,0:T(8,128)(2,1)S(1)} %fusion.6), channel_id=1, source_target_pairs={{0,16},{1,17},{2,18},{3,19},{4,20},{5,21},{6,22},{7,23},{8,24},{9,... | collective-permute-start | bytes 1179656 | tf_op jit(solution)/shard_map/ppermute | solution.py:40
  61.2 33.8 %collective-permute-start.3 = (bf16[384,512]{1,0:T(8,128)(2,1)S(1)}, bf16[384,512]{1,0:T(8,128)(2,1)S(1)}, u32[]{:S(2)}, u32[]{:S(2)}) collective-permute-start(bf16[384,512]{1,0:T(8,128)(2,1)S(1)} %fusion.6), channel_id=1, source_target_pairs={{0,28},{1,29},{2,30},{3,31},{4,24},{5,25},{6,26},{7,27},{8,20},{9,... | collective-permute-start | bytes 1179656 | tf_op jit(solution)/shard_map/ppermute | solution.py:40
  63.3 31.8 %collective-permute-start.10 = (bf16[1024,512]{1,0:T(8,128)(2,1)S(1)}, bf16[1024,512]{1,0:T(8,128)(2,1)S(1)}, u32[]{:S(2)}, u32[]{:S(2)}) collective-permute-start(bf16[1024,512]{1,0:T(8,128)(2,1)S(1)} %pad_maximum_fusion.5), channel_id=1, source_target_pairs={{0,1},{1,0},{2,3},{3,2},{4,5},{5,4},{6,7},{7,6},{8,9},{9,8},{10,11... | collective-permute-start | bytes 3145736 | tf_op jit(solution)/shard_map/ppermute | solution.py:40
  67.7 27.4 %collective-permute-start.9 = (bf16[512,1024]{1,0:T(8,128)(2,1)S(1)}, bf16[512,1024]{1,0:T(8,128)(2,1)S(1)}, u32[]{:S(2)}, u32[]{:S(2)}) collective-permute-start(bf16[512,1024]{1,0:T(8,128)(2,1)S(1)} %pad_maximum_fusion.4), channel_id=1, source_target_pairs={{0,3},{1,2},{2,1},{3,0},{4,7},{5,6},{6,5},{7,4},{8,11},{9,10},{10,... | collective-permute-start | bytes 3145736 | tf_op jit(solution)/shard_map/ppermute | solution.py:40
  89.9 12.8 %collective-permute-start.14 = (bf16[384,512]{1,0:T(8,128)(2,1)S(1)}, bf16[384,512]{1,0:T(8,128)(2,1)S(1)}, u32[]{:S(2)}, u32[]{:S(2)}) collective-permute-start(bf16[384,512]{1,0:T(8,128)(2,1)S(1)} %slice.31), channel_id=1, source_target_pairs={{0,1},{1,0},{2,3},{3,2},{4,5},{5,4},{6,7},{7,6},{8,9},{9,8},{10,11... | collective-permute-start | bytes 1179656 | tf_op jit(solution)/shard_map/ppermute | solution.py:40
  95.1 13.9 %collective-permute-start.11 = (bf16[384,512]{1,0:T(8,128)(2,1)S(1)}, bf16[384,512]{1,0:T(8,128)(2,1)S(1)}, u32[]{:S(2)}, u32[]{:S(2)}) collective-permute-start(bf16[384,512]{1,0:T(8,128)(2,1)S(1)} %add_convert_fusion.5), channel_id=1, source_target_pairs={{0,12},{1,13},{2,14},{3,15},{4,8},{5,9},{6,10},{7,11},{8,4},{9,5},... | collective-permute-start | bytes 1179656 | tf_op jit(solution)/shard_map/ppermute | solution.py:40
  100.7 15.5 %collective-permute-start.16 = (bf16[1024,256]{1,0:T(8,128)(2,1)S(1)}, bf16[1024,256]{1,0:T(8,128)(2,1)S(1)}, u32[]{:S(2)}, u32[]{:S(2)}) collective-permute-start(bf16[1024,256]{1,0:T(8,128)(2,1)S(1)} %convolution_convert_fusion.1), channel_id=1, source_target_pairs={{0,3},{1,2},{2,1},{3,0},{4,7},{5,6},{6,5},{7,4},{8,11},{9,10},{10,... | collective-permute-start | bytes 1572872 | tf_op jit(solution)/shard_map/ppermute | solution.py:40
  109.1 9.5 %collective-permute-start.13 = (bf16[384,512]{1,0:T(8,128)(2,1)S(1)}, bf16[384,512]{1,0:T(8,128)(2,1)S(1)}, u32[]{:S(2)}, u32[]{:S(2)}) collective-permute-start(bf16[384,512]{1,0:T(8,128)(2,1)S(1)} %get-tuple-element.34), channel_id=1, source_target_pairs={{0,3},{1,2},{2,1},{3,0},{4,7},{5,6},{6,5},{7,4},{8,11},{9,10},{10,... | collective-permute-start | bytes 1179656 | tf_op jit(solution)/shard_map/ppermute | solution.py:40
  111.7 11.7 %collective-permute-start.15 = (bf16[256,1024]{1,0:T(8,128)(2,1)S(1)}, bf16[256,1024]{1,0:T(8,128)(2,1)S(1)}, u32[]{:S(2)}, u32[]{:S(2)}) collective-permute-start(bf16[256,1024]{1,0:T(8,128)(2,1)S(1)} %convolution_convert_fusion), channel_id=1, source_target_pairs={{0,1},{1,0},{2,3},{3,2},{4,5},{5,4},{6,7},{7,6},{8,9},{9,8},{10,11... | collective-permute-start | bytes 1572872 | tf_op jit(solution)/shard_map/ppermute | solution.py:40

commit v4 on v3

--- a/solution.py
+++ b/solution.py
@@ -68,15 +68,6 @@
         two = send(half, lambda s, t, r: (s + step, t, r))
         return one, two
 
-    def gather_pairs(half):
-        groups = []
-        for at in range(sections):
-            for one, two in ((0, 1), (3, 2)) if at % 2 == 1 else ((0, 3), (1, 2)):
-                for r in range(4):
-                    groups.append([(at * 4 + one) * 4 + r, (at * 4 + two) * 4 + r])
-        both = lax.all_gather(half, AXES, axis=0, tiled=True, axis_index_groups=groups)
-        return both[:384], both[384:]
-
     def other_half(half):
         return send(half, tp_pair(1))
 
@@ -91,38 +82,38 @@
     back_half = half_sum(c, c_in, jnp.concatenate([wu, wu_in], 0), ((1,), (1,)))
     code_half = half_sum(h, h_in, jnp.concatenate([wd, wd_in], 1), ((1,), (0,)))
     back_half, back_kept = shift(back_half, -1)
+    code_half, wu, wd, wu_in, wd_in = barrier((code_half, wu, wd, wu_in, wd_in))
     code_half, code_kept = shift(code_half, 1)
-    back_kept, wu, wd, wu_in, wd_in = barrier((back_kept, wu, wd, wu_in, wd_in))
     wus = barrier(jnp.concatenate([wu, wu_in], 0))
     wds = barrier(jnp.concatenate([wd, wd_in], 1))
     back_half = bf(f32(back_half) + f32(back_kept))
     code_half = bf(f32(code_half) + f32(code_kept))
     wus_far = send(wus, rep_pair(1))
     wds_far = send(wds, rep_pair(0))
-    code_half, wus_far, wds_far = barrier((code_half, wus_far, wds_far))
     hs = barrier(jnp.concatenate([h, h_in], 0))
     cs = barrier(jnp.concatenate([c, c_in], 0))
-    back_own, back_other = gather_pairs(back_half)
+    back_own, back_other = in_order(back_half, other_half(back_half))
     code_rest = other_half(code_half)
+    back = jnp.concatenate([back_own, back_other], 0)
     back_far = send(back_other, rep_pair(0))
-    back = jnp.concatenate([back_own, back_other], 0)
     d_out = bf(dot(hs, back[:, 256:], ((0,), (0,))))
     d_in = send(d_out, rep_pair(1))
     g_own = dot(back_own, wds, ((1,), (1,)))
     d_own = dot(hs, back[:, :256], ((0,), (0,)))
-    code_rest, d_out, g_own, d_own = barrier((code_rest, d_out, g_own, d_own))
+    code_rest, d_out, wus_far, wds_far = barrier((code_rest, d_out, wus_far, wds_far))
     code_own, code_other = in_order(code_half, code_rest)
     code_far = send(code_other, rep_pair(1))
     code = jnp.concatenate([code_own, code_other], 0)
     u_out = bf(dot(code[:, 256:], cs, ((0,), (0,))))
     u_in = send(u_out, rep_pair(0))
-    code_own, code, u_out = barrier((code_own, code, u_out))
+    code_own, code, u_out, back_far = barrier((code_own, code, u_out, back_far))
     r_own = dot(code_own, wus, ((1,), (0,)))
     u_own = dot(code[:, :256], cs, ((0,), (0,)))
     r_own, u_own = barrier((r_own, u_own))
     grad_hidden = bf(g_own + dot(back_far, wds_far, ((1,), (1,))))
     grad_down = bf(d_own + f32(d_in))
     rebuilt = bf(r_own + dot(code_far, wus_far, ((1,), (0,))))
+    grad_hidden, grad_down, rebuilt, u_in = barrier((grad_hidden, grad_down, rebuilt, u_in))
     grad_up = bf(u_own + f32(u_in))
     return (rebuilt[None], grad_hidden[None], grad_up[None], grad_down[None])
 

time: 127 us -> 123 us (0.969)
  the two profiles are of different devices: /device:TPU:1 before, /device:TPU:16 now
where the time goes in v4:
time: 123 us; the launch traced here: 122 us
  starting transfers between devices  86.8 us (71%)
  waiting for transfers between devices  21.5 us (17%)
  matrix products  11.1 us (9%)
  other arithmetic  1.71 us (1%)
    ppermute x18, starting transfers between devices, send(): return lax.ppermute(x, AXES, route(sections, target))  86.8 us
    ppermute x18, waiting for transfers between devices, send(): return lax.ppermute(x, AXES, route(sections, target))  21.5 us
    dot_general x12, matrix products, dot(): lax.dot_general(left, right, (dims, ((), ())), preferred_element_type=jnp...  11.1 us
  transfers between devices with their start and end apart: 18, of which 7 were waited for; matrix products, arithmetic and copies ran while one was open for 10% of the time, Pallas kernels for 0%

profile of v4, /device:TPU:16, one launch (start us, length us, event | category | flops | bytes accessed | tf_op | source)
XLA Modules:
  0.0 122.2 jit_solution(4877975465779934229)
XLA Ops:
  0.6 4.7 %collective-permute-start = (bf16[384,1024]{1,0:T(8,128)(2,1)}, bf16[384,1024]{1,0:T(8,128)(2,1)S(1)}, u32[]{:S(2)}, u32[]{:S(2)}) collective-permute-start(bf16[384,1024]{1,0:T(8,128)(2,1)} %bitcast.37), channel_id=1, source_target_pairs={{0,3},{1,2},{2,1},{3,0},{4,7},{5,6},{6,5},{7,4},{8,11},{9,10},{10,... | collective-permute-start | bytes 2359304 | tf_op jit(solution)/shard_map/ppermute | solution.py:40
  5.3 2.1 %collective-permute-start.1 = (bf16[256,1024]{1,0:T(8,128)(2,1)}, bf16[256,1024]{1,0:T(8,128)(2,1)S(1)}, u32[]{:S(2)}, u32[]{:S(2)}) collective-permute-start(bf16[256,1024]{1,0:T(8,128)(2,1)} %bitcast.47), channel_id=1, source_target_pairs={{0,1},{1,0},{2,3},{3,2},{4,5},{5,4},{6,7},{7,6},{8,9},{9,8},{10,11... | collective-permute-start | bytes 1572872 | tf_op jit(solution)/shard_map/ppermute | solution.py:40
  7.4 3.7 %collective-permute-start.6 = (bf16[384,1024]{1,0:T(8,128)(2,1)}, bf16[384,1024]{1,0:T(8,128)(2,1)S(1)}, u32[]{:S(2)}, u32[]{:S(2)}) collective-permute-start(bf16[384,1024]{1,0:T(8,128)(2,1)} %bitcast.39), channel_id=1, source_target_pairs={{0,1},{1,0},{2,3},{3,2},{4,5},{5,4},{6,7},{7,6},{8,9},{9,8},{10,11... | collective-permute-start | bytes 2359304 | tf_op jit(solution)/shard_map/ppermute | solution.py:40
  11.2 2.4 %collective-permute-start.7 = (bf16[1024,256]{1,0:T(8,128)(2,1)}, bf16[1024,256]{1,0:T(8,128)(2,1)S(1)}, u32[]{:S(2)}, u32[]{:S(2)}) collective-permute-start(bf16[1024,256]{1,0:T(8,128)(2,1)} %bitcast.43), channel_id=1, source_target_pairs={{0,3},{1,2},{2,1},{3,0},{4,7},{5,6},{6,5},{7,4},{8,11},{9,10},{10,... | collective-permute-start | bytes 1572872 | tf_op jit(solution)/shard_map/ppermute | solution.py:40
  13.6 8.7 %collective-permute-done.1 = bf16[256,1024]{1,0:T(8,128)(2,1)S(1)} collective-permute-done((bf16[256,1024]{1,0:T(8,128)(2,1)}, bf16[256,1024]{1,0:T(8,128)(2,1)S(1)}, u32[]{:S(2)}, u32[]{:S(2)}) %collective-permute-start.1) | collective-permute-done | bytes 524320 | tf_op jit(solution)/shard_map/ppermute | solution.py:40
  22.3 1.9 %convolution_convert_fusion.4 = bf16[384,512]{1,0:T(8,128)(2,1)S(1)} fusion(bf16[384,1024]{1,0:T(8,128)(2,1)S(1)} %collective-permute-done, pred[]{:T(512)S(6)} %eq.28, bf16[256,1024]{1,0:T(8,128)(2,1)S(1)} %collective-permute-done.1, bf16[256,1024]{1,0:T(8,128)(2,1)} %bitcast.48, bf16[1,384,1024]{2,1,0:T(8,128)(2,1)} %param.5), kind=kOutput, calls=%fused_computation.13 | convolution fusion | flops 405340160 | bytes 3014657 | tf_op jit(solution)/shard_map/dot_general | solution.py:22
  24.2 9.9 %collective-permute-start.2 = (bf16[384,512]{1,0:T(8,128)(2,1)S(1)}, bf16[384,512]{1,0:T(8,128)(2,1)S(1)}, u32[]{:S(2)}, u32[]{:S(2)}) collective-permute-start(bf16[384,512]{1,0:T(8,128)(2,1)S(1)} %convolution_convert_fusion.4), channel_id=1, source_target_pairs={{0,4},{1,5},{2,6},{3,7},{4,0},{5,1},{6,2},{7,3},{8,12},{9,13},{10,... | collective-permute-start | bytes 1179656 | tf_op jit(solution)/shard_map/ppermute | solution.py:40
  34.7 5.8 %collective-permute-start.8 = (bf16[384,512]{1,0:T(8,128)(2,1)S(1)}, bf16[384,512]{1,0:T(8,128)(2,1)S(1)}, u32[]{:S(2)}, u32[]{:S(2)}) collective-permute-start(bf16[384,512]{1,0:T(8,128)(2,1)S(1)} %convolution_convert_fusion.2), channel_id=1, source_target_pairs={{0,4},{1,5},{2,6},{3,7},{4,0},{5,1},{6,2},{7,3},{8,12},{9,13},{10,... | collective-permute-start | bytes 1179656 | tf_op jit(solution)/shard_map/ppermute | solution.py:40
  40.7 1.9 %collective-permute-done.2 = bf16[384,512]{1,0:T(8,128)(2,1)S(1)} collective-permute-done((bf16[384,512]{1,0:T(8,128)(2,1)S(1)}, bf16[384,512]{1,0:T(8,128)(2,1)S(1)}, u32[]{:S(2)}, u32[]{:S(2)}) %collective-permute-start.2) | collective-permute-done | bytes 393248 | tf_op jit(solution)/shard_map/ppermute | solution.py:40
  43.3 9.9 %collective-permute-start.4 = (bf16[384,512]{1,0:T(8,128)(2,1)S(1)}, bf16[384,512]{1,0:T(8,128)(2,1)S(1)}, u32[]{:S(2)}, u32[]{:S(2)}) collective-permute-start(bf16[384,512]{1,0:T(8,128)(2,1)S(1)} %fusion.6), channel_id=1, source_target_pairs={{0,496},{1,497},{2,498},{3,499},{4,500},{5,501},{6,502},{7,503},{8... | collective-permute-start | bytes 1179656 | tf_op jit(solution)/shard_map/ppermute | solution.py:40
  53.2 2.6 %collective-permute-start.3 = (bf16[384,512]{1,0:T(8,128)(2,1)S(1)}, bf16[384,512]{1,0:T(8,128)(2,1)S(1)}, u32[]{:S(2)}, u32[]{:S(2)}) collective-permute-start(bf16[384,512]{1,0:T(8,128)(2,1)S(1)} %fusion.6), channel_id=1, source_target_pairs={{0,508},{1,509},{2,510},{3,511},{4,504},{5,505},{6,506},{7,507},{8... | collective-permute-start | bytes 1179656 | tf_op jit(solution)/shard_map/ppermute | solution.py:40
  56.4 2.1 %collective-permute-start.10 = (bf16[384,512]{1,0:T(8,128)(2,1)S(1)}, bf16[384,512]{1,0:T(8,128)(2,1)S(1)}, u32[]{:S(2)}, u32[]{:S(2)}) collective-permute-start(bf16[384,512]{1,0:T(8,128)(2,1)S(1)} %fusion.3), channel_id=1, source_target_pairs={{0,16},{1,17},{2,18},{3,19},{4,20},{5,21},{6,22},{7,23},{8,24},{9,... | collective-permute-start | bytes 1179656 | tf_op jit(solution)/shard_map/ppermute | solution.py:40
  58.5 4.5 %collective-permute-start.9 = (bf16[384,512]{1,0:T(8,128)(2,1)S(1)}, bf16[384,512]{1,0:T(8,128)(2,1)S(1)}, u32[]{:S(2)}, u32[]{:S(2)}) collective-permute-start(bf16[384,512]{1,0:T(8,128)(2,1)S(1)} %fusion.3), channel_id=1, source_target_pairs={{0,28},{1,29},{2,30},{3,31},{4,24},{5,25},{6,26},{7,27},{8,20},{9,... | collective-permute-start | bytes 1179656 | tf_op jit(solution)/shard_map/ppermute | solution.py:40
  63.2 4.7 %collective-permute-start.12 = (bf16[512,1024]{1,0:T(8,128)(2,1)S(1)}, bf16[512,1024]{1,0:T(8,128)(2,1)S(1)}, u32[]{:S(2)}, u32[]{:S(2)}) collective-permute-start(bf16[512,1024]{1,0:T(8,128)(2,1)S(1)} %pad_maximum_fusion.5), channel_id=1, source_target_pairs={{0,3},{1,2},{2,1},{3,0},{4,7},{5,6},{6,5},{7,4},{8,11},{9,10},{10,... | collective-permute-start | bytes 3145736 | tf_op jit(solution)/shard_map/ppermute | solution.py:40
  67.9 1.9 %collective-permute-start.13 = (bf16[1024,512]{1,0:T(8,128)(2,1)S(1)}, bf16[1024,512]{1,0:T(8,128)(2,1)S(1)}, u32[]{:S(2)}, u32[]{:S(2)}) collective-permute-start(bf16[1024,512]{1,0:T(8,128)(2,1)S(1)} %pad_maximum_fusion.4), channel_id=1, source_target_pairs={{0,1},{1,0},{2,3},{3,2},{4,5},{5,4},{6,7},{7,6},{8,9},{9,8},{10,11... | collective-permute-start | bytes 3145736 | tf_op jit(solution)/shard_map/ppermute | solution.py:40
  69.8 2.3 %collective-permute-done.3 = bf16[384,512]{1,0:T(8,128)(2,1)S(1)} collective-permute-done((bf16[384,512]{1,0:T(8,128)(2,1)S(1)}, bf16[384,512]{1,0:T(8,128)(2,1)S(1)}, u32[]{:S(2)}, u32[]{:S(2)}) %collective-permute-start.3) | collective-permute-done | bytes 393248 | tf_op jit(solution)/shard_map/ppermute | solution.py:40
  72.3 1.9 %collective-permute-start.5 = (bf16[384,512]{1,0:T(8,128)(2,1)S(1)}, bf16[384,512]{1,0:T(8,128)(2,1)S(1)}, u32[]{:S(2)}, u32[]{:S(2)}) collective-permute-start(bf16[384,512]{1,0:T(8,128)(2,1)S(1)} %add_convert_fusion.4), channel_id=1, source_target_pairs={{0,12},{1,13},{2,14},{3,15},{4,8},{5,9},{6,10},{7,11},{8,4},{9,5},... | collective-permute-start | bytes 1179656 | tf_op jit(solution)/shard_map/ppermute | solution.py:40
  76.1 18.9 %collective-permute-start.11 = (bf16[384,512]{1,0:T(8,128)(2,1)S(1)}, bf16[384,512]{1,0:T(8,128)(2,1)S(1)}, u32[]{:S(2)}, u32[]{:S(2)}) collective-permute-start(bf16[384,512]{1,0:T(8,128)(2,1)S(1)} %add_convert_fusion.3), channel_id=1, source_target_pairs={{0,12},{1,13},{2,14},{3,15},{4,8},{5,9},{6,10},{7,11},{8,4},{9,5},... | collective-permute-start | bytes 1179656 | tf_op jit(solution)/shard_map/ppermute | solution.py:40
  95.1 1.9 %collective-permute-start.14 = (bf16[384,512]{1,0:T(8,128)(2,1)S(1)}, bf16[384,512]{1,0:T(8,128)(2,1)S(1)}, u32[]{:S(2)}, u32[]{:S(2)}) collective-permute-start(bf16[384,512]{1,0:T(8,128)(2,1)S(1)} %get-tuple-element.40), channel_id=1, source_target_pairs={{0,1},{1,0},{2,3},{3,2},{4,5},{5,4},{6,7},{7,6},{8,9},{9,8},{10,11... | collective-permute-start | bytes 1179656 | tf_op jit(solution)/shard_map/ppermute | solution.py:40
  97.6 4.3 %collective-permute-start.15 = (bf16[1024,256]{1,0:T(8,128)(2,1)S(1)}, bf16[1024,256]{1,0:T(8,128)(2,1)S(1)}, u32[]{:S(2)}, u32[]{:S(2)}) collective-permute-start(bf16[1024,256]{1,0:T(8,128)(2,1)S(1)} %convolution_convert_fusion.1), channel_id=1, source_target_pairs={{0,3},{1,2},{2,1},{3,0},{4,7},{5,6},{6,5},{7,4},{8,11},{9,10},{10,... | collective-permute-start | bytes 1572872 | tf_op jit(solution)/shard_map/ppermute | solution.py:40
  101.9 3.0 %collective-permute-done.11 = bf16[384,512]{1,0:T(8,128)(2,1)S(1)} collective-permute-done((bf16[384,512]{1,0:T(8,128)(2,1)S(1)}, bf16[384,512]{1,0:T(8,128)(2,1)S(1)}, u32[]{:S(2)}, u32[]{:S(2)}) %collective-permute-start.11) | collective-permute-done | bytes 393248 | tf_op jit(solution)/shard_map/ppermute | solution.py:40
  104.9 3.5 %collective-permute-start.16 = (bf16[384,512]{1,0:T(8,128)(2,1)S(1)}, bf16[384,512]{1,0:T(8,128)(2,1)S(1)}, u32[]{:S(2)}, u32[]{:S(2)}) collective-permute-start(bf16[384,512]{1,0:T(8,128)(2,1)S(1)} %get-tuple-element.38), channel_id=1, source_target_pairs={{0,3},{1,2},{2,1},{3,0},{4,7},{5,6},{6,5},{7,4},{8,11},{9,10},{10,... | collective-permute-start | bytes 1179656 | tf_op jit(solution)/shard_map/ppermute | solution.py:40
  109.1 1.9 %collective-permute-start.17 = (bf16[256,1024]{1,0:T(8,128)(2,1)S(1)}, bf16[256,1024]{1,0:T(8,128)(2,1)S(1)}, u32[]{:S(2)}, u32[]{:S(2)}) collective-permute-start(bf16[256,1024]{1,0:T(8,128)(2,1)S(1)} %convolution_convert_fusion), channel_id=1, source_target_pairs={{0,1},{1,0},{2,3},{3,2},{4,5},{5,4},{6,7},{7,6},{8,9},{9,8},{10,11... | collective-permute-start | bytes 1572872 | tf_op jit(solution)/shard_map/ppermute | solution.py:40
  115.8 4.0 %collective-permute-done.16 = bf16[384,512]{1,0:T(8,128)(2,1)S(1)} collective-permute-done((bf16[384,512]{1,0:T(8,128)(2,1)S(1)}, bf16[384,512]{1,0:T(8,128)(2,1)S(1)}, u32[]{:S(2)}, u32[]{:S(2)}) %collective-permute-start.16) | collective-permute-done | bytes 393248 | tf_op jit(solution)/shard_map/ppermute | solution.py:40
  (42 shorter events, 12.7 us)
Async XLA Ops:
  0.6 21.7 %collective-permute-start = (bf16[384,1024]{1,0:T(8,128)(2,1)}, bf16[384,1024]{1,0:T(8,128)(2,1)S(1)}, u32[]{:S(2)}, u32[]{:S(2)}) collective-permute-start(bf16[384,1024]{1,0:T(8,128)(2,1)} %bitcast.37), channel_id=1, source_target_pairs={{0,3},{1,2},{2,1},{3,0},{4,7},{5,6},{6,5},{7,4},{8,11},{9,10},{10,... | collective-permute-start | bytes 2359304 | tf_op jit(solution)/shard_map/ppermute | solution.py:40
  5.3 17.0 %collective-permute-start.1 = (bf16[256,1024]{1,0:T(8,128)(2,1)}, bf16[256,1024]{1,0:T(8,128)(2,1)S(1)}, u32[]{:S(2)}, u32[]{:S(2)}) collective-permute-start(bf16[256,1024]{1,0:T(8,128)(2,1)} %bitcast.47), channel_id=1, source_target_pairs={{0,1},{1,0},{2,3},{3,2},{4,5},{5,4},{6,7},{7,6},{8,9},{9,8},{10,11... | collective-permute-start | bytes 1572872 | tf_op jit(solution)/shard_map/ppermute | solution.py:40
  7.4 26.7 %collective-permute-start.6 = (bf16[384,1024]{1,0:T(8,128)(2,1)}, bf16[384,1024]{1,0:T(8,128)(2,1)S(1)}, u32[]{:S(2)}, u32[]{:S(2)}) collective-permute-start(bf16[384,1024]{1,0:T(8,128)(2,1)} %bitcast.39), channel_id=1, source_target_pairs={{0,1},{1,0},{2,3},{3,2},{4,5},{5,4},{6,7},{7,6},{8,9},{9,8},{10,11... | collective-permute-start | bytes 2359304 | tf_op jit(solution)/shard_map/ppermute | solution.py:40
  11.2 22.9 %collective-permute-start.7 = (bf16[1024,256]{1,0:T(8,128)(2,1)}, bf16[1024,256]{1,0:T(8,128)(2,1)S(1)}, u32[]{:S(2)}, u32[]{:S(2)}) collective-permute-start(bf16[1024,256]{1,0:T(8,128)(2,1)} %bitcast.43), channel_id=1, source_target_pairs={{0,3},{1,2},{2,1},{3,0},{4,7},{5,6},{6,5},{7,4},{8,11},{9,10},{10,... | collective-permute-start | bytes 1572872 | tf_op jit(solution)/shard_map/ppermute | solution.py:40
  13.6 20.5 %copy-start.1 = (bf16[1,384,1024]{2,1,0:T(8,128)(2,1)S(1)}, bf16[1,384,1024]{2,1,0:T(8,128)(2,1)}, u32[]{:S(2)}) copy-start(bf16[1,384,1024]{2,1,0:T(8,128)(2,1)} %param.4) | copy-start | bytes 2359300
  13.6 20.5 %copy-start.2 = (bf16[1,1024,256]{2,1,0:T(8,128)(2,1)S(1)}, bf16[1,1024,256]{2,1,0:T(8,128)(2,1)}, u32[]{:S(2)}) copy-start(bf16[1,1024,256]{2,1,0:T(8,128)(2,1)} %param.6) | copy-start | bytes 1572868
  24.2 16.4 %copy-start = (bf16[1,384,1024]{2,1,0:T(8,128)(2,1)S(1)}, bf16[1,384,1024]{2,1,0:T(8,128)(2,1)}, u32[]{:S(2)}) copy-start(bf16[1,384,1024]{2,1,0:T(8,128)(2,1)} %param.5) | copy-start | bytes 2359300
  24.2 18.4 %collective-permute-start.2 = (bf16[384,512]{1,0:T(8,128)(2,1)S(1)}, bf16[384,512]{1,0:T(8,128)(2,1)S(1)}, u32[]{:S(2)}, u32[]{:S(2)}) collective-permute-start(bf16[384,512]{1,0:T(8,128)(2,1)S(1)} %convolution_convert_fusion.4), channel_id=1, source_target_pairs={{0,4},{1,5},{2,6},{3,7},{4,0},{5,1},{6,2},{7,3},{8,12},{9,13},{10,... | collective-permute-start | bytes 1179656 | tf_op jit(solution)/shard_map/ppermute | solution.py:40
  34.7 7.9 %copy-start.3 = (bf16[1,256,1024]{2,1,0:T(8,128)(2,1)S(1)}, bf16[1,256,1024]{2,1,0:T(8,128)(2,1)}, u32[]{:S(2)}) copy-start(bf16[1,256,1024]{2,1,0:T(8,128)(2,1)} %param.7) | copy-start | bytes 1572868
  34.7 21.1 %collective-permute-start.8 = (bf16[384,512]{1,0:T(8,128)(2,1)S(1)}, bf16[384,512]{1,0:T(8,128)(2,1)S(1)}, u32[]{:S(2)}, u32[]{:S(2)}) collective-permute-start(bf16[384,512]{1,0:T(8,128)(2,1)S(1)} %convolution_convert_fusion.2), channel_id=1, source_target_pairs={{0,4},{1,5},{2,6},{3,7},{4,0},{5,1},{6,2},{7,3},{8,12},{9,13},{10,... | collective-permute-start | bytes 1179656 | tf_op jit(solution)/shard_map/ppermute | solution.py:40
  43.3 24.6 %collective-permute-start.4 = (bf16[384,512]{1,0:T(8,128)(2,1)S(1)}, bf16[384,512]{1,0:T(8,128)(2,1)S(1)}, u32[]{:S(2)}, u32[]{:S(2)}) collective-permute-start(bf16[384,512]{1,0:T(8,128)(2,1)S(1)} %fusion.6), channel_id=1, source_target_pairs={{0,496},{1,497},{2,498},{3,499},{4,500},{5,501},{6,502},{7,503},{8... | collective-permute-start | bytes 1179656 | tf_op jit(solution)/shard_map/ppermute | solution.py:40
  53.2 19.0 %collective-permute-start.3 = (bf16[384,512]{1,0:T(8,128)(2,1)S(1)}, bf16[384,512]{1,0:T(8,128)(2,1)S(1)}, u32[]{:S(2)}, u32[]{:S(2)}) collective-permute-start(bf16[384,512]{1,0:T(8,128)(2,1)S(1)} %fusion.6), channel_id=1, source_target_pairs={{0,508},{1,509},{2,510},{3,511},{4,504},{5,505},{6,506},{7,507},{8... | collective-permute-start | bytes 1179656 | tf_op jit(solution)/shard_map/ppermute | solution.py:40
  56.4 18.9 %collective-permute-start.10 = (bf16[384,512]{1,0:T(8,128)(2,1)S(1)}, bf16[384,512]{1,0:T(8,128)(2,1)S(1)}, u32[]{:S(2)}, u32[]{:S(2)}) collective-permute-start(bf16[384,512]{1,0:T(8,128)(2,1)S(1)} %fusion.3), channel_id=1, source_target_pairs={{0,16},{1,17},{2,18},{3,19},{4,20},{5,21},{6,22},{7,23},{8,24},{9,... | collective-permute-start | bytes 1179656 | tf_op jit(solution)/shard_map/ppermute | solution.py:40
  58.5 17.5 %collective-permute-start.9 = (bf16[384,512]{1,0:T(8,128)(2,1)S(1)}, bf16[384,512]{1,0:T(8,128)(2,1)S(1)}, u32[]{:S(2)}, u32[]{:S(2)}) collective-permute-start(bf16[384,512]{1,0:T(8,128)(2,1)S(1)} %fusion.3), channel_id=1, source_target_pairs={{0,28},{1,29},{2,30},{3,31},{4,24},{5,25},{6,26},{7,27},{8,20},{9,... | collective-permute-start | bytes 1179656 | tf_op jit(solution)/shard_map/ppermute | solution.py:40
  63.2 41.6 %collective-permute-start.12 = (bf16[512,1024]{1,0:T(8,128)(2,1)S(1)}, bf16[512,1024]{1,0:T(8,128)(2,1)S(1)}, u32[]{:S(2)}, u32[]{:S(2)}) collective-permute-start(bf16[512,1024]{1,0:T(8,128)(2,1)S(1)} %pad_maximum_fusion.5), channel_id=1, source_target_pairs={{0,3},{1,2},{2,1},{3,0},{4,7},{5,6},{6,5},{7,4},{8,11},{9,10},{10,... | collective-permute-start | bytes 3145736 | tf_op jit(solution)/shard_map/ppermute | solution.py:40
  67.9 36.9 %collective-permute-start.13 = (bf16[1024,512]{1,0:T(8,128)(2,1)S(1)}, bf16[1024,512]{1,0:T(8,128)(2,1)S(1)}, u32[]{:S(2)}, u32[]{:S(2)}) collective-permute-start(bf16[1024,512]{1,0:T(8,128)(2,1)S(1)} %pad_maximum_fusion.4), channel_id=1, source_target_pairs={{0,1},{1,0},{2,3},{3,2},{4,5},{5,4},{6,7},{7,6},{8,9},{9,8},{10,11... | collective-permute-start | bytes 3145736 | tf_op jit(solution)/shard_map/ppermute | solution.py:40
  72.3 22.8 %collective-permute-start.5 = (bf16[384,512]{1,0:T(8,128)(2,1)S(1)}, bf16[384,512]{1,0:T(8,128)(2,1)S(1)}, u32[]{:S(2)}, u32[]{:S(2)}) collective-permute-start(bf16[384,512]{1,0:T(8,128)(2,1)S(1)} %add_convert_fusion.4), channel_id=1, source_target_pairs={{0,12},{1,13},{2,14},{3,15},{4,8},{5,9},{6,10},{7,11},{8,4},{9,5},... | collective-permute-start | bytes 1179656 | tf_op jit(solution)/shard_map/ppermute | solution.py:40
  76.1 28.7 %collective-permute-start.11 = (bf16[384,512]{1,0:T(8,128)(2,1)S(1)}, bf16[384,512]{1,0:T(8,128)(2,1)S(1)}, u32[]{:S(2)}, u32[]{:S(2)}) collective-permute-start(bf16[384,512]{1,0:T(8,128)(2,1)S(1)} %add_convert_fusion.3), channel_id=1, source_target_pairs={{0,12},{1,13},{2,14},{3,15},{4,8},{5,9},{6,10},{7,11},{8,4},{9,5},... | collective-permute-start | bytes 1179656 | tf_op jit(solution)/shard_map/ppermute | solution.py:40
  95.1 16.0 %collective-permute-start.14 = (bf16[384,512]{1,0:T(8,128)(2,1)S(1)}, bf16[384,512]{1,0:T(8,128)(2,1)S(1)}, u32[]{:S(2)}, u32[]{:S(2)}) collective-permute-start(bf16[384,512]{1,0:T(8,128)(2,1)S(1)} %get-tuple-element.40), channel_id=1, source_target_pairs={{0,1},{1,0},{2,3},{3,2},{4,5},{5,4},{6,7},{7,6},{8,9},{9,8},{10,11... | collective-permute-start | bytes 1179656 | tf_op jit(solution)/shard_map/ppermute | solution.py:40
  97.6 16.7 %collective-permute-start.15 = (bf16[1024,256]{1,0:T(8,128)(2,1)S(1)}, bf16[1024,256]{1,0:T(8,128)(2,1)S(1)}, u32[]{:S(2)}, u32[]{:S(2)}) collective-permute-start(bf16[1024,256]{1,0:T(8,128)(2,1)S(1)} %convolution_convert_fusion.1), channel_id=1, source_target_pairs={{0,3},{1,2},{2,1},{3,0},{4,7},{5,6},{6,5},{7,4},{8,11},{9,10},{10,... | collective-permute-start | bytes 1572872 | tf_op jit(solution)/shard_map/ppermute | solution.py:40
  104.9 14.8 %collective-permute-start.16 = (bf16[384,512]{1,0:T(8,128)(2,1)S(1)}, bf16[384,512]{1,0:T(8,128)(2,1)S(1)}, u32[]{:S(2)}, u32[]{:S(2)}) collective-permute-start(bf16[384,512]{1,0:T(8,128)(2,1)S(1)} %get-tuple-element.38), channel_id=1, source_target_pairs={{0,3},{1,2},{2,1},{3,0},{4,7},{5,6},{6,5},{7,4},{8,11},{9,10},{10,... | collective-permute-start | bytes 1179656 | tf_op jit(solution)/shard_map/ppermute | solution.py:40
  109.1 12.2 %collective-permute-start.17 = (bf16[256,1024]{1,0:T(8,128)(2,1)S(1)}, bf16[256,1024]{1,0:T(8,128)(2,1)S(1)}, u32[]{:S(2)}, u32[]{:S(2)}) collective-permute-start(bf16[256,1024]{1,0:T(8,128)(2,1)S(1)} %convolution_convert_fusion), channel_id=1, source_target_pairs={{0,1},{1,0},{2,3},{3,2},{4,5},{5,4},{6,7},{7,6},{8,9},{9,8},{10,11... | collective-permute-start | bytes 1572872 | tf_op jit(solution)/shard_map/ppermute | solution.py:40

commit v5 on v4

--- a/solution.py
+++ b/solution.py
@@ -64,9 +64,9 @@
         return bf(f32(kept) + f32(came))
 
     def shift(half, step):
+        two = send(half, lambda s, t, r: (s + step, t, r))
         one = send(half, tp_pair(1, step))
-        two = send(half, lambda s, t, r: (s + step, t, r))
-        return one, two
+        return two, one
 
     def other_half(half):
         return send(half, tp_pair(1))
@@ -102,10 +102,11 @@
     d_own = dot(hs, back[:, :256], ((0,), (0,)))
     code_rest, d_out, wus_far, wds_far = barrier((code_rest, d_out, wus_far, wds_far))
     code_own, code_other = in_order(code_half, code_rest)
-    code_far = send(code_other, rep_pair(1))
     code = jnp.concatenate([code_own, code_other], 0)
     u_out = bf(dot(code[:, 256:], cs, ((0,), (0,))))
     u_in = send(u_out, rep_pair(0))
+    u_out, code_other = barrier((u_out, code_other))
+    code_far = send(code_other, rep_pair(1))
     code_own, code, u_out, back_far = barrier((code_own, code, u_out, back_far))
     r_own = dot(code_own, wus, ((1,), (0,)))
     u_own = dot(code[:, :256], cs, ((0,), (0,)))

time: 123 us -> 120 us (0.976)
  the two profiles are of different devices: /device:TPU:16 before, /device:TPU:1 now
where the time goes in v5:
time: 120 us; the launch traced here: 119 us
  starting transfers between devices  74.3 us (62%)
  waiting for transfers between devices  30.6 us (26%)
  matrix products  11.1 us (9%)
  other arithmetic  1.71 us (1%)
    ppermute x18, starting transfers between devices, send(): return lax.ppermute(x, AXES, route(sections, target))  74.3 us
    ppermute x18, waiting for transfers between devices, send(): return lax.ppermute(x, AXES, route(sections, target))  30.6 us
    dot_general x12, matrix products, dot(): lax.dot_general(left, right, (dims, ((), ())), preferred_element_type=jnp...  11.1 us
  transfers between devices with their start and end apart: 18, of which 5 were waited for; matrix products, arithmetic and copies ran while one was open for 10% of the time, Pallas kernels for 0%

profile of v5, /device:TPU:1, one launch (start us, length us, event | category | flops | bytes accessed | tf_op | source)
XLA Modules:
  0.0 118.8 jit_solution(9519498253707259758)
XLA Ops:
  0.6 4.0 %collective-permute-start = (bf16[384,1024]{1,0:T(8,128)(2,1)}, bf16[384,1024]{1,0:T(8,128)(2,1)S(1)}, u32[]{:S(2)}, u32[]{:S(2)}) collective-permute-start(bf16[384,1024]{1,0:T(8,128)(2,1)} %bitcast.37), channel_id=1, source_target_pairs={{0,3},{1,2},{2,1},{3,0},{4,7},{5,6},{6,5},{7,4},{8,11},{9,10},{10,... | collective-permute-start | bytes 2359304 | tf_op jit(solution)/shard_map/ppermute | solution.py:40
  4.6 3.7 %collective-permute-start.1 = (bf16[256,1024]{1,0:T(8,128)(2,1)}, bf16[256,1024]{1,0:T(8,128)(2,1)S(1)}, u32[]{:S(2)}, u32[]{:S(2)}) collective-permute-start(bf16[256,1024]{1,0:T(8,128)(2,1)} %bitcast.47), channel_id=1, source_target_pairs={{0,1},{1,0},{2,3},{3,2},{4,5},{5,4},{6,7},{7,6},{8,9},{9,8},{10,11... | collective-permute-start | bytes 1572872 | tf_op jit(solution)/shard_map/ppermute | solution.py:40
  8.3 2.8 %collective-permute-start.6 = (bf16[384,1024]{1,0:T(8,128)(2,1)}, bf16[384,1024]{1,0:T(8,128)(2,1)S(1)}, u32[]{:S(2)}, u32[]{:S(2)}) collective-permute-start(bf16[384,1024]{1,0:T(8,128)(2,1)} %bitcast.39), channel_id=1, source_target_pairs={{0,1},{1,0},{2,3},{3,2},{4,5},{5,4},{6,7},{7,6},{8,9},{9,8},{10,11... | collective-permute-start | bytes 2359304 | tf_op jit(solution)/shard_map/ppermute | solution.py:40
  11.1 1.9 %collective-permute-start.7 = (bf16[1024,256]{1,0:T(8,128)(2,1)}, bf16[1024,256]{1,0:T(8,128)(2,1)S(1)}, u32[]{:S(2)}, u32[]{:S(2)}) collective-permute-start(bf16[1024,256]{1,0:T(8,128)(2,1)} %bitcast.43), channel_id=1, source_target_pairs={{0,3},{1,2},{2,1},{3,0},{4,7},{5,6},{6,5},{7,4},{8,11},{9,10},{10,... | collective-permute-start | bytes 1572872 | tf_op jit(solution)/shard_map/ppermute | solution.py:40
  13.1 5.9 %collective-permute-done.1 = bf16[256,1024]{1,0:T(8,128)(2,1)S(1)} collective-permute-done((bf16[256,1024]{1,0:T(8,128)(2,1)}, bf16[256,1024]{1,0:T(8,128)(2,1)S(1)}, u32[]{:S(2)}, u32[]{:S(2)}) %collective-permute-start.1) | collective-permute-done | bytes 524320 | tf_op jit(solution)/shard_map/ppermute | solution.py:40
  19.0 1.9 %convolution_convert_fusion.4 = bf16[384,512]{1,0:T(8,128)(2,1)S(1)} fusion(bf16[384,1024]{1,0:T(8,128)(2,1)S(1)} %collective-permute-done, pred[]{:T(512)S(6)} %eq.28, bf16[256,1024]{1,0:T(8,128)(2,1)S(1)} %collective-permute-done.1, bf16[256,1024]{1,0:T(8,128)(2,1)} %bitcast.48, bf16[1,384,1024]{2,1,0:T(8,128)(2,1)} %param.5), kind=kOutput, calls=%fused_computation.13 | convolution fusion | flops 405340160 | bytes 3014657 | tf_op jit(solution)/shard_map/dot_general | solution.py:22
  20.9 8.9 %collective-permute-start.2 = (bf16[384,512]{1,0:T(8,128)(2,1)S(1)}, bf16[384,512]{1,0:T(8,128)(2,1)S(1)}, u32[]{:S(2)}, u32[]{:S(2)}) collective-permute-start(bf16[384,512]{1,0:T(8,128)(2,1)S(1)} %convolution_convert_fusion.4), channel_id=1, source_target_pairs={{0,4},{1,5},{2,6},{3,7},{4,0},{5,1},{6,2},{7,3},{8,12},{9,13},{10,... | collective-permute-start | bytes 1179656 | tf_op jit(solution)/shard_map/ppermute | solution.py:40
  29.9 6.0 %collective-permute-done.6 = bf16[384,1024]{1,0:T(8,128)(2,1)S(1)} collective-permute-done((bf16[384,1024]{1,0:T(8,128)(2,1)}, bf16[384,1024]{1,0:T(8,128)(2,1)S(1)}, u32[]{:S(2)}, u32[]{:S(2)}) %collective-permute-start.6) | collective-permute-done | bytes 786464 | tf_op jit(solution)/shard_map/ppermute | solution.py:40
  36.5 6.7 %collective-permute-start.8 = (bf16[384,512]{1,0:T(8,128)(2,1)S(1)}, bf16[384,512]{1,0:T(8,128)(2,1)S(1)}, u32[]{:S(2)}, u32[]{:S(2)}) collective-permute-start(bf16[384,512]{1,0:T(8,128)(2,1)S(1)} %convolution_convert_fusion.2), channel_id=1, source_target_pairs={{0,4},{1,5},{2,6},{3,7},{4,0},{5,1},{6,2},{7,3},{8,12},{9,13},{10,... | collective-permute-start | bytes 1179656 | tf_op jit(solution)/shard_map/ppermute | solution.py:40
  44.0 4.9 %collective-permute-start.4 = (bf16[384,512]{1,0:T(8,128)(2,1)S(1)}, bf16[384,512]{1,0:T(8,128)(2,1)S(1)}, u32[]{:S(2)}, u32[]{:S(2)}) collective-permute-start(bf16[384,512]{1,0:T(8,128)(2,1)S(1)} %fusion.6), channel_id=1, source_target_pairs={{0,508},{1,509},{2,510},{3,511},{4,504},{5,505},{6,506},{7,507},{8... | collective-permute-start | bytes 1179656 | tf_op jit(solution)/shard_map/ppermute | solution.py:40
  48.9 7.5 %collective-permute-start.3 = (bf16[384,512]{1,0:T(8,128)(2,1)S(1)}, bf16[384,512]{1,0:T(8,128)(2,1)S(1)}, u32[]{:S(2)}, u32[]{:S(2)}) collective-permute-start(bf16[384,512]{1,0:T(8,128)(2,1)S(1)} %fusion.6), channel_id=1, source_target_pairs={{0,496},{1,497},{2,498},{3,499},{4,500},{5,501},{6,502},{7,503},{8... | collective-permute-start | bytes 1179656 | tf_op jit(solution)/shard_map/ppermute | solution.py:40
  57.0 7.8 %collective-permute-start.10 = (bf16[384,512]{1,0:T(8,128)(2,1)S(1)}, bf16[384,512]{1,0:T(8,128)(2,1)S(1)}, u32[]{:S(2)}, u32[]{:S(2)}) collective-permute-start(bf16[384,512]{1,0:T(8,128)(2,1)S(1)} %fusion.3), channel_id=1, source_target_pairs={{0,28},{1,29},{2,30},{3,31},{4,24},{5,25},{6,26},{7,27},{8,20},{9,... | collective-permute-start | bytes 1179656 | tf_op jit(solution)/shard_map/ppermute | solution.py:40
  64.8 1.9 %collective-permute-start.9 = (bf16[384,512]{1,0:T(8,128)(2,1)S(1)}, bf16[384,512]{1,0:T(8,128)(2,1)S(1)}, u32[]{:S(2)}, u32[]{:S(2)}) collective-permute-start(bf16[384,512]{1,0:T(8,128)(2,1)S(1)} %fusion.3), channel_id=1, source_target_pairs={{0,16},{1,17},{2,18},{3,19},{4,20},{5,21},{6,22},{7,23},{8,24},{9,... | collective-permute-start | bytes 1179656 | tf_op jit(solution)/shard_map/ppermute | solution.py:40
  66.9 1.9 %collective-permute-start.12 = (bf16[512,1024]{1,0:T(8,128)(2,1)S(1)}, bf16[512,1024]{1,0:T(8,128)(2,1)S(1)}, u32[]{:S(2)}, u32[]{:S(2)}) collective-permute-start(bf16[512,1024]{1,0:T(8,128)(2,1)S(1)} %pad_maximum_fusion.5), channel_id=1, source_target_pairs={{0,3},{1,2},{2,1},{3,0},{4,7},{5,6},{6,5},{7,4},{8,11},{9,10},{10,... | collective-permute-start | bytes 3145736 | tf_op jit(solution)/shard_map/ppermute | solution.py:40
  68.8 3.7 %collective-permute-start.13 = (bf16[1024,512]{1,0:T(8,128)(2,1)S(1)}, bf16[1024,512]{1,0:T(8,128)(2,1)S(1)}, u32[]{:S(2)}, u32[]{:S(2)}) collective-permute-start(bf16[1024,512]{1,0:T(8,128)(2,1)S(1)} %pad_maximum_fusion.4), channel_id=1, source_target_pairs={{0,1},{1,0},{2,3},{3,2},{4,5},{5,4},{6,7},{7,6},{8,9},{9,8},{10,11... | collective-permute-start | bytes 3145736 | tf_op jit(solution)/shard_map/ppermute | solution.py:40
  72.6 2.2 %collective-permute-start.5 = (bf16[384,512]{1,0:T(8,128)(2,1)S(1)}, bf16[384,512]{1,0:T(8,128)(2,1)S(1)}, u32[]{:S(2)}, u32[]{:S(2)}) collective-permute-start(bf16[384,512]{1,0:T(8,128)(2,1)S(1)} %add_convert_fusion.4), channel_id=1, source_target_pairs={{0,12},{1,13},{2,14},{3,15},{4,8},{5,9},{6,10},{7,11},{8,4},{9,5},... | collective-permute-start | bytes 1179656 | tf_op jit(solution)/shard_map/ppermute | solution.py:40
  74.9 11.2 %collective-permute-done.10 = bf16[384,512]{1,0:T(8,128)(2,1)S(1)} collective-permute-done((bf16[384,512]{1,0:T(8,128)(2,1)S(1)}, bf16[384,512]{1,0:T(8,128)(2,1)S(1)}, u32[]{:S(2)}, u32[]{:S(2)}) %collective-permute-start.10) | collective-permute-done | bytes 393248 | tf_op jit(solution)/shard_map/ppermute | solution.py:40
  86.3 1.9 %collective-permute-start.11 = (bf16[384,512]{1,0:T(8,128)(2,1)S(1)}, bf16[384,512]{1,0:T(8,128)(2,1)S(1)}, u32[]{:S(2)}, u32[]{:S(2)}) collective-permute-start(bf16[384,512]{1,0:T(8,128)(2,1)S(1)} %add_convert_fusion.3), channel_id=1, source_target_pairs={{0,12},{1,13},{2,14},{3,15},{4,8},{5,9},{6,10},{7,11},{8,4},{9,5},... | collective-permute-start | bytes 1179656 | tf_op jit(solution)/shard_map/ppermute | solution.py:40
  88.3 5.5 %collective-permute-start.14 = (bf16[384,512]{1,0:T(8,128)(2,1)S(1)}, bf16[384,512]{1,0:T(8,128)(2,1)S(1)}, u32[]{:S(2)}, u32[]{:S(2)}) collective-permute-start(bf16[384,512]{1,0:T(8,128)(2,1)S(1)} %get-tuple-element.42), channel_id=1, source_target_pairs={{0,1},{1,0},{2,3},{3,2},{4,5},{5,4},{6,7},{7,6},{8,9},{9,8},{10,11... | collective-permute-start | bytes 1179656 | tf_op jit(solution)/shard_map/ppermute | solution.py:40
  94.4 1.9 %collective-permute-start.15 = (bf16[1024,256]{1,0:T(8,128)(2,1)S(1)}, bf16[1024,256]{1,0:T(8,128)(2,1)S(1)}, u32[]{:S(2)}, u32[]{:S(2)}) collective-permute-start(bf16[1024,256]{1,0:T(8,128)(2,1)S(1)} %convolution_convert_fusion.1), channel_id=1, source_target_pairs={{0,3},{1,2},{2,1},{3,0},{4,7},{5,6},{6,5},{7,4},{8,11},{9,10},{10,... | collective-permute-start | bytes 1572872 | tf_op jit(solution)/shard_map/ppermute | solution.py:40
  98.1 5.2 %collective-permute-start.17 = (bf16[256,1024]{1,0:T(8,128)(2,1)S(1)}, bf16[256,1024]{1,0:T(8,128)(2,1)S(1)}, u32[]{:S(2)}, u32[]{:S(2)}) collective-permute-start(bf16[256,1024]{1,0:T(8,128)(2,1)S(1)} %convolution_convert_fusion), channel_id=1, source_target_pairs={{0,1},{1,0},{2,3},{3,2},{4,5},{5,4},{6,7},{7,6},{8,9},{9,8},{10,11... | collective-permute-start | bytes 1572872 | tf_op jit(solution)/shard_map/ppermute | solution.py:40
  103.3 1.9 %collective-permute-start.16 = (bf16[384,512]{1,0:T(8,128)(2,1)S(1)}, bf16[384,512]{1,0:T(8,128)(2,1)S(1)}, u32[]{:S(2)}, u32[]{:S(2)}) collective-permute-start(bf16[384,512]{1,0:T(8,128)(2,1)S(1)} %get-tuple-element.33), channel_id=1, source_target_pairs={{0,3},{1,2},{2,1},{3,0},{4,7},{5,6},{6,5},{7,4},{8,11},{9,10},{10,... | collective-permute-start | bytes 1179656 | tf_op jit(solution)/shard_map/ppermute | solution.py:40
  105.9 1.5 %add_convert_fusion.1 = bf16[384,1024]{1,0:T(8,128)(2,1)} fusion(f32[384,1024]{1,0:T(8,128)S(1)} %fusion.34, bf16[384,512]{1,0:T(8,128)(2,1)S(1)} %get-tuple-element.43, bf16[1024,512]{1,0:T(8,128)(2,1)S(1)} %pad_maximum_fusion.4), kind=kOutput, calls=%fused_computation.3 | convolution fusion | flops 403439616 | bytes 3801088 | tf_op jit(solution)/shard_map/dot_general | solution.py:22
  110.1 6.3 %collective-permute-done.16 = bf16[384,512]{1,0:T(8,128)(2,1)S(1)} collective-permute-done((bf16[384,512]{1,0:T(8,128)(2,1)S(1)}, bf16[384,512]{1,0:T(8,128)(2,1)S(1)}, u32[]{:S(2)}, u32[]{:S(2)}) %collective-permute-start.16) | collective-permute-done | bytes 393248 | tf_op jit(solution)/shard_map/ppermute | solution.py:40
  (42 shorter events, 10.5 us)
Async XLA Ops:
  0.6 18.4 %collective-permute-start = (bf16[384,1024]{1,0:T(8,128)(2,1)}, bf16[384,1024]{1,0:T(8,128)(2,1)S(1)}, u32[]{:S(2)}, u32[]{:S(2)}) collective-permute-start(bf16[384,1024]{1,0:T(8,128)(2,1)} %bitcast.37), channel_id=1, source_target_pairs={{0,3},{1,2},{2,1},{3,0},{4,7},{5,6},{6,5},{7,4},{8,11},{9,10},{10,... | collective-permute-start | bytes 2359304 | tf_op jit(solution)/shard_map/ppermute | solution.py:40
  4.6 14.4 %collective-permute-start.1 = (bf16[256,1024]{1,0:T(8,128)(2,1)}, bf16[256,1024]{1,0:T(8,128)(2,1)S(1)}, u32[]{:S(2)}, u32[]{:S(2)}) collective-permute-start(bf16[256,1024]{1,0:T(8,128)(2,1)} %bitcast.47), channel_id=1, source_target_pairs={{0,1},{1,0},{2,3},{3,2},{4,5},{5,4},{6,7},{7,6},{8,9},{9,8},{10,11... | collective-permute-start | bytes 1572872 | tf_op jit(solution)/shard_map/ppermute | solution.py:40
  8.3 27.6 %collective-permute-start.6 = (bf16[384,1024]{1,0:T(8,128)(2,1)}, bf16[384,1024]{1,0:T(8,128)(2,1)S(1)}, u32[]{:S(2)}, u32[]{:S(2)}) collective-permute-start(bf16[384,1024]{1,0:T(8,128)(2,1)} %bitcast.39), channel_id=1, source_target_pairs={{0,1},{1,0},{2,3},{3,2},{4,5},{5,4},{6,7},{7,6},{8,9},{9,8},{10,11... | collective-permute-start | bytes 2359304 | tf_op jit(solution)/shard_map/ppermute | solution.py:40
  11.1 18.8 %collective-permute-start.7 = (bf16[1024,256]{1,0:T(8,128)(2,1)}, bf16[1024,256]{1,0:T(8,128)(2,1)S(1)}, u32[]{:S(2)}, u32[]{:S(2)}) collective-permute-start(bf16[1024,256]{1,0:T(8,128)(2,1)} %bitcast.43), channel_id=1, source_target_pairs={{0,3},{1,2},{2,1},{3,0},{4,7},{5,6},{6,5},{7,4},{8,11},{9,10},{10,... | collective-permute-start | bytes 1572872 | tf_op jit(solution)/shard_map/ppermute | solution.py:40
  13.1 22.8 %copy-start.1 = (bf16[1,384,1024]{2,1,0:T(8,128)(2,1)S(1)}, bf16[1,384,1024]{2,1,0:T(8,128)(2,1)}, u32[]{:S(2)}) copy-start(bf16[1,384,1024]{2,1,0:T(8,128)(2,1)} %param.4) | copy-start | bytes 2359300
  13.1 22.8 %copy-start.2 = (bf16[1,1024,256]{2,1,0:T(8,128)(2,1)S(1)}, bf16[1,1024,256]{2,1,0:T(8,128)(2,1)}, u32[]{:S(2)}) copy-start(bf16[1,1024,256]{2,1,0:T(8,128)(2,1)} %param.6) | copy-start | bytes 1572868
  20.9 22.3 %copy-start = (bf16[1,384,1024]{2,1,0:T(8,128)(2,1)S(1)}, bf16[1,384,1024]{2,1,0:T(8,128)(2,1)}, u32[]{:S(2)}) copy-start(bf16[1,384,1024]{2,1,0:T(8,128)(2,1)} %param.5) | copy-start | bytes 2359300
  20.9 22.4 %collective-permute-start.2 = (bf16[384,512]{1,0:T(8,128)(2,1)S(1)}, bf16[384,512]{1,0:T(8,128)(2,1)S(1)}, u32[]{:S(2)}, u32[]{:S(2)}) collective-permute-start(bf16[384,512]{1,0:T(8,128)(2,1)S(1)} %convolution_convert_fusion.4), channel_id=1, source_target_pairs={{0,4},{1,5},{2,6},{3,7},{4,0},{5,1},{6,2},{7,3},{8,12},{9,13},{10,... | collective-permute-start | bytes 1179656 | tf_op jit(solution)/shard_map/ppermute | solution.py:40
  36.5 6.9 %copy-start.3 = (bf16[1,256,1024]{2,1,0:T(8,128)(2,1)S(1)}, bf16[1,256,1024]{2,1,0:T(8,128)(2,1)}, u32[]{:S(2)}) copy-start(bf16[1,256,1024]{2,1,0:T(8,128)(2,1)} %param.7) | copy-start | bytes 1572868
  36.5 19.9 %collective-permute-start.8 = (bf16[384,512]{1,0:T(8,128)(2,1)S(1)}, bf16[384,512]{1,0:T(8,128)(2,1)S(1)}, u32[]{:S(2)}, u32[]{:S(2)}) collective-permute-start(bf16[384,512]{1,0:T(8,128)(2,1)S(1)} %convolution_convert_fusion.2), channel_id=1, source_target_pairs={{0,4},{1,5},{2,6},{3,7},{4,0},{5,1},{6,2},{7,3},{8,12},{9,13},{10,... | collective-permute-start | bytes 1179656 | tf_op jit(solution)/shard_map/ppermute | solution.py:40
  44.0 24.9 %collective-permute-start.4 = (bf16[384,512]{1,0:T(8,128)(2,1)S(1)}, bf16[384,512]{1,0:T(8,128)(2,1)S(1)}, u32[]{:S(2)}, u32[]{:S(2)}) collective-permute-start(bf16[384,512]{1,0:T(8,128)(2,1)S(1)} %fusion.6), channel_id=1, source_target_pairs={{0,508},{1,509},{2,510},{3,511},{4,504},{5,505},{6,506},{7,507},{8... | collective-permute-start | bytes 1179656 | tf_op jit(solution)/shard_map/ppermute | solution.py:40
  48.9 23.6 %collective-permute-start.3 = (bf16[384,512]{1,0:T(8,128)(2,1)S(1)}, bf16[384,512]{1,0:T(8,128)(2,1)S(1)}, u32[]{:S(2)}, u32[]{:S(2)}) collective-permute-start(bf16[384,512]{1,0:T(8,128)(2,1)S(1)} %fusion.6), channel_id=1, source_target_pairs={{0,496},{1,497},{2,498},{3,499},{4,500},{5,501},{6,502},{7,503},{8... | collective-permute-start | bytes 1179656 | tf_op jit(solution)/shard_map/ppermute | solution.py:40
  57.0 29.2 %collective-permute-start.10 = (bf16[384,512]{1,0:T(8,128)(2,1)S(1)}, bf16[384,512]{1,0:T(8,128)(2,1)S(1)}, u32[]{:S(2)}, u32[]{:S(2)}) collective-permute-start(bf16[384,512]{1,0:T(8,128)(2,1)S(1)} %fusion.3), channel_id=1, source_target_pairs={{0,28},{1,29},{2,30},{3,31},{4,24},{5,25},{6,26},{7,27},{8,20},{9,... | collective-permute-start | bytes 1179656 | tf_op jit(solution)/shard_map/ppermute | solution.py:40
  64.8 21.4 %collective-permute-start.9 = (bf16[384,512]{1,0:T(8,128)(2,1)S(1)}, bf16[384,512]{1,0:T(8,128)(2,1)S(1)}, u32[]{:S(2)}, u32[]{:S(2)}) collective-permute-start(bf16[384,512]{1,0:T(8,128)(2,1)S(1)} %fusion.3), channel_id=1, source_target_pairs={{0,16},{1,17},{2,18},{3,19},{4,20},{5,21},{6,22},{7,23},{8,24},{9,... | collective-permute-start | bytes 1179656 | tf_op jit(solution)/shard_map/ppermute | solution.py:40
  66.9 30.5 %collective-permute-start.12 = (bf16[512,1024]{1,0:T(8,128)(2,1)S(1)}, bf16[512,1024]{1,0:T(8,128)(2,1)S(1)}, u32[]{:S(2)}, u32[]{:S(2)}) collective-permute-start(bf16[512,1024]{1,0:T(8,128)(2,1)S(1)} %pad_maximum_fusion.5), channel_id=1, source_target_pairs={{0,3},{1,2},{2,1},{3,0},{4,7},{5,6},{6,5},{7,4},{8,11},{9,10},{10,... | collective-permute-start | bytes 3145736 | tf_op jit(solution)/shard_map/ppermute | solution.py:40
  68.8 28.6 %collective-permute-start.13 = (bf16[1024,512]{1,0:T(8,128)(2,1)S(1)}, bf16[1024,512]{1,0:T(8,128)(2,1)S(1)}, u32[]{:S(2)}, u32[]{:S(2)}) collective-permute-start(bf16[1024,512]{1,0:T(8,128)(2,1)S(1)} %pad_maximum_fusion.4), channel_id=1, source_target_pairs={{0,1},{1,0},{2,3},{3,2},{4,5},{5,4},{6,7},{7,6},{8,9},{9,8},{10,11... | collective-permute-start | bytes 3145736 | tf_op jit(solution)/shard_map/ppermute | solution.py:40
  72.6 15.6 %collective-permute-start.5 = (bf16[384,512]{1,0:T(8,128)(2,1)S(1)}, bf16[384,512]{1,0:T(8,128)(2,1)S(1)}, u32[]{:S(2)}, u32[]{:S(2)}) collective-permute-start(bf16[384,512]{1,0:T(8,128)(2,1)S(1)} %add_convert_fusion.4), channel_id=1, source_target_pairs={{0,12},{1,13},{2,14},{3,15},{4,8},{5,9},{6,10},{7,11},{8,4},{9,5},... | collective-permute-start | bytes 1179656 | tf_op jit(solution)/shard_map/ppermute | solution.py:40
  86.3 11.1 %collective-permute-start.11 = (bf16[384,512]{1,0:T(8,128)(2,1)S(1)}, bf16[384,512]{1,0:T(8,128)(2,1)S(1)}, u32[]{:S(2)}, u32[]{:S(2)}) collective-permute-start(bf16[384,512]{1,0:T(8,128)(2,1)S(1)} %add_convert_fusion.3), channel_id=1, source_target_pairs={{0,12},{1,13},{2,14},{3,15},{4,8},{5,9},{6,10},{7,11},{8,4},{9,5},... | collective-permute-start | bytes 1179656 | tf_op jit(solution)/shard_map/ppermute | solution.py:40
  88.3 17.0 %collective-permute-start.14 = (bf16[384,512]{1,0:T(8,128)(2,1)S(1)}, bf16[384,512]{1,0:T(8,128)(2,1)S(1)}, u32[]{:S(2)}, u32[]{:S(2)}) collective-permute-start(bf16[384,512]{1,0:T(8,128)(2,1)S(1)} %get-tuple-element.42), channel_id=1, source_target_pairs={{0,1},{1,0},{2,3},{3,2},{4,5},{5,4},{6,7},{7,6},{8,9},{9,8},{10,11... | collective-permute-start | bytes 1179656 | tf_op jit(solution)/shard_map/ppermute | solution.py:40
  94.4 14.2 %collective-permute-start.15 = (bf16[1024,256]{1,0:T(8,128)(2,1)S(1)}, bf16[1024,256]{1,0:T(8,128)(2,1)S(1)}, u32[]{:S(2)}, u32[]{:S(2)}) collective-permute-start(bf16[1024,256]{1,0:T(8,128)(2,1)S(1)} %convolution_convert_fusion.1), channel_id=1, source_target_pairs={{0,3},{1,2},{2,1},{3,0},{4,7},{5,6},{6,5},{7,4},{8,11},{9,10},{10,... | collective-permute-start | bytes 1572872 | tf_op jit(solution)/shard_map/ppermute | solution.py:40
  98.1 19.8 %collective-permute-start.17 = (bf16[256,1024]{1,0:T(8,128)(2,1)S(1)}, bf16[256,1024]{1,0:T(8,128)(2,1)S(1)}, u32[]{:S(2)}, u32[]{:S(2)}) collective-permute-start(bf16[256,1024]{1,0:T(8,128)(2,1)S(1)} %convolution_convert_fusion), channel_id=1, source_target_pairs={{0,1},{1,0},{2,3},{3,2},{4,5},{5,4},{6,7},{7,6},{8,9},{9,8},{10,11... | collective-permute-start | bytes 1572872 | tf_op jit(solution)/shard_map/ppermute | solution.py:40
  103.3 13.1 %collective-permute-start.16 = (bf16[384,512]{1,0:T(8,128)(2,1)S(1)}, bf16[384,512]{1,0:T(8,128)(2,1)S(1)}, u32[]{:S(2)}, u32[]{:S(2)}) collective-permute-start(bf16[384,512]{1,0:T(8,128)(2,1)S(1)} %get-tuple-element.33), channel_id=1, source_target_pairs={{0,3},{1,2},{2,1},{3,0},{4,7},{5,6},{6,5},{7,4},{8,11},{9,10},{10,... | collective-permute-start | bytes 1179656 | tf_op jit(solution)/shard_map/ppermute | solution.py:40

commit v6 on v5

--- a/solution.py
+++ b/solution.py
@@ -95,9 +95,10 @@
     back_own, back_other = in_order(back_half, other_half(back_half))
     code_rest = other_half(code_half)
     back = jnp.concatenate([back_own, back_other], 0)
-    back_far = send(back_other, rep_pair(0))
     d_out = bf(dot(hs, back[:, 256:], ((0,), (0,))))
     d_in = send(d_out, rep_pair(1))
+    d_out, back_other = barrier((d_out, back_other))
+    back_far = send(back_other, rep_pair(0))
     g_own = dot(back_own, wds, ((1,), (1,)))
     d_own = dot(hs, back[:, :256], ((0,), (0,)))
     code_rest, d_out, wus_far, wds_far = barrier((code_rest, d_out, wus_far, wds_far))

time: 120 us -> 119 us (level)
  no operation moved by 1% of the time
where the time goes in v6:
time: 119 us
  starting transfers between devices  74.3 us (62%)
  waiting for transfers between devices  30.6 us (26%)
  matrix products  11.1 us (9%)
  other arithmetic  1.71 us (1%)
    ppermute x18, starting transfers between devices, send(): return lax.ppermute(x, AXES, route(sections, target))  74.3 us
    ppermute x18, waiting for transfers between devices, send(): return lax.ppermute(x, AXES, route(sections, target))  30.6 us
    dot_general x12, matrix products, dot(): lax.dot_general(left, right, (dims, ((), ())), preferred_element_type=jnp...  11.1 us
  transfers between devices with their start and end apart: 18, of which 5 were waited for; matrix products, arithmetic and copies ran while one was open for 10% of the time, Pallas kernels for 0%

profile of v6, /device:TPU:1, one launch (start us, length us, event | category | flops | bytes accessed | tf_op | source)
XLA Modules:
  0.0 118.8 jit_solution(13027947202277517489)
XLA Ops:
  0.6 4.0 %collective-permute-start = (bf16[384,1024]{1,0:T(8,128)(2,1)}, bf16[384,1024]{1,0:T(8,128)(2,1)S(1)}, u32[]{:S(2)}, u32[]{:S(2)}) collective-permute-start(bf16[384,1024]{1,0:T(8,128)(2,1)} %bitcast.37), channel_id=1, source_target_pairs={{0,3},{1,2},{2,1},{3,0},{4,7},{5,6},{6,5},{7,4},{8,11},{9,10},{10,... | collective-permute-start | bytes 2359304 | tf_op jit(solution)/shard_map/ppermute | solution.py:40
  4.6 3.7 %collective-permute-start.1 = (bf16[256,1024]{1,0:T(8,128)(2,1)}, bf16[256,1024]{1,0:T(8,128)(2,1)S(1)}, u32[]{:S(2)}, u32[]{:S(2)}) collective-permute-start(bf16[256,1024]{1,0:T(8,128)(2,1)} %bitcast.47), channel_id=1, source_target_pairs={{0,1},{1,0},{2,3},{3,2},{4,5},{5,4},{6,7},{7,6},{8,9},{9,8},{10,11... | collective-permute-start | bytes 1572872 | tf_op jit(solution)/shard_map/ppermute | solution.py:40
  8.3 2.8 %collective-permute-start.6 = (bf16[384,1024]{1,0:T(8,128)(2,1)}, bf16[384,1024]{1,0:T(8,128)(2,1)S(1)}, u32[]{:S(2)}, u32[]{:S(2)}) collective-permute-start(bf16[384,1024]{1,0:T(8,128)(2,1)} %bitcast.39), channel_id=1, source_target_pairs={{0,1},{1,0},{2,3},{3,2},{4,5},{5,4},{6,7},{7,6},{8,9},{9,8},{10,11... | collective-permute-start | bytes 2359304 | tf_op jit(solution)/shard_map/ppermute | solution.py:40
  11.1 1.9 %collective-permute-start.7 = (bf16[1024,256]{1,0:T(8,128)(2,1)}, bf16[1024,256]{1,0:T(8,128)(2,1)S(1)}, u32[]{:S(2)}, u32[]{:S(2)}) collective-permute-start(bf16[1024,256]{1,0:T(8,128)(2,1)} %bitcast.43), channel_id=1, source_target_pairs={{0,3},{1,2},{2,1},{3,0},{4,7},{5,6},{6,5},{7,4},{8,11},{9,10},{10,... | collective-permute-start | bytes 1572872 | tf_op jit(solution)/shard_map/ppermute | solution.py:40
  13.1 5.9 %collective-permute-done.1 = bf16[256,1024]{1,0:T(8,128)(2,1)S(1)} collective-permute-done((bf16[256,1024]{1,0:T(8,128)(2,1)}, bf16[256,1024]{1,0:T(8,128)(2,1)S(1)}, u32[]{:S(2)}, u32[]{:S(2)}) %collective-permute-start.1) | collective-permute-done | bytes 524320 | tf_op jit(solution)/shard_map/ppermute | solution.py:40
  19.0 1.9 %convolution_convert_fusion.4 = bf16[384,512]{1,0:T(8,128)(2,1)S(1)} fusion(bf16[384,1024]{1,0:T(8,128)(2,1)S(1)} %collective-permute-done, pred[]{:T(512)S(6)} %eq.28, bf16[256,1024]{1,0:T(8,128)(2,1)S(1)} %collective-permute-done.1, bf16[256,1024]{1,0:T(8,128)(2,1)} %bitcast.48, bf16[1,384,1024]{2,1,0:T(8,128)(2,1)} %param.5), kind=kOutput, calls=%fused_computation.13 | convolution fusion | flops 405340160 | bytes 3014657 | tf_op jit(solution)/shard_map/dot_general | solution.py:22
  20.9 8.9 %collective-permute-start.2 = (bf16[384,512]{1,0:T(8,128)(2,1)S(1)}, bf16[384,512]{1,0:T(8,128)(2,1)S(1)}, u32[]{:S(2)}, u32[]{:S(2)}) collective-permute-start(bf16[384,512]{1,0:T(8,128)(2,1)S(1)} %convolution_convert_fusion.4), channel_id=1, source_target_pairs={{0,4},{1,5},{2,6},{3,7},{4,0},{5,1},{6,2},{7,3},{8,12},{9,13},{10,... | collective-permute-start | bytes 1179656 | tf_op jit(solution)/shard_map/ppermute | solution.py:40
  29.9 6.0 %collective-permute-done.6 = bf16[384,1024]{1,0:T(8,128)(2,1)S(1)} collective-permute-done((bf16[384,1024]{1,0:T(8,128)(2,1)}, bf16[384,1024]{1,0:T(8,128)(2,1)S(1)}, u32[]{:S(2)}, u32[]{:S(2)}) %collective-permute-start.6) | collective-permute-done | bytes 786464 | tf_op jit(solution)/shard_map/ppermute | solution.py:40
  36.5 6.7 %collective-permute-start.8 = (bf16[384,512]{1,0:T(8,128)(2,1)S(1)}, bf16[384,512]{1,0:T(8,128)(2,1)S(1)}, u32[]{:S(2)}, u32[]{:S(2)}) collective-permute-start(bf16[384,512]{1,0:T(8,128)(2,1)S(1)} %convolution_convert_fusion.2), channel_id=1, source_target_pairs={{0,4},{1,5},{2,6},{3,7},{4,0},{5,1},{6,2},{7,3},{8,12},{9,13},{10,... | collective-permute-start | bytes 1179656 | tf_op jit(solution)/shard_map/ppermute | solution.py:40
  44.0 4.9 %collective-permute-start.4 = (bf16[384,512]{1,0:T(8,128)(2,1)S(1)}, bf16[384,512]{1,0:T(8,128)(2,1)S(1)}, u32[]{:S(2)}, u32[]{:S(2)}) collective-permute-start(bf16[384,512]{1,0:T(8,128)(2,1)S(1)} %fusion.6), channel_id=1, source_target_pairs={{0,508},{1,509},{2,510},{3,511},{4,504},{5,505},{6,506},{7,507},{8... | collective-permute-start | bytes 1179656 | tf_op jit(solution)/shard_map/ppermute | solution.py:40
  48.9 7.5 %collective-permute-start.3 = (bf16[384,512]{1,0:T(8,128)(2,1)S(1)}, bf16[384,512]{1,0:T(8,128)(2,1)S(1)}, u32[]{:S(2)}, u32[]{:S(2)}) collective-permute-start(bf16[384,512]{1,0:T(8,128)(2,1)S(1)} %fusion.6), channel_id=1, source_target_pairs={{0,496},{1,497},{2,498},{3,499},{4,500},{5,501},{6,502},{7,503},{8... | collective-permute-start | bytes 1179656 | tf_op jit(solution)/shard_map/ppermute | solution.py:40
  57.0 7.8 %collective-permute-start.10 = (bf16[384,512]{1,0:T(8,128)(2,1)S(1)}, bf16[384,512]{1,0:T(8,128)(2,1)S(1)}, u32[]{:S(2)}, u32[]{:S(2)}) collective-permute-start(bf16[384,512]{1,0:T(8,128)(2,1)S(1)} %fusion.3), channel_id=1, source_target_pairs={{0,28},{1,29},{2,30},{3,31},{4,24},{5,25},{6,26},{7,27},{8,20},{9,... | collective-permute-start | bytes 1179656 | tf_op jit(solution)/shard_map/ppermute | solution.py:40
  64.8 1.9 %collective-permute-start.9 = (bf16[384,512]{1,0:T(8,128)(2,1)S(1)}, bf16[384,512]{1,0:T(8,128)(2,1)S(1)}, u32[]{:S(2)}, u32[]{:S(2)}) collective-permute-start(bf16[384,512]{1,0:T(8,128)(2,1)S(1)} %fusion.3), channel_id=1, source_target_pairs={{0,16},{1,17},{2,18},{3,19},{4,20},{5,21},{6,22},{7,23},{8,24},{9,... | collective-permute-start | bytes 1179656 | tf_op jit(solution)/shard_map/ppermute | solution.py:40
  66.9 1.9 %collective-permute-start.12 = (bf16[512,1024]{1,0:T(8,128)(2,1)S(1)}, bf16[512,1024]{1,0:T(8,128)(2,1)S(1)}, u32[]{:S(2)}, u32[]{:S(2)}) collective-permute-start(bf16[512,1024]{1,0:T(8,128)(2,1)S(1)} %pad_maximum_fusion.5), channel_id=1, source_target_pairs={{0,3},{1,2},{2,1},{3,0},{4,7},{5,6},{6,5},{7,4},{8,11},{9,10},{10,... | collective-permute-start | bytes 3145736 | tf_op jit(solution)/shard_map/ppermute | solution.py:40
  68.8 3.7 %collective-permute-start.13 = (bf16[1024,512]{1,0:T(8,128)(2,1)S(1)}, bf16[1024,512]{1,0:T(8,128)(2,1)S(1)}, u32[]{:S(2)}, u32[]{:S(2)}) collective-permute-start(bf16[1024,512]{1,0:T(8,128)(2,1)S(1)} %pad_maximum_fusion.4), channel_id=1, source_target_pairs={{0,1},{1,0},{2,3},{3,2},{4,5},{5,4},{6,7},{7,6},{8,9},{9,8},{10,11... | collective-permute-start | bytes 3145736 | tf_op jit(solution)/shard_map/ppermute | solution.py:40
  72.6 2.2 %collective-permute-start.5 = (bf16[384,512]{1,0:T(8,128)(2,1)S(1)}, bf16[384,512]{1,0:T(8,128)(2,1)S(1)}, u32[]{:S(2)}, u32[]{:S(2)}) collective-permute-start(bf16[384,512]{1,0:T(8,128)(2,1)S(1)} %add_convert_fusion.4), channel_id=1, source_target_pairs={{0,12},{1,13},{2,14},{3,15},{4,8},{5,9},{6,10},{7,11},{8,4},{9,5},... | collective-permute-start | bytes 1179656 | tf_op jit(solution)/shard_map/ppermute | solution.py:40
  74.9 11.2 %collective-permute-done.10 = bf16[384,512]{1,0:T(8,128)(2,1)S(1)} collective-permute-done((bf16[384,512]{1,0:T(8,128)(2,1)S(1)}, bf16[384,512]{1,0:T(8,128)(2,1)S(1)}, u32[]{:S(2)}, u32[]{:S(2)}) %collective-permute-start.10) | collective-permute-done | bytes 393248 | tf_op jit(solution)/shard_map/ppermute | solution.py:40
  86.3 1.9 %collective-permute-start.11 = (bf16[384,512]{1,0:T(8,128)(2,1)S(1)}, bf16[384,512]{1,0:T(8,128)(2,1)S(1)}, u32[]{:S(2)}, u32[]{:S(2)}) collective-permute-start(bf16[384,512]{1,0:T(8,128)(2,1)S(1)} %add_convert_fusion.3), channel_id=1, source_target_pairs={{0,12},{1,13},{2,14},{3,15},{4,8},{5,9},{6,10},{7,11},{8,4},{9,5},... | collective-permute-start | bytes 1179656 | tf_op jit(solution)/shard_map/ppermute | solution.py:40
  88.9 1.9 %collective-permute-start.15 = (bf16[1024,256]{1,0:T(8,128)(2,1)S(1)}, bf16[1024,256]{1,0:T(8,128)(2,1)S(1)}, u32[]{:S(2)}, u32[]{:S(2)}) collective-permute-start(bf16[1024,256]{1,0:T(8,128)(2,1)S(1)} %convolution_convert_fusion.1), channel_id=1, source_target_pairs={{0,3},{1,2},{2,1},{3,0},{4,7},{5,6},{6,5},{7,4},{8,11},{9,10},{10,... | collective-permute-start | bytes 1572872 | tf_op jit(solution)/shard_map/ppermute | solution.py:40
  90.9 5.5 %collective-permute-start.14 = (bf16[384,512]{1,0:T(8,128)(2,1)S(1)}, bf16[384,512]{1,0:T(8,128)(2,1)S(1)}, u32[]{:S(2)}, u32[]{:S(2)}) collective-permute-start(bf16[384,512]{1,0:T(8,128)(2,1)S(1)} %get-tuple-element.29), channel_id=1, source_target_pairs={{0,1},{1,0},{2,3},{3,2},{4,5},{5,4},{6,7},{7,6},{8,9},{9,8},{10,11... | collective-permute-start | bytes 1179656 | tf_op jit(solution)/shard_map/ppermute | solution.py:40
  98.1 5.2 %collective-permute-start.17 = (bf16[256,1024]{1,0:T(8,128)(2,1)S(1)}, bf16[256,1024]{1,0:T(8,128)(2,1)S(1)}, u32[]{:S(2)}, u32[]{:S(2)}) collective-permute-start(bf16[256,1024]{1,0:T(8,128)(2,1)S(1)} %convolution_convert_fusion), channel_id=1, source_target_pairs={{0,1},{1,0},{2,3},{3,2},{4,5},{5,4},{6,7},{7,6},{8,9},{9,8},{10,11... | collective-permute-start | bytes 1572872 | tf_op jit(solution)/shard_map/ppermute | solution.py:40
  103.3 1.9 %collective-permute-start.16 = (bf16[384,512]{1,0:T(8,128)(2,1)S(1)}, bf16[384,512]{1,0:T(8,128)(2,1)S(1)}, u32[]{:S(2)}, u32[]{:S(2)}) collective-permute-start(bf16[384,512]{1,0:T(8,128)(2,1)S(1)} %get-tuple-element.35), channel_id=1, source_target_pairs={{0,3},{1,2},{2,1},{3,0},{4,7},{5,6},{6,5},{7,4},{8,11},{9,10},{10,... | collective-permute-start | bytes 1179656 | tf_op jit(solution)/shard_map/ppermute | solution.py:40
  105.9 1.5 %add_convert_fusion.1 = bf16[384,1024]{1,0:T(8,128)(2,1)} fusion(f32[384,1024]{1,0:T(8,128)S(1)} %fusion.34, bf16[384,512]{1,0:T(8,128)(2,1)S(1)} %get-tuple-element.43, bf16[1024,512]{1,0:T(8,128)(2,1)S(1)} %pad_maximum_fusion.4), kind=kOutput, calls=%fused_computation.3 | convolution fusion | flops 403439616 | bytes 3801088 | tf_op jit(solution)/shard_map/dot_general | solution.py:22
  110.1 6.3 %collective-permute-done.16 = bf16[384,512]{1,0:T(8,128)(2,1)S(1)} collective-permute-done((bf16[384,512]{1,0:T(8,128)(2,1)S(1)}, bf16[384,512]{1,0:T(8,128)(2,1)S(1)}, u32[]{:S(2)}, u32[]{:S(2)}) %collective-permute-start.16) | collective-permute-done | bytes 393248 | tf_op jit(solution)/shard_map/ppermute | solution.py:40
  (42 shorter events, 10.5 us)
Async XLA Ops:
  0.6 18.4 %collective-permute-start = (bf16[384,1024]{1,0:T(8,128)(2,1)}, bf16[384,1024]{1,0:T(8,128)(2,1)S(1)}, u32[]{:S(2)}, u32[]{:S(2)}) collective-permute-start(bf16[384,1024]{1,0:T(8,128)(2,1)} %bitcast.37), channel_id=1, source_target_pairs={{0,3},{1,2},{2,1},{3,0},{4,7},{5,6},{6,5},{7,4},{8,11},{9,10},{10,... | collective-permute-start | bytes 2359304 | tf_op jit(solution)/shard_map/ppermute | solution.py:40
  4.6 14.4 %collective-permute-start.1 = (bf16[256,1024]{1,0:T(8,128)(2,1)}, bf16[256,1024]{1,0:T(8,128)(2,1)S(1)}, u32[]{:S(2)}, u32[]{:S(2)}) collective-permute-start(bf16[256,1024]{1,0:T(8,128)(2,1)} %bitcast.47), channel_id=1, source_target_pairs={{0,1},{1,0},{2,3},{3,2},{4,5},{5,4},{6,7},{7,6},{8,9},{9,8},{10,11... | collective-permute-start | bytes 1572872 | tf_op jit(solution)/shard_map/ppermute | solution.py:40
  8.3 27.6 %collective-permute-start.6 = (bf16[384,1024]{1,0:T(8,128)(2,1)}, bf16[384,1024]{1,0:T(8,128)(2,1)S(1)}, u32[]{:S(2)}, u32[]{:S(2)}) collective-permute-start(bf16[384,1024]{1,0:T(8,128)(2,1)} %bitcast.39), channel_id=1, source_target_pairs={{0,1},{1,0},{2,3},{3,2},{4,5},{5,4},{6,7},{7,6},{8,9},{9,8},{10,11... | collective-permute-start | bytes 2359304 | tf_op jit(solution)/shard_map/ppermute | solution.py:40
  11.1 18.8 %collective-permute-start.7 = (bf16[1024,256]{1,0:T(8,128)(2,1)}, bf16[1024,256]{1,0:T(8,128)(2,1)S(1)}, u32[]{:S(2)}, u32[]{:S(2)}) collective-permute-start(bf16[1024,256]{1,0:T(8,128)(2,1)} %bitcast.43), channel_id=1, source_target_pairs={{0,3},{1,2},{2,1},{3,0},{4,7},{5,6},{6,5},{7,4},{8,11},{9,10},{10,... | collective-permute-start | bytes 1572872 | tf_op jit(solution)/shard_map/ppermute | solution.py:40
  13.1 22.8 %copy-start.1 = (bf16[1,384,1024]{2,1,0:T(8,128)(2,1)S(1)}, bf16[1,384,1024]{2,1,0:T(8,128)(2,1)}, u32[]{:S(2)}) copy-start(bf16[1,384,1024]{2,1,0:T(8,128)(2,1)} %param.4) | copy-start | bytes 2359300
  13.1 22.8 %copy-start.2 = (bf16[1,1024,256]{2,1,0:T(8,128)(2,1)S(1)}, bf16[1,1024,256]{2,1,0:T(8,128)(2,1)}, u32[]{:S(2)}) copy-start(bf16[1,1024,256]{2,1,0:T(8,128)(2,1)} %param.6) | copy-start | bytes 1572868
  20.9 22.3 %copy-start = (bf16[1,384,1024]{2,1,0:T(8,128)(2,1)S(1)}, bf16[1,384,1024]{2,1,0:T(8,128)(2,1)}, u32[]{:S(2)}) copy-start(bf16[1,384,1024]{2,1,0:T(8,128)(2,1)} %param.5) | copy-start | bytes 2359300
  20.9 22.4 %collective-permute-start.2 = (bf16[384,512]{1,0:T(8,128)(2,1)S(1)}, bf16[384,512]{1,0:T(8,128)(2,1)S(1)}, u32[]{:S(2)}, u32[]{:S(2)}) collective-permute-start(bf16[384,512]{1,0:T(8,128)(2,1)S(1)} %convolution_convert_fusion.4), channel_id=1, source_target_pairs={{0,4},{1,5},{2,6},{3,7},{4,0},{5,1},{6,2},{7,3},{8,12},{9,13},{10,... | collective-permute-start | bytes 1179656 | tf_op jit(solution)/shard_map/ppermute | solution.py:40
  36.5 6.9 %copy-start.3 = (bf16[1,256,1024]{2,1,0:T(8,128)(2,1)S(1)}, bf16[1,256,1024]{2,1,0:T(8,128)(2,1)}, u32[]{:S(2)}) copy-start(bf16[1,256,1024]{2,1,0:T(8,128)(2,1)} %param.7) | copy-start | bytes 1572868
  36.5 19.9 %collective-permute-start.8 = (bf16[384,512]{1,0:T(8,128)(2,1)S(1)}, bf16[384,512]{1,0:T(8,128)(2,1)S(1)}, u32[]{:S(2)}, u32[]{:S(2)}) collective-permute-start(bf16[384,512]{1,0:T(8,128)(2,1)S(1)} %convolution_convert_fusion.2), channel_id=1, source_target_pairs={{0,4},{1,5},{2,6},{3,7},{4,0},{5,1},{6,2},{7,3},{8,12},{9,13},{10,... | collective-permute-start | bytes 1179656 | tf_op jit(solution)/shard_map/ppermute | solution.py:40
  44.0 24.9 %collective-permute-start.4 = (bf16[384,512]{1,0:T(8,128)(2,1)S(1)}, bf16[384,512]{1,0:T(8,128)(2,1)S(1)}, u32[]{:S(2)}, u32[]{:S(2)}) collective-permute-start(bf16[384,512]{1,0:T(8,128)(2,1)S(1)} %fusion.6), channel_id=1, source_target_pairs={{0,508},{1,509},{2,510},{3,511},{4,504},{5,505},{6,506},{7,507},{8... | collective-permute-start | bytes 1179656 | tf_op jit(solution)/shard_map/ppermute | solution.py:40
  48.9 23.6 %collective-permute-start.3 = (bf16[384,512]{1,0:T(8,128)(2,1)S(1)}, bf16[384,512]{1,0:T(8,128)(2,1)S(1)}, u32[]{:S(2)}, u32[]{:S(2)}) collective-permute-start(bf16[384,512]{1,0:T(8,128)(2,1)S(1)} %fusion.6), channel_id=1, source_target_pairs={{0,496},{1,497},{2,498},{3,499},{4,500},{5,501},{6,502},{7,503},{8... | collective-permute-start | bytes 1179656 | tf_op jit(solution)/shard_map/ppermute | solution.py:40
  57.0 29.2 %collective-permute-start.10 = (bf16[384,512]{1,0:T(8,128)(2,1)S(1)}, bf16[384,512]{1,0:T(8,128)(2,1)S(1)}, u32[]{:S(2)}, u32[]{:S(2)}) collective-permute-start(bf16[384,512]{1,0:T(8,128)(2,1)S(1)} %fusion.3), channel_id=1, source_target_pairs={{0,28},{1,29},{2,30},{3,31},{4,24},{5,25},{6,26},{7,27},{8,20},{9,... | collective-permute-start | bytes 1179656 | tf_op jit(solution)/shard_map/ppermute | solution.py:40
  64.8 21.4 %collective-permute-start.9 = (bf16[384,512]{1,0:T(8,128)(2,1)S(1)}, bf16[384,512]{1,0:T(8,128)(2,1)S(1)}, u32[]{:S(2)}, u32[]{:S(2)}) collective-permute-start(bf16[384,512]{1,0:T(8,128)(2,1)S(1)} %fusion.3), channel_id=1, source_target_pairs={{0,16},{1,17},{2,18},{3,19},{4,20},{5,21},{6,22},{7,23},{8,24},{9,... | collective-permute-start | bytes 1179656 | tf_op jit(solution)/shard_map/ppermute | solution.py:40
  66.9 30.5 %collective-permute-start.12 = (bf16[512,1024]{1,0:T(8,128)(2,1)S(1)}, bf16[512,1024]{1,0:T(8,128)(2,1)S(1)}, u32[]{:S(2)}, u32[]{:S(2)}) collective-permute-start(bf16[512,1024]{1,0:T(8,128)(2,1)S(1)} %pad_maximum_fusion.5), channel_id=1, source_target_pairs={{0,3},{1,2},{2,1},{3,0},{4,7},{5,6},{6,5},{7,4},{8,11},{9,10},{10,... | collective-permute-start | bytes 3145736 | tf_op jit(solution)/shard_map/ppermute | solution.py:40
  68.8 28.6 %collective-permute-start.13 = (bf16[1024,512]{1,0:T(8,128)(2,1)S(1)}, bf16[1024,512]{1,0:T(8,128)(2,1)S(1)}, u32[]{:S(2)}, u32[]{:S(2)}) collective-permute-start(bf16[1024,512]{1,0:T(8,128)(2,1)S(1)} %pad_maximum_fusion.4), channel_id=1, source_target_pairs={{0,1},{1,0},{2,3},{3,2},{4,5},{5,4},{6,7},{7,6},{8,9},{9,8},{10,11... | collective-permute-start | bytes 3145736 | tf_op jit(solution)/shard_map/ppermute | solution.py:40
  72.6 15.6 %collective-permute-start.5 = (bf16[384,512]{1,0:T(8,128)(2,1)S(1)}, bf16[384,512]{1,0:T(8,128)(2,1)S(1)}, u32[]{:S(2)}, u32[]{:S(2)}) collective-permute-start(bf16[384,512]{1,0:T(8,128)(2,1)S(1)} %add_convert_fusion.4), channel_id=1, source_target_pairs={{0,12},{1,13},{2,14},{3,15},{4,8},{5,9},{6,10},{7,11},{8,4},{9,5},... | collective-permute-start | bytes 1179656 | tf_op jit(solution)/shard_map/ppermute | solution.py:40
  86.3 11.1 %collective-permute-start.11 = (bf16[384,512]{1,0:T(8,128)(2,1)S(1)}, bf16[384,512]{1,0:T(8,128)(2,1)S(1)}, u32[]{:S(2)}, u32[]{:S(2)}) collective-permute-start(bf16[384,512]{1,0:T(8,128)(2,1)S(1)} %add_convert_fusion.3), channel_id=1, source_target_pairs={{0,12},{1,13},{2,14},{3,15},{4,8},{5,9},{6,10},{7,11},{8,4},{9,5},... | collective-permute-start | bytes 1179656 | tf_op jit(solution)/shard_map/ppermute | solution.py:40
  88.9 19.7 %collective-permute-start.15 = (bf16[1024,256]{1,0:T(8,128)(2,1)S(1)}, bf16[1024,256]{1,0:T(8,128)(2,1)S(1)}, u32[]{:S(2)}, u32[]{:S(2)}) collective-permute-start(bf16[1024,256]{1,0:T(8,128)(2,1)S(1)} %convolution_convert_fusion.1), channel_id=1, source_target_pairs={{0,3},{1,2},{2,1},{3,0},{4,7},{5,6},{6,5},{7,4},{8,11},{9,10},{10,... | collective-permute-start | bytes 1572872 | tf_op jit(solution)/shard_map/ppermute | solution.py:40
  90.9 14.4 %collective-permute-start.14 = (bf16[384,512]{1,0:T(8,128)(2,1)S(1)}, bf16[384,512]{1,0:T(8,128)(2,1)S(1)}, u32[]{:S(2)}, u32[]{:S(2)}) collective-permute-start(bf16[384,512]{1,0:T(8,128)(2,1)S(1)} %get-tuple-element.29), channel_id=1, source_target_pairs={{0,1},{1,0},{2,3},{3,2},{4,5},{5,4},{6,7},{7,6},{8,9},{9,8},{10,11... | collective-permute-start | bytes 1179656 | tf_op jit(solution)/shard_map/ppermute | solution.py:40
  98.1 19.8 %collective-permute-start.17 = (bf16[256,1024]{1,0:T(8,128)(2,1)S(1)}, bf16[256,1024]{1,0:T(8,128)(2,1)S(1)}, u32[]{:S(2)}, u32[]{:S(2)}) collective-permute-start(bf16[256,1024]{1,0:T(8,128)(2,1)S(1)} %convolution_convert_fusion), channel_id=1, source_target_pairs={{0,1},{1,0},{2,3},{3,2},{4,5},{5,4},{6,7},{7,6},{8,9},{9,8},{10,11... | collective-permute-start | bytes 1572872 | tf_op jit(solution)/shard_map/ppermute | solution.py:40
  103.3 13.1 %collective-permute-start.16 = (bf16[384,512]{1,0:T(8,128)(2,1)S(1)}, bf16[384,512]{1,0:T(8,128)(2,1)S(1)}, u32[]{:S(2)}, u32[]{:S(2)}) collective-permute-start(bf16[384,512]{1,0:T(8,128)(2,1)S(1)} %get-tuple-element.35), channel_id=1, source_target_pairs={{0,3},{1,2},{2,1},{3,0},{4,7},{5,6},{6,5},{7,4},{8,11},{9,10},{10,... | collective-permute-start | bytes 1179656 | tf_op jit(solution)/shard_map/ppermute | solution.py:40
